TPU v7x, 256 devices: a whole 4x4x8 slice. The times are simulated.
256 devices in a mesh: dp: 8 (over z), vocab: 32 (over x, y, core).
Axes of the slice: x: 4, y: 4, z: 8, core: 2. Of those that a mesh axis runs over, the one named last changes fastest.
Arguments:
- hidden: bfloat16 [768, 5120], P('dp', 'vocab'), may hold values from -64 to 64
- head_weight: bfloat16 [5120, 151552], P(None, ('dp', 'vocab')), may hold values from -3 to 3
- targets: int32 [768], P('dp'), may hold values from 0 to 151551
- advantage: float32 [768], P('dp'), may hold values from -4 to 4
- policy_mask: int32 [768], P('dp'), may hold values from 0 to 1, as said below
Outputs:
- hidden_grad: bfloat16 [768, 5120], P('dp', 'vocab')
- head_grad: bfloat16 [5120, 151552], P(None, ('dp', 'vocab'))
- loss: float32 [], replicated
Inputs may be any that keep to these rules, and one draw needn't show every extreme that they name: `policy_mask`: exactly 384 tokens are marked 1 in all, and the 96 tokens of one index of dp are all marked.
All inputs are finite; a program needn't handle non-finite values.
Results may differ from a plain program's by a relative error of at most 0.012.
Values may be sent and summed in bfloat16 or wider, within the bound.
No kernel may reach another device: no remote copies, remote signals or barrier semaphores. Data moves between devices by JAX's collectives and lax.ppermute only.
A program may use at most 128 MiB of HBM per device.

v0:
```python
import jax
import jax.numpy as jnp
from jax import lax
from jax.sharding import PartitionSpec as P

entropy_coef = 0.02


def body(hidden, head_weight, targets, advantage, policy_mask):
    dp_count = lax.axis_size("dp")
    vocab_count = lax.axis_size("vocab")
    tok_count = hidden.shape[0]
    col_count = head_weight.shape[1]
    all_tokens = tok_count * dp_count
    policy_total = all_tokens // 2
    dp_index = lax.axis_index("dp")
    first_col = (dp_index * vocab_count + lax.axis_index("vocab")) * col_count
    marked = jnp.where(policy_mask > 0, targets, -1)
    all_marked, all_adv = (
        lax.all_gather(marked, "dp", axis=0, tiled=True),
        lax.all_gather(advantage, "dp", axis=0, tiled=True),
    )
    all_on = all_marked >= 0
    row_on = all_on.astype(jnp.float32)
    row_adv = all_adv * row_on
    row_block = lax.all_gather(hidden, "dp", axis=0, tiled=True)
    gathered = lax.all_gather(row_block, "vocab", axis=1, tiled=True)
    logits = jnp.dot(gathered, head_weight, preferred_element_type=jnp.float32)
    columns = first_col + jnp.arange(col_count, dtype=jnp.int32)
    is_target = all_marked[:, None] == columns[None, :]
    local_chosen = jnp.sum(jnp.where(is_target, logits, 0.0), axis=1)
    local_top = jnp.max(logits, axis=1)
    row_top = lax.pmax(local_top, ("dp", "vocab"))
    shifted = jnp.exp(logits - row_top[:, None])
    row_total, row_mix, chosen = lax.psum(
        (jnp.sum(shifted, axis=1), jnp.sum(shifted * logits, axis=1), local_chosen), ("dp", "vocab")
    )
    probs = shifted / row_total[:, None]
    log_total = row_top + jnp.log(row_total)
    mean_logit = row_mix / row_total
    dlogits = (
        (
            row_adv[:, None] * (probs - is_target.astype(jnp.float32))
            + entropy_coef * row_on[:, None] * probs * (logits - mean_logit[:, None])
        )
        / policy_total
    ).astype(jnp.bfloat16)
    loss = (
        -jnp.sum(row_adv * (chosen - log_total) + entropy_coef * row_on * (log_total - mean_logit))
        / policy_total
    )
    head_grad = lax.dot_general(
        gathered, dlogits, (((0,), (0,)), ((), ())), preferred_element_type=jnp.float32
    ).astype(jnp.bfloat16)
    width_sums = lax.psum_scatter(
        lax.dot_general(
            head_weight, dlogits, (((1,), (1,)), ((), ())), preferred_element_type=jnp.float32
        ),
        "vocab",
        scatter_dimension=0,
        tiled=True,
    )
    mine_sums = lax.psum_scatter(width_sums, "dp", scatter_dimension=1, tiled=True)
    grad_rows = mine_sums.T.astype(jnp.bfloat16)
    return (grad_rows, head_grad, loss)


def solution(mesh):
    in_specs = (P("dp", "vocab"), P(None, ("dp", "vocab")), P("dp"), P("dp"), P("dp"))
    out_specs = (P("dp", "vocab"), P(None, ("dp", "vocab")), P())
    return jax.shard_map(body, mesh=mesh, in_specs=in_specs, out_specs=out_specs, check_vma=False)
```

profile of v0, /device:TPU:2, one launch (start us, length us, event | category | flops | bytes accessed | tf_op | source)
XLA Modules:
  0.0 448.5 jit_solution(14546391111112924375)
XLA Ops:
  7.2 0.0 copy-start.3
  7.2 0.0 copy-start.2
  7.2 0.0 copy-start.1
  7.2 0.0 copy-start
  7.2 0.0 all-gather.3.cloned.1.call-start
  7.3 28.9 %all-gather = bf16[8,96,160]{1,2,0:T(8,128)(2,1)S(1)} all-gather(bf16[1,96,160]{1,2,0:T(8,128)(2,1)} %bitcast.15), channel_id=1, replica_groups=mesh['dp'=8,'vocab'=32] {'dp'}, dimensions={0}, use_global_device_ids=true | all-gather | bytes 276480 | tf_op jit(solution)/shard_map/all_gather | solution.py:26
  36.2 0.1 copy.11
  36.3 1.0 reshape.24
  37.3 0.0 all-gather.3.cloned.1.call-update
  37.3 0.0 reduce-scatter.7.cloned.1.call-start
  37.4 0.0 copy-done.3
  37.4 0.6 dynamic-slice
  38.6 0.0 copy-done.2
  38.6 0.2 dynamic-update-slice.1
  38.9 0.0 copy-done.1
  38.9 0.0 copy-done
  38.9 0.1 fusion.8
  39.0 11.3 %all-reduce = s32[768]{0:T(1024)S(1)} all-reduce(s32[768]{0:T(1024)S(1)} %fusion.8), channel_id=1, replica_groups=mesh['dp'=8,'vocab'=32] {'dp'}, use_global_device_ids=true, to_apply=%add | all-reduce | flops 768 | bytes 6144
  50.3 16.2 %all-reduce.1 = f32[768]{0:T(1024)S(1)} all-reduce(f32[768]{0:T(1024)S(1)} %dynamic-update-slice.1), channel_id=1, replica_groups=mesh['dp'=8,'vocab'=32] {'dp'}, use_global_device_ids=true, to_apply=%add.1 | all-reduce | flops 768 | bytes 6144
  66.5 26.8 %all-gather.3.cloned.1.call-done = bf16[768,5120]{0,1:T(8,128)(2,1)} async-done(((bf16[768,160]{0,1:T(8,128)(2,1)}), bf16[768,5120]{0,1:T(8,128)(2,1)}) %all-gather.3.cloned.1.call-update) | async-done | bytes 7864336 | tf_op jit(solution)/shard_map/all_gather | solution.py:27
  93.3 9.0 %fusion.11 = (f32[768]{0:T(1024)S(1)}, f32[768,592]{0,1:T(8,128)S(1)}) fusion(bf16[5120,592]{0,1:T(8,128)(2,1)} %param.6, bf16[768,5120]{0,1:T(8,128)(2,1)} %all-gather.3.cloned.1.call-done), kind=kOutput, calls=%fused_computation.22 | convolution fusion | flops 4656131072 | bytes 15748096 | tf_op jit(solution)/shard_map/dot_general | solution.py:28
  102.3 76.0 %pmax.7 = f32[768]{0:T(1024)S(1)} all-reduce(f32[768]{0:T(1024)S(1)} %get-tuple-element.23), channel_id=1, replica_groups=mesh['dp'=8,'vocab'=32] {'dp','vocab'}, use_global_device_ids=true, to_apply=%region_1.2 | all-reduce | flops 768 | bytes 6144 | tf_op jit(solution)/shard_map/pmax | solution.py:33
  178.3 0.6 fusion.7
  178.9 74.4 %all-reduce.2 = (f32[768]{0:T(1024)S(1)}, f32[768]{0:T(1024)S(1)}, f32[768]{0:T(1024)S(1)}) all-reduce(f32[768]{0:T(1024)S(1)} %get-tuple-element.13, f32[768]{0:T(1024)S(1)} %get-tuple-element.12, f32[768]{0:T(1024)S(1)} %get-tuple-element.14), channel_id=1, replica_groups=mesh['dp'=8,'vocab'=32] {'dp','vocab'}, use_global_device_ids=true, to_apply=%region_5.6 | all-reduce | flops 2304 | bytes 18432 | tf_op jit(solution)/shard_map/psum | solution.py:35
  253.3 0.6 add_reduce_fusion
  253.9 12.4 %convolution_bitcast_fusion = f32[5120,768]{0,1:T(8,128)} fusion(bf16[5120,592]{0,1:T(8,128)(2,1)} %param.6, f32[768,592]{0,1:T(8,128)S(1)} %get-tuple-element.24, f32[768]{0:T(1024)S(1)} %get-tuple-element.20, f32[768]{0:T(1024)S(1)} %get-tuple-element.22, s32[768]{0:T(1024)S(1)} %all-reduce, f32[768]{0:T(1024)S(1)} %get-tuple-element.16, f32[768]{0:T(1024)S(1)} %pmax.7, ...), kind=kOutput, calls=%fused_computation | convolution fusion | flops 4661133312 | bytes 23630144 | tf_op jit(solution)/shard_map/dot_general | solution.py:56
  266.3 15.6 %copy.13 = f32[5120,768]{1,0:T(8,128)} copy(f32[5120,768]{0,1:T(8,128)} %convolution_bitcast_fusion) | data formatting | bytes 31457280
  281.9 0.0 reduce-scatter.7.cloned.1.call-update
  282.0 0.0 reduce-scatter.5.cloned.1.call-start
  282.7 116.5 %reduce-scatter.7.cloned.1.call-done = f32[160,768]{1,0:T(8,128)} async-done(((f32[5120,768]{1,0:T(8,128)}), f32[160,768]{1,0:T(8,128)}) %reduce-scatter.7.cloned.1.call-update) | async-done | bytes 491536
  399.1 2.2 copy.14
  401.3 0.0 reduce-scatter.5.cloned.1.call-update
  401.3 10.8 %fusion = bf16[5120,592]{0,1:T(8,128)(2,1)} fusion(bf16[768,5120]{0,1:T(8,128)(2,1)} %all-gather.3.cloned.1.call-done, f32[768,592]{0,1:T(8,128)S(1)} %get-tuple-element.24, f32[768]{0:T(1024)S(1)} %get-tuple-element.20, f32[768]{0:T(1024)S(1)} %get-tuple-element.22, s32[768]{0:T(1024)S(1)} %all-reduce, f32[768]{0:T(1024)S(1)} %get-tuple-element.16, ...), kind=kOutput, calls=%fused_computation.2 | convolution fusion | flops 4664164352 | bytes 15765824 | tf_op jit(solution)/shard_map/dot_general | solution.py:52
  412.1 27.1 %reduce-scatter.5.cloned.1.call-done = f32[160,96]{0,1:T(8,128)} async-done(((f32[160,768]{0,1:T(8,128)}), f32[160,96]{0,1:T(8,128)}) %reduce-scatter.5.cloned.1.call-update) | async-done | bytes 61456 | tf_op jit(solution)/shard_map/reduce_scatter | solution.py:63
  439.2 0.9 convert_bitcast_fusion
  440.1 0.7 copy.12
  (4 shorter events, 0.0 us)
Async XLA Ops:
  7.2 30.2 %copy-start.3 = (u32[256]{0:T(256)S(1)}, u32[256]{0:T(256)}, u32[]{:S(2)}) copy-start(u32[256]{0:T(256)} %constant.36) | copy-start | bytes 3076
  7.2 31.5 %copy-start.2 = (f32[96]{0:T(128)S(1)}, f32[96]{0:T(128)}, u32[]{:S(2)}) copy-start(f32[96]{0:T(128)} %param.8) | copy-start | bytes 1156
  7.2 31.7 %copy-start.1 = (s32[96]{0:T(128)S(1)}, s32[96]{0:T(128)}, u32[]{:S(2)}) copy-start(s32[96]{0:T(128)} %param.9) | copy-start | bytes 1156
  7.2 31.7 %copy-start = (s32[96]{0:T(128)S(1)}, s32[96]{0:T(128)}, u32[]{:S(2)}) copy-start(s32[96]{0:T(128)} %param.7) | copy-start | bytes 1156
  7.2 86.1 %all-gather.3.cloned.1.call-start = ((), (), s32[]{:S(2)}) async-start(), calls=%async_computation.2 | async-start | bytes 8110080 | tf_op jit(solution)/shard_map/all_gather | solution.py:27
  37.3 361.8 %reduce-scatter.7.cloned.1.call-start = ((), (), s32[]{:S(2)}) async-start(), calls=%async_computation.4 | async-start | bytes 16220160
  282.0 157.2 %reduce-scatter.5.cloned.1.call-start = ((), (), s32[]{:S(2)}) async-start(), calls=%async_computation.3 | async-start | bytes 884736 | tf_op jit(solution)/shard_map/reduce_scatter | solution.py:63
Sparse Core Ops, SparseCore 0:
  37.4 55.8 all-gather.2
  282.1 116.9 reduce-scatter.6
  401.8 37.3 reduce-scatter.4
where the time goes:
time: 449 us; the launch traced here: 448 us
  blocking collectives  207 us (46%)
  waiting for transfers between devices  170 us (38%)
  matrix products  32.2 us (7%)
  local copies, waits for them, and re-layouts  20.5 us (5%)
  between operations  16.3 us (4%)
    unnamed x4, waiting for transfers between devices  117 us
    pmax x1, blocking collectives, body(): row_top = lax.pmax(local_top, ('dp', 'vocab'))  76 us
    psum x1, blocking collectives, body(): lax.psum((jnp.sum(shifted, axis=1), jnp.sum(shifted * logits, axis=1), lo...  74.4 us
    all_gather x1, blocking collectives, body(): row_block = lax.all_gather(hidden, 'dp', axis=0, tiled=True)  28.9 us
    unnamed x2, blocking collectives  27.5 us
    reduce_scatter x1, waiting for transfers between devices, body(): lax.psum_scatter(width_sums, 'dp', scatter_dimension=1, tiled=True)  27.1 us
    all_gather x1, waiting for transfers between devices, body(): gathered = lax.all_gather(row_block, 'vocab', axis=1, tiled=True)  26.8 us
    unnamed x16, local copies, waits for them, and re-layouts  20.3 us
  transfers between devices with their start and end apart: 3, of which 3 were waited for; matrix products, arithmetic and copies ran while one was open for 3% of the time, Pallas kernels for 0%

commit v1 on v0

v1 whole, which is shorter than its diff:
```python
import functools

import jax
import jax.numpy as jnp
from jax import lax
from jax.experimental import pallas as pl
from jax.experimental.pallas import tpu as pltpu
from jax.sharding import Mesh, PartitionSpec as P

entropy_coef = 0.02
tok = 96
policy = 384
width = 160
cols = 592
meta_rows = 16
bf16 = jnp.bfloat16
f32 = jnp.float32
nt_dims = (((1,), (1,)), ((), ()))
tn_dims = (((0,), (0,)), ((), ()))
vmem = pltpu.CompilerParams(vmem_limit_bytes=48 * 1024 * 1024)


def pack_kernel(hidden_ref, targets_ref, adv_ref, mask_ref, out_ref):
    adv = adv_ref[...]
    high = adv.astype(bf16).astype(f32)
    rest = adv - high
    mid = rest.astype(bf16).astype(f32)
    low = rest - mid
    targets = targets_ref[...]
    rows = [
        jnp.where(mask_ref[...] > 0, 1.0, 0.0),
        high,
        mid,
        low,
        (targets & 63).astype(f32),
        ((targets >> 6) & 63).astype(f32),
        (targets >> 12).astype(f32),
    ]
    rows.append(jnp.zeros((meta_rows - len(rows), tok), f32))
    meta = jnp.concatenate(rows, axis=0).astype(bf16)
    for z in range(out_ref.shape[0]):
        out_ref[z, :width, :] = hidden_ref[...]
        out_ref[z, width:, :] = meta


def compact_kernel(blocks_ref, rows_ref, meta_ref, rank_ref):
    groups = blocks_ref.shape[0]
    mask = jnp.concatenate(
        [blocks_ref[z, width : width + meta_rows, :].astype(f32)[:1] for z in range(groups)], axis=0
    )
    before = lax.broadcasted_iota(jnp.int32, (tok, tok), 0) < lax.broadcasted_iota(jnp.int32, (tok, tok), 1)
    prefix = jnp.dot(mask.astype(bf16), before.astype(bf16), preferred_element_type=f32)
    total = jnp.broadcast_to(jnp.sum(mask, axis=1, keepdims=True), mask.shape)
    start = jnp.zeros((1, tok), f32)
    starts = []
    for z in range(groups):
        starts.append(start)
        start = start + total[z : z + 1]
    rank = jnp.where(mask > 0, prefix + jnp.concatenate(starts, axis=0), -1.0).astype(jnp.int32)
    rank_ref[...] = rank
    place = lax.broadcasted_iota(jnp.int32, (policy, tok), 0)
    acc = jnp.zeros((width + meta_rows, policy), f32)
    for z in range(groups):
        pick = (place == rank[z : z + 1]).astype(f32).astype(bf16)
        acc += lax.dot_general(blocks_ref[z], pick, nt_dims, preferred_element_type=f32)
    meta_ref[...] = acc[width:]
    rows = acc[:width].astype(bf16)
    for other in range(rows_ref.shape[0]):
        rows_ref[other] = rows


def row_tile(core, mine, partner):
    first = jnp.where(core == 0, mine, partner)
    second = jnp.where(core == 0, partner, mine)
    pieces = []
    for block in range(mine.shape[0]):
        pieces += [first[block], second[block]]
    return jnp.concatenate(pieces, axis=0)


def meta_target(meta):
    return (meta[4:5] + 64.0 * meta[5:6] + 4096.0 * meta[6:7]).astype(jnp.int32)


def meta_advantage(meta):
    return meta[1:2] + meta[2:3] + meta[3:4]


def column_is_target(place_ref, meta):
    column = place_ref[1] + lax.broadcasted_iota(jnp.int32, (cols, policy), 0)
    return column == meta_target(meta)


def logits_kernel(place_ref, weight_ref, mine_ref, partner_ref, meta_ref, logits_ref, stats_ref):
    step = pl.program_id(0)
    tile = row_tile(place_ref[0], mine_ref[...], partner_ref[...])
    part = jnp.dot(weight_ref[...], tile, preferred_element_type=f32)

    @pl.when(step == 0)
    def _():
        logits_ref[...] = part

    @pl.when(step > 0)
    def _():
        logits_ref[...] += part

    @pl.when(step == pl.num_programs(0) - 1)
    def _():
        logits = logits_ref[...]
        top = jnp.max(logits, axis=0, keepdims=True)
        shifted = jnp.exp(logits - top)
        total = jnp.sum(shifted, axis=0, keepdims=True)
        mix = jnp.sum(shifted * logits, axis=0, keepdims=True)
        chosen = jnp.sum(
            jnp.where(column_is_target(place_ref, meta_ref[...]), logits, 0.0), axis=0, keepdims=True
        )
        stats = jnp.concatenate([top, total, mix, chosen, jnp.zeros((4, policy), f32)], axis=0)
        for other in range(stats_ref.shape[0]):
            stats_ref[other] = stats


def combine(stats):
    tops = stats[:, 0:1, :]
    top = jnp.max(tops, axis=0)
    scale = jnp.exp(tops - top[None])
    total = jnp.sum(stats[:, 1:2, :] * scale, axis=0)
    mix = jnp.sum(stats[:, 2:3, :] * scale, axis=0)
    chosen = jnp.sum(stats[:, 3:4, :], axis=0)
    return top, total, mix, chosen


def combine_kernel(in_ref, out_ref):
    top, total, mix, chosen = combine(in_ref[...])
    stats = jnp.concatenate([top, total, mix, chosen, jnp.zeros((4, policy), f32)], axis=0)
    for other in range(out_ref.shape[0]):
        out_ref[other] = stats


def grad_kernel(place_ref, stats_ref, meta_ref, logits_ref, weight_ref, grad_ref, dlogits_ref, loss_ref):
    @pl.when(pl.program_id(0) == 0)
    def _():
        top, total, mix, chosen = combine(stats_ref[...])
        meta = meta_ref[...]
        adv = meta_advantage(meta)
        mean = mix / total
        log_total = top + jnp.log(total)
        loss = jnp.sum(
            adv * (chosen - log_total) + entropy_coef * (log_total - mean), axis=1, keepdims=True
        )
        loss_ref[...] = -loss / policy
        logits = logits_ref[...]
        probs = jnp.exp(logits - top) / total
        hit = column_is_target(place_ref, meta).astype(f32)
        dlogits = (adv * (probs - hit) + entropy_coef * probs * (logits - mean)) / policy
        dlogits_ref[...] = dlogits.astype(bf16)

    tile = lax.dot_general(weight_ref[...], dlogits_ref[...], tn_dims, preferred_element_type=f32)
    tile = tile.astype(bf16)
    for block in range(grad_ref.shape[1]):
        for core in range(2):
            at = (2 * block + core) * width
            grad_ref[core, block] = tile[at : at + width]


def head_kernel(place_ref, dlogits_ref, mine_ref, partner_ref, out_ref):
    tile = row_tile(place_ref[0], mine_ref[...], partner_ref[...])
    out_ref[...] = lax.dot_general(
        dlogits_ref[...], tile, nt_dims, preferred_element_type=f32
    ).astype(bf16)


def add_kernel(mine_ref, partner_ref, out_ref):
    out_ref[...] = (mine_ref[...].astype(f32) + partner_ref[...].astype(f32)).astype(bf16)


def spread_kernel(parts_ref, rank_ref, out_ref):
    total = jnp.sum(parts_ref[...].astype(f32), axis=0).astype(bf16)
    place = lax.broadcasted_iota(jnp.int32, (policy, tok), 0)
    for z in range(out_ref.shape[0]):
        pick = (place == rank_ref[z : z + 1, :]).astype(f32).astype(bf16)
        out_ref[z] = jnp.dot(total, pick, preferred_element_type=f32).astype(bf16)


def sum_kernel(parts_ref, out_ref):
    out_ref[...] = jnp.sum(parts_ref[...].astype(f32), axis=0).astype(bf16)


def shape(*dims, dtype=bf16):
    return jax.ShapeDtypeStruct(dims, dtype)


def body(hidden, head_weight, targets, advantage, policy_mask):
    n_dp = lax.axis_size("z")
    n_plane = lax.axis_size("x") * lax.axis_size("y")
    core = lax.axis_index("c")
    device = lax.axis_index(("z", "x", "y", "c"))
    place = jnp.stack([core, device * cols]).astype(jnp.int32)
    weight = head_weight.T
    depth = weight.shape[1]
    swap = [(0, 1), (1, 0)]
    tiles = 4
    tile = depth // tiles
    blocks = n_plane // tiles

    packed = pl.pallas_call(
        pack_kernel, out_shape=shape(n_dp, width + meta_rows, tok), name="pack"
    )(hidden.T, targets[None], advantage[None], policy_mask[None])
    packed = lax.all_to_all(packed, "z", 0, 0)
    rows, meta, rank = pl.pallas_call(
        compact_kernel,
        out_shape=(
            shape(n_plane, width, policy),
            shape(meta_rows, policy, dtype=f32),
            shape(n_dp, tok, dtype=jnp.int32),
        ),
        name="compact",
    )(packed)
    mine = lax.all_to_all(rows, ("x", "y"), 0, 0)
    partner = lax.ppermute(mine, "c", swap)

    smem = pl.BlockSpec(memory_space=pltpu.SMEM)
    weight_spec = pl.BlockSpec((cols, tile), lambda i: (0, i))
    rows_spec = pl.BlockSpec((blocks, width, policy), lambda i: (i, 0, 0))

    def whole(*dims):
        return pl.BlockSpec(dims, lambda i: (0,) * len(dims))

    logits, stats = pl.pallas_call(
        logits_kernel,
        grid=(tiles,),
        in_specs=[smem, weight_spec, rows_spec, rows_spec, whole(meta_rows, policy)],
        out_specs=[whole(cols, policy), whole(2 * n_dp, 8, policy)],
        out_shape=(shape(cols, policy, dtype=f32), shape(2 * n_dp, 8, policy, dtype=f32)),
        compiler_params=vmem,
        name="logits",
    )(place, weight, mine, partner, meta)

    stats = lax.all_to_all(stats, ("z", "c"), 0, 0)
    stats = pl.pallas_call(
        combine_kernel, out_shape=shape(n_plane, 8, policy, dtype=f32), name="combine"
    )(stats)
    stats = lax.all_to_all(stats, ("x", "y"), 0, 0)

    grad, dlogits, loss = pl.pallas_call(
        grad_kernel,
        grid=(tiles,),
        in_specs=[
            smem,
            whole(n_plane, 8, policy),
            whole(meta_rows, policy),
            whole(cols, policy),
            weight_spec,
        ],
        out_specs=[
            pl.BlockSpec((2, blocks, width, policy), lambda i: (0, i, 0, 0)),
            whole(cols, policy),
            whole(1, 1),
        ],
        out_shape=(
            shape(2, n_plane, width, policy),
            shape(cols, policy),
            shape(1, 1, dtype=f32),
        ),
        compiler_params=vmem,
        name="grad",
    )(place, stats, meta, logits, weight)

    kept = lax.dynamic_index_in_dim(grad, core, 0, keepdims=False)
    sent = lax.dynamic_index_in_dim(grad, 1 - core, 0, keepdims=False)
    got = lax.ppermute(sent, "c", swap)
    head_grad = pl.pallas_call(
        head_kernel,
        grid=(tiles,),
        in_specs=[smem, whole(cols, policy), rows_spec, rows_spec],
        out_specs=weight_spec,
        out_shape=shape(cols, depth),
        compiler_params=vmem,
        cost_estimate=pl.CostEstimate(
            flops=2 * cols * depth * policy, bytes_accessed=10_000_000, transcendentals=0
        ),
        name="head",
    )(place, dlogits, mine, partner)
    summed = pl.pallas_call(
        add_kernel,
        grid=(tiles,),
        in_specs=[rows_spec, rows_spec],
        out_specs=rows_spec,
        out_shape=shape(n_plane, width, policy),
        compiler_params=vmem,
        name="pair",
    )(kept, got)
    parts = lax.all_to_all(summed, ("x", "y"), 0, 0)
    spread = pl.pallas_call(
        spread_kernel, out_shape=shape(n_dp, width, tok), compiler_params=vmem, name="spread"
    )(parts, rank)
    parts = lax.all_to_all(spread, "z", 0, 0)
    grad_rows = pl.pallas_call(sum_kernel, out_shape=shape(width, tok), name="total")(parts)
    return grad_rows.T, head_grad.T, loss[0, 0]


def solution(mesh):
    fine = Mesh(mesh.devices.reshape(8, 4, 4, 2), ("z", "x", "y", "c"))
    every = ("z", "x", "y", "c")
    in_specs = (P("z", ("x", "y", "c")), P(None, every), P("z"), P("z"), P("z"))
    out_specs = (P("z", ("x", "y", "c")), P(None, every), P())
    return jax.shard_map(body, mesh=fine, in_specs=in_specs, out_specs=out_specs, check_vma=False)
```

time: 449 us -> 161 us (0.36)
  waiting for transfers between devices: 170 us -> 20.7 us
  blocking collectives: 207 us -> 97.4 us
  matrix products: 32.2 us -> 0 us
  Pallas kernels: 0 us -> 31.3 us
  local copies, waits for them, and re-layouts: 20.5 us -> 1.14 us
  between operations: 16.3 us -> 0.69 us
  starting transfers between devices: 0.12 us -> 8.83 us
    unnamed x4 -> x0, waiting for transfers between devices: 117 us -> none
    all_to_all x0 -> x4, blocking collectives: none -> 97.4 us  [the longest x1 31.5 us: body(): mine = lax.all_to_all(rows, ('x', 'y'), 0, 0)]
    pmax x1 -> x0, blocking collectives: 76 us -> none  [body(): row_top = lax.pmax(local_top, ('dp', 'vocab'))]
    psum x1 -> x0, blocking collectives: 74.4 us -> none  [body(): lax.psum((jnp.sum(shifted, axis=1), jnp.sum(shifted * logits, axis=1), lo...]
    dot_general x3 -> x0, matrix products: 32.2 us -> none  [the longest x1 12.4 us: body(): lax.dot_general(head_weight, dlogits, (((1,), (1,)), ((), ())), preferred...]
    pallas_call x0 -> x9, Pallas kernels: none -> 31.3 us  [the longest x1 7.93 us: body(): pl.pallas_call(grad_kernel, grid=(tiles,), in_specs=[smem, whole(n_plane,...]
    all_gather x1 -> x0, blocking collectives: 28.9 us -> none  [body(): row_block = lax.all_gather(hidden, 'dp', axis=0, tiled=True)]
    unnamed x2 -> x0, blocking collectives: 27.5 us -> none
  transfers between devices with their start and end apart: 3 -> 4, of which waited for: 3 -> 4; matrix products, arithmetic and copies ran while one was open for 3% -> 0% of each run, Pallas kernels for 0% -> 4%
where the time goes in v1:
time: 161 us; the launch traced here: 160 us
  blocking collectives  97.4 us (60%)
  Pallas kernels  31.3 us (19%)
  waiting for transfers between devices  20.7 us (13%)
  starting transfers between devices  8.83 us (5%)
    all_to_all x1, blocking collectives, body(): mine = lax.all_to_all(rows, ('x', 'y'), 0, 0)  31.5 us
    all_to_all x1, blocking collectives, body(): parts = lax.all_to_all(summed, ('x', 'y'), 0, 0)  30.2 us
    all_to_all x1, blocking collectives, body(): packed = lax.all_to_all(packed, 'z', 0, 0)  22.5 us
    all_to_all x1, blocking collectives, body(): stats = lax.all_to_all(stats, ('z', 'c'), 0, 0)  13.2 us
    pallas_call x1, Pallas kernels, body(): pl.pallas_call(grad_kernel, grid=(tiles,), in_specs=[smem, whole(n_plane,...  7.93 us
    all_to_all x1, waiting for transfers between devices, body(): stats = lax.all_to_all(stats, ('x', 'y'), 0, 0)  7.16 us
    pallas_call x1, Pallas kernels, body(): pl.pallas_call(logits_kernel, grid=(tiles,), in_specs=[smem, weight_spec,...  6.72 us
    pallas_call x1, Pallas kernels, body(): pl.pallas_call(head_kernel, grid=(tiles,), in_specs=[smem, whole(cols, po...  6.72 us
  transfers between devices with their start and end apart: 4, of which 4 were waited for; matrix products, arithmetic and copies ran while one was open for 0% of the time, Pallas kernels for 4%

profile of v1, /device:TPU:2, one launch (start us, length us, event | category | flops | bytes accessed | tf_op | source)
XLA Modules:
  0.0 160.1 jit_solution(16025165128246001541)
XLA Ops:
  0.6 1.6 pack.1
  2.2 22.5 %all_to_all.30.blocks_ref = bf16[8,176,96]{2,1,0:T(8,128)(2,1)} all-to-all(bf16[8,176,96]{2,1,0:T(8,128)(2,1)} %pack.1), channel_id=1, replica_groups=mesh['z'=8,'x'=4,'y'=4,'c'=2] {'z'}, dimensions={0} | all-to-all | bytes 540672 | tf_op jit(solution)/shard_map/all_to_all | solution.py:208
  24.8 3.1 %compact.1 = (bf16[16,160,384]{2,1,0:T(8,128)(2,1)}, f32[16,384]{1,0:T(8,128)}, s32[8,96]{1,0:T(8,128)}) custom-call(bf16[8,176,96]{2,1,0:T(8,128)(2,1)} %all_to_all.30.blocks_ref), custom_call_target="tpu_custom_call" | custom-call | tf_op jit(solution)/shard_map/compact/pallas_call | solution.py:209
  27.8 0.0 copy-start
  27.8 31.5 %all_to_all.31.mine_ref = bf16[16,160,384]{2,1,0:T(8,128)(2,1)S(1)} all-to-all(bf16[16,160,384]{2,1,0:T(8,128)(2,1)} %get-tuple-element.11), channel_id=1, replica_groups=mesh['z'=8,'x'=4,'y'=4,'c'=2] {'x','y'}, dimensions={0} | all-to-all | bytes 3932160 | tf_op jit(solution)/shard_map/all_to_all | solution.py:218
  59.4 0.0 collective-permute-start
  59.4 0.1 pad_add_fusion.place_ref
  59.4 4.0 %collective-permute-done.partner_ref = bf16[16,160,384]{2,1,0:T(8,128)(2,1)} collective-permute-done((bf16[16,160,384]{2,1,0:T(8,128)(2,1)S(1)}, bf16[16,160,384]{2,1,0:T(8,128)(2,1)}, u32[]{:S(2)}, u32[]{:S(2)}) %collective-permute-start) | collective-permute-done | bytes 1966112 | tf_op jit(solution)/shard_map/ppermute | solution.py:219
  63.5 0.0 copy-done
  63.5 6.7 %logits.1 = (f32[592,384]{1,0:T(8,128)S(1)}, f32[16,8,384]{2,1,0:T(8,128)S(1)}) custom-call(s32[2]{0:T(128)S(1)} %pad_add_fusion.place_ref, bf16[592,5120]{1,0:T(8,128)(2,1)} %bitcast.14, bf16[16,160,384]{2,1,0:T(8,128)(2,1)S(1)} %all_to_all.31.mine_ref, bf16[16,160,384]{2,1,0:T(8,128)(2,1)} %collective-permute-done.partner_ref, f32[16,384]{1,0:T(8,128)S(1)} %copy-done), custom_call_target="tpu_custom_call" | custom-call | tf_op jit(solution)/shard_map/logits/pallas_call | solution.py:228
  70.2 13.2 %all_to_all.32.in_ref = f32[16,8,384]{2,1,0:T(8,128)} all-to-all(f32[16,8,384]{2,1,0:T(8,128)S(1)} %get-tuple-element.13), channel_id=1, replica_groups=mesh['z'=8,'x'=4,'y'=4,'c'=2] {'z','c'}, dimensions={0} | all-to-all | bytes 393216 | tf_op jit(solution)/shard_map/all_to_all | solution.py:238
  83.3 1.7 %combine.1 = f32[16,8,384]{2,1,0:T(8,128)} custom-call(f32[16,8,384]{2,1,0:T(8,128)} %all_to_all.32.in_ref), custom_call_target="tpu_custom_call" | custom-call | tf_op jit(solution)/shard_map/combine/pallas_call | solution.py:239
  85.1 5.3 %all-to-all-start.3 = ((f32[16,8,384]{2,1,0:T(8,128)}), f32[16,8,384]{2,1,0:T(8,128)S(1)}, u32[]{:S(2)}, u32[]{:S(2)}) async-start(f32[16,8,384]{2,1,0:T(8,128)} %combine.1), calls=%async_computation.3 | async-start | bytes 393216 | tf_op jit(solution)/shard_map/all_to_all | solution.py:242
  90.4 7.2 %all-to-all-done.3.stats_ref = f32[16,8,384]{2,1,0:T(8,128)S(1)} async-done(((f32[16,8,384]{2,1,0:T(8,128)}), f32[16,8,384]{2,1,0:T(8,128)S(1)}, u32[]{:S(2)}, u32[]{:S(2)}) %all-to-all-start.3) | async-done | bytes 196640 | tf_op jit(solution)/shard_map/all_to_all | solution.py:242
  97.5 7.9 %grad.1 = (bf16[2,16,160,384]{3,2,1,0:T(8,128)(2,1)S(1)}, bf16[592,384]{1,0:T(8,128)(2,1)S(1)}, f32[1,1]{1,0:T(1,128)}) custom-call(s32[2]{0:T(128)S(1)} %pad_add_fusion.place_ref, f32[16,8,384]{2,1,0:T(8,128)S(1)} %all-to-all-done.3.stats_ref, f32[16,384]{1,0:T(8,128)S(1)} %copy-done, f32[592,384]{1,0:T(8,128)S(1)} %get-tuple-element.14.logits_ref, ...), custom_call_target="tpu_custom_call" | custom-call | tf_op jit(solution)/shard_map/grad/pallas_call | solution.py:244
  105.5 0.4 dynamic-slice_bitcast_fusion
  105.9 0.1 collective-permute-start.1
  106.0 4.0 %collective-permute-done.1.partner_ref = bf16[16,160,384]{2,1,0:T(8,128)(2,1)S(1)} collective-permute-done((bf16[16,160,384]{2,1,0:T(8,128)(2,1)S(1)}, bf16[16,160,384]{2,1,0:T(8,128)(2,1)S(1)}, u32[]{:S(2)}, u32[]{:S(2)}) %collective-permute-start.1) | collective-permute-done | bytes 1966112 | tf_op jit(solution)/shard_map/ppermute | solution.py:270
  109.9 0.5 pair.1
  110.5 0.0 copy-start.1
  110.5 30.2 %all_to_all.33.parts_ref = bf16[16,160,384]{2,1,0:T(8,128)(2,1)S(1)} all-to-all(bf16[16,160,384]{2,1,0:T(8,128)(2,1)S(1)} %pair.1), channel_id=1, replica_groups=mesh['z'=8,'x'=4,'y'=4,'c'=2] {'x','y'}, dimensions={0} | all-to-all | bytes 3932160 | tf_op jit(solution)/shard_map/all_to_all | solution.py:292
  140.6 0.0 copy-done.1
  140.6 1.4 spread.1
  142.0 3.4 %all-to-all-start.5 = ((bf16[8,160,96]{2,1,0:T(8,128)(2,1)}), bf16[8,160,96]{2,1,0:T(8,128)(2,1)S(1)}, u32[]{:S(2)}, u32[]{:S(2)}) async-start(bf16[8,160,96]{2,1,0:T(8,128)(2,1)} %spread.1), calls=%async_computation.5 | async-start | bytes 655360 | tf_op jit(solution)/shard_map/all_to_all | solution.py:296
  145.4 6.7 %head.1 = bf16[592,5120]{1,0:T(8,128)(2,1)} custom-call(s32[2]{0:T(128)S(1)} %pad_add_fusion.place_ref, bf16[592,384]{1,0:T(8,128)(2,1)S(1)} %get-tuple-element.17.dlogits_ref, bf16[16,160,384]{2,1,0:T(8,128)(2,1)S(1)} %all_to_all.31.mine_ref, bf16[16,160,384]{2,1,0:T(8,128)(2,1)} %collective-permute-done.partner_ref), custom_call_target="tpu_custom_call" | custom-call | flops 2327838720 | bytes 10000000 | tf_op jit(solution)/shard_map/head/pallas_call | solution.py:271
  152.2 5.6 %all-to-all-done.5.parts_ref = bf16[8,160,96]{2,1,0:T(8,128)(2,1)S(1)} async-done(((bf16[8,160,96]{2,1,0:T(8,128)(2,1)}), bf16[8,160,96]{2,1,0:T(8,128)(2,1)S(1)}, u32[]{:S(2)}, u32[]{:S(2)}) %all-to-all-start.5) | async-done | bytes 245792 | tf_op jit(solution)/shard_map/all_to_all | solution.py:296
  157.8 0.0 copy-start.2
  157.8 0.7 copy-done.2
  158.5 1.7 %total.1 = bf16[160,96]{1,0:T(8,128)(2,1)} custom-call(bf16[8,160,96]{2,1,0:T(8,128)(2,1)} %copy-done.2), custom_call_target="tpu_custom_call" | custom-call | tf_op jit(solution)/shard_map/total/pallas_call | solution.py:297
Async XLA Ops:
  27.8 35.7 %copy-start = (f32[16,384]{1,0:T(8,128)S(1)}, f32[16,384]{1,0:T(8,128)}, u32[]{:S(2)}) copy-start(f32[16,384]{1,0:T(8,128)} %get-tuple-element.12.meta_ref) | copy-start | bytes 73732
  59.4 4.1 %collective-permute-start = (bf16[16,160,384]{2,1,0:T(8,128)(2,1)S(1)}, bf16[16,160,384]{2,1,0:T(8,128)(2,1)}, u32[]{:S(2)}, u32[]{:S(2)}) collective-permute-start(bf16[16,160,384]{2,1,0:T(8,128)(2,1)S(1)} %all_to_all.31.mine_ref), channel_id=1, source_target_pairs={{0,1},{1,0},{2,3},{3,2},{4,5},{5,4},{6,7},{7,6},{8,9},{9,8},{10,11... | collective-permute-start | bytes 5898248 | tf_op jit(solution)/shard_map/ppermute | solution.py:219
  85.1 12.5 %all-to-all-start.3 = ((f32[16,8,384]{2,1,0:T(8,128)}), f32[16,8,384]{2,1,0:T(8,128)S(1)}, u32[]{:S(2)}, u32[]{:S(2)}) async-start(f32[16,8,384]{2,1,0:T(8,128)} %combine.1), calls=%async_computation.3 | async-start | bytes 393216 | tf_op jit(solution)/shard_map/all_to_all | solution.py:242
  105.9 4.1 %collective-permute-start.1 = (bf16[16,160,384]{2,1,0:T(8,128)(2,1)S(1)}, bf16[16,160,384]{2,1,0:T(8,128)(2,1)S(1)}, u32[]{:S(2)}, u32[]{:S(2)}) collective-permute-start(bf16[16,160,384]{2,1,0:T(8,128)(2,1)S(1)} %get-tuple-element.19), channel_id=1, source_target_pairs={{0,1},{1,0},{2,3},{3,2},{4,5},{5,4},{6,7},{7,6},{8,9},{9,8},{10,11... | collective-permute-start | bytes 5898248 | tf_op jit(solution)/shard_map/ppermute | solution.py:270
  110.5 30.2 %copy-start.1 = (s32[8,96]{1,0:T(8,128)S(1)}, s32[8,96]{1,0:T(8,128)}, u32[]{:S(2)}) copy-start(s32[8,96]{1,0:T(8,128)} %get-tuple-element.16.rank_ref) | copy-start | bytes 9220
  142.0 15.8 %all-to-all-start.5 = ((bf16[8,160,96]{2,1,0:T(8,128)(2,1)}), bf16[8,160,96]{2,1,0:T(8,128)(2,1)S(1)}, u32[]{:S(2)}, u32[]{:S(2)}) async-start(bf16[8,160,96]{2,1,0:T(8,128)(2,1)} %spread.1), calls=%async_computation.5 | async-start | bytes 655360 | tf_op jit(solution)/shard_map/all_to_all | solution.py:296
  157.8 0.7 copy-start.2

commit v2 on v1

--- a/solution.py
+++ b/solution.py
@@ -1,5 +1,3 @@
-import functools
-
 import jax
 import jax.numpy as jnp
 from jax import lax
@@ -17,7 +15,8 @@
 f32 = jnp.float32
 nt_dims = (((1,), (1,)), ((), ()))
 tn_dims = (((0,), (0,)), ((), ()))
-vmem = pltpu.CompilerParams(vmem_limit_bytes=48 * 1024 * 1024)
+small = pltpu.CompilerParams(vmem_limit_bytes=20 * 1024 * 1024)
+large = pltpu.CompilerParams(vmem_limit_bytes=60 * 1024 * 1024)
 
 
 def pack_kernel(hidden_ref, targets_ref, adv_ref, mask_ref, out_ref):
@@ -69,15 +68,6 @@
         rows_ref[other] = rows
 
 
-def row_tile(core, mine, partner):
-    first = jnp.where(core == 0, mine, partner)
-    second = jnp.where(core == 0, partner, mine)
-    pieces = []
-    for block in range(mine.shape[0]):
-        pieces += [first[block], second[block]]
-    return jnp.concatenate(pieces, axis=0)
-
-
 def meta_target(meta):
     return (meta[4:5] + 64.0 * meta[5:6] + 4096.0 * meta[6:7]).astype(jnp.int32)
 
@@ -91,22 +81,42 @@
     return column == meta_target(meta)
 
 
-def logits_kernel(place_ref, weight_ref, mine_ref, partner_ref, meta_ref, logits_ref, stats_ref):
-    step = pl.program_id(0)
-    tile = row_tile(place_ref[0], mine_ref[...], partner_ref[...])
-    part = jnp.dot(weight_ref[...], tile, preferred_element_type=f32)
-
+def prepare_kernel(place_ref, weight_ref, mine_ref, partner_ref):
+    for block in range(mine_ref.shape[1] // width):
+        pair = weight_ref[:, 2 * block * width : (2 * block + 2) * width]
+        first, second = pair[:, :width], pair[:, width:]
+        at = slice(block * width, (block + 1) * width)
+        own = place_ref[0] == 0
+        mine_ref[:, at] = jnp.where(own, first, second)
+        partner_ref[:, at] = jnp.where(own, second, first)
+
+
+def accumulate(step, out_ref, part):
     @pl.when(step == 0)
     def _():
-        logits_ref[...] = part
+        out_ref[...] = part
 
     @pl.when(step > 0)
     def _():
-        logits_ref[...] += part
+        out_ref[...] += part
+
+
+def first_half_kernel(weight_ref, rows_ref, out_ref):
+    rows = rows_ref[...].reshape(-1, policy)
+    accumulate(pl.program_id(0), out_ref, jnp.dot(weight_ref[...], rows, preferred_element_type=f32))
+
+
+def second_half_kernel(
+    place_ref, weight_ref, rows_ref, first_ref, meta_ref, logits_ref, stats_ref
+):
+    step = pl.program_id(0)
+    rows = rows_ref[...].reshape(-1, policy)
+    accumulate(step, logits_ref, jnp.dot(weight_ref[...], rows, preferred_element_type=f32))
 
     @pl.when(step == pl.num_programs(0) - 1)
     def _():
-        logits = logits_ref[...]
+        logits = logits_ref[...] + first_ref[...]
+        logits_ref[...] = logits
         top = jnp.max(logits, axis=0, keepdims=True)
         shifted = jnp.exp(logits - top)
         total = jnp.sum(shifted, axis=0, keepdims=True)
@@ -136,7 +146,7 @@
         out_ref[other] = stats
 
 
-def grad_kernel(place_ref, stats_ref, meta_ref, logits_ref, weight_ref, grad_ref, dlogits_ref, loss_ref):
+def sent_kernel(place_ref, stats_ref, meta_ref, logits_ref, weight_ref, out_ref, dlogits_ref, loss_ref):
     @pl.when(pl.program_id(0) == 0)
     def _():
         top, total, mix, chosen = combine(stats_ref[...])
@@ -154,23 +164,31 @@
         dlogits = (adv * (probs - hit) + entropy_coef * probs * (logits - mean)) / policy
         dlogits_ref[...] = dlogits.astype(bf16)
 
-    tile = lax.dot_general(weight_ref[...], dlogits_ref[...], tn_dims, preferred_element_type=f32)
-    tile = tile.astype(bf16)
-    for block in range(grad_ref.shape[1]):
-        for core in range(2):
-            at = (2 * block + core) * width
-            grad_ref[core, block] = tile[at : at + width]
+    out = lax.dot_general(weight_ref[...], dlogits_ref[...], tn_dims, preferred_element_type=f32)
+    out_ref[...] = out.astype(bf16).reshape(out_ref.shape)
+
+
+def kept_kernel(dlogits_ref, weight_ref, out_ref):
+    out = lax.dot_general(weight_ref[...], dlogits_ref[...], tn_dims, preferred_element_type=f32)
+    out_ref[...] = out.reshape(out_ref.shape)
 
 
 def head_kernel(place_ref, dlogits_ref, mine_ref, partner_ref, out_ref):
-    tile = row_tile(place_ref[0], mine_ref[...], partner_ref[...])
+    own = place_ref[0] == 0
+    mine, partner = mine_ref[...], partner_ref[...]
+    first = jnp.where(own, mine, partner)
+    second = jnp.where(own, partner, mine)
+    pieces = []
+    for block in range(mine.shape[0]):
+        pieces += [first[block], second[block]]
+    tile = jnp.concatenate(pieces, axis=0)
     out_ref[...] = lax.dot_general(
         dlogits_ref[...], tile, nt_dims, preferred_element_type=f32
     ).astype(bf16)
 
 
 def add_kernel(mine_ref, partner_ref, out_ref):
-    out_ref[...] = (mine_ref[...].astype(f32) + partner_ref[...].astype(f32)).astype(bf16)
+    out_ref[...] = (mine_ref[...] + partner_ref[...].astype(f32)).astype(bf16)
 
 
 def spread_kernel(parts_ref, rank_ref, out_ref):
@@ -187,6 +205,10 @@
 
 def shape(*dims, dtype=bf16):
     return jax.ShapeDtypeStruct(dims, dtype)
+
+
+def cost(flops, nbytes):
+    return pl.CostEstimate(flops=flops, bytes_accessed=nbytes, transcendentals=0)
 
 
 def body(hidden, head_weight, targets, advantage, policy_mask):
@@ -197,15 +219,36 @@
     place = jnp.stack([core, device * cols]).astype(jnp.int32)
     weight = head_weight.T
     depth = weight.shape[1]
+    half = depth // 2
     swap = [(0, 1), (1, 0)]
-    tiles = 4
-    tile = depth // tiles
+    tiles = 2
     blocks = n_plane // tiles
+    smem = pl.BlockSpec(memory_space=pltpu.SMEM)
+
+    def whole(*dims):
+        return pl.BlockSpec(dims, lambda *i: (0,) * len(dims))
 
     packed = pl.pallas_call(
-        pack_kernel, out_shape=shape(n_dp, width + meta_rows, tok), name="pack"
+        pack_kernel,
+        out_shape=shape(n_dp, width + meta_rows, tok),
+        compiler_params=large,
+        name="pack",
     )(hidden.T, targets[None], advantage[None], policy_mask[None])
+    packed, weight = lax.optimization_barrier((packed, weight))
     packed = lax.all_to_all(packed, "z", 0, 0)
+    weight_mine, weight_partner = pl.pallas_call(
+        prepare_kernel,
+        grid=(4,),
+        in_specs=[smem, pl.BlockSpec((cols, depth // 4), lambda i: (0, i))],
+        out_specs=[pl.BlockSpec((cols, half // 4), lambda i: (0, i))] * 2,
+        out_shape=(shape(cols, half), shape(cols, half)),
+        compiler_params=large,
+        cost_estimate=cost(0, 24_000_000),
+        name="prepare",
+    )(place, weight)
+    packed, weight_mine, weight_partner = lax.optimization_barrier(
+        (packed, weight_mine, weight_partner)
+    )
     rows, meta, rank = pl.pallas_call(
         compact_kernel,
         out_shape=(
@@ -213,88 +256,113 @@
             shape(meta_rows, policy, dtype=f32),
             shape(n_dp, tok, dtype=jnp.int32),
         ),
+        compiler_params=small,
         name="compact",
     )(packed)
     mine = lax.all_to_all(rows, ("x", "y"), 0, 0)
     partner = lax.ppermute(mine, "c", swap)
 
-    smem = pl.BlockSpec(memory_space=pltpu.SMEM)
-    weight_spec = pl.BlockSpec((cols, tile), lambda i: (0, i))
     rows_spec = pl.BlockSpec((blocks, width, policy), lambda i: (i, 0, 0))
-
-    def whole(*dims):
-        return pl.BlockSpec(dims, lambda i: (0,) * len(dims))
-
+    half_spec = pl.BlockSpec((cols, half // tiles), lambda i: (0, i))
+
+    first = pl.pallas_call(
+        first_half_kernel,
+        grid=(tiles,),
+        in_specs=[half_spec, rows_spec],
+        out_specs=whole(cols, policy),
+        out_shape=shape(cols, policy, dtype=f32),
+        compiler_params=small,
+        cost_estimate=cost(cols * depth * policy, 6_000_000),
+        name="first",
+    )(weight_mine, mine)
     logits, stats = pl.pallas_call(
-        logits_kernel,
-        grid=(tiles,),
-        in_specs=[smem, weight_spec, rows_spec, rows_spec, whole(meta_rows, policy)],
+        second_half_kernel,
+        grid=(tiles,),
+        in_specs=[smem, half_spec, rows_spec, whole(cols, policy), whole(meta_rows, policy)],
         out_specs=[whole(cols, policy), whole(2 * n_dp, 8, policy)],
-        out_shape=(shape(cols, policy, dtype=f32), shape(2 * n_dp, 8, policy, dtype=f32)),
-        compiler_params=vmem,
-        name="logits",
-    )(place, weight, mine, partner, meta)
+        out_shape=(
+            shape(cols, policy, dtype=f32),
+            shape(2 * n_dp, 8, policy, dtype=f32),
+        ),
+        compiler_params=small,
+        cost_estimate=cost(cols * depth * policy, 6_000_000),
+        name="second",
+    )(place, weight_partner, partner, first, meta)
 
     stats = lax.all_to_all(stats, ("z", "c"), 0, 0)
     stats = pl.pallas_call(
-        combine_kernel, out_shape=shape(n_plane, 8, policy, dtype=f32), name="combine"
+        combine_kernel,
+        out_shape=shape(n_plane, 8, policy, dtype=f32),
+        compiler_params=small,
+        name="combine",
     )(stats)
     stats = lax.all_to_all(stats, ("x", "y"), 0, 0)
 
-    grad, dlogits, loss = pl.pallas_call(
-        grad_kernel,
+    sent, dlogits, loss = pl.pallas_call(
+        sent_kernel,
         grid=(tiles,),
         in_specs=[
             smem,
             whole(n_plane, 8, policy),
             whole(meta_rows, policy),
             whole(cols, policy),
-            weight_spec,
+            half_spec,
         ],
-        out_specs=[
-            pl.BlockSpec((2, blocks, width, policy), lambda i: (0, i, 0, 0)),
-            whole(cols, policy),
-            whole(1, 1),
-        ],
+        out_specs=[rows_spec, whole(cols, policy), whole(1, 1)],
         out_shape=(
-            shape(2, n_plane, width, policy),
+            shape(n_plane, width, policy),
             shape(cols, policy),
             shape(1, 1, dtype=f32),
         ),
-        compiler_params=vmem,
-        name="grad",
-    )(place, stats, meta, logits, weight)
-
-    kept = lax.dynamic_index_in_dim(grad, core, 0, keepdims=False)
-    sent = lax.dynamic_index_in_dim(grad, 1 - core, 0, keepdims=False)
+        compiler_params=small,
+        cost_estimate=cost(cols * depth * policy, 6_000_000),
+        name="sent",
+    )(place, stats, meta, logits, weight_partner)
     got = lax.ppermute(sent, "c", swap)
-    head_grad = pl.pallas_call(
-        head_kernel,
-        grid=(tiles,),
-        in_specs=[smem, whole(cols, policy), rows_spec, rows_spec],
-        out_specs=weight_spec,
-        out_shape=shape(cols, depth),
-        compiler_params=vmem,
-        cost_estimate=pl.CostEstimate(
-            flops=2 * cols * depth * policy, bytes_accessed=10_000_000, transcendentals=0
-        ),
-        name="head",
-    )(place, dlogits, mine, partner)
+    kept = pl.pallas_call(
+        kept_kernel,
+        grid=(tiles,),
+        in_specs=[whole(cols, policy), half_spec],
+        out_specs=rows_spec,
+        out_shape=shape(n_plane, width, policy, dtype=f32),
+        compiler_params=small,
+        cost_estimate=cost(cols * depth * policy, 6_000_000),
+        name="kept",
+    )(dlogits, weight_mine)
     summed = pl.pallas_call(
         add_kernel,
         grid=(tiles,),
         in_specs=[rows_spec, rows_spec],
         out_specs=rows_spec,
         out_shape=shape(n_plane, width, policy),
-        compiler_params=vmem,
+        compiler_params=small,
         name="pair",
     )(kept, got)
     parts = lax.all_to_all(summed, ("x", "y"), 0, 0)
     spread = pl.pallas_call(
-        spread_kernel, out_shape=shape(n_dp, width, tok), compiler_params=vmem, name="spread"
+        spread_kernel, out_shape=shape(n_dp, width, tok), compiler_params=small, name="spread"
     )(parts, rank)
+    spread, dlogits = lax.optimization_barrier((spread, dlogits))
     parts = lax.all_to_all(spread, "z", 0, 0)
-    grad_rows = pl.pallas_call(sum_kernel, out_shape=shape(width, tok), name="total")(parts)
+    head_grad = pl.pallas_call(
+        head_kernel,
+        grid=(4,),
+        in_specs=[
+            smem,
+            whole(cols, policy),
+            pl.BlockSpec((n_plane // 4, width, policy), lambda i: (i, 0, 0)),
+            pl.BlockSpec((n_plane // 4, width, policy), lambda i: (i, 0, 0)),
+        ],
+        out_specs=pl.BlockSpec((cols, depth // 4), lambda i: (0, i)),
+        out_shape=shape(cols, depth),
+        compiler_params=large,
+        cost_estimate=cost(2 * cols * depth * policy, 10_000_000),
+        name="head",
+    )(place, dlogits, mine, partner)
+    parts, head_grad = lax.optimization_barrier((parts, head_grad))
+    grad_rows = pl.pallas_call(
+        sum_kernel, out_shape=shape(width, tok), compiler_params=small, name="total"
+    )(parts)
     return grad_rows.T, head_grad.T, loss[0, 0]
 
 

time: 161 us -> 147 us (0.913)
  blocking collectives: 97.4 us -> 87.1 us
  waiting for transfers between devices: 20.7 us -> 12.5 us
  starting transfers between devices: 8.83 us -> 11.9 us
  Pallas kernels: 31.3 us -> 33.2 us
    all_to_all x1, blocking collectives: 22.5 us -> 12.6 us  [body(): stats = lax.all_to_all(stats, ('x', 'y'), 0, 0)]
    pallas_call x4 -> x7, Pallas kernels: 23 us -> 29 us  [the longest x1 8.92 us: body(): pl.pallas_call(prepare_kernel, grid=(4,), in_specs=[smem, pl.BlockSpec((c...]
    all_to_all x1, starting transfers between devices: 5.31 us -> 8.47 us  [body(): packed = lax.all_to_all(packed, 'z', 0, 0)]
    all_to_all x1, waiting for transfers between devices: 7.16 us -> 4.41 us  [body(): packed = lax.all_to_all(packed, 'z', 0, 0)]
    ppermute x1, waiting for transfers between devices: 3.96 us -> 1.46 us  [body(): got = lax.ppermute(sent, 'c', swap)]
    ppermute x1, waiting for transfers between devices: 4.03 us -> 1.62 us  [body(): partner = lax.ppermute(mine, 'c', swap)]
    pallas_call x1, Pallas kernels: 3.05 us -> 0.79 us  [body(): pl.pallas_call(compact_kernel, out_shape=(shape(n_plane, width, policy),...]
  transfers between devices with their start and end apart: 4 -> 4, of which waited for: 4 -> 4; matrix products, arithmetic and copies ran while one was open for 0% -> 0% of each run, Pallas kernels for 4% -> 14%
where the time goes in v2:
time: 147 us; the launch traced here: 146 us
  blocking collectives  87.1 us (59%)
  Pallas kernels  33.2 us (23%)
  waiting for transfers between devices  12.5 us (9%)
  starting transfers between devices  11.9 us (8%)
    all_to_all x1, blocking collectives, body(): mine = lax.all_to_all(rows, ('x', 'y'), 0, 0)  31.5 us
    all_to_all x1, blocking collectives, body(): parts = lax.all_to_all(summed, ('x', 'y'), 0, 0)  30.1 us
    all_to_all x1, blocking collectives, body(): stats = lax.all_to_all(stats, ('z', 'c'), 0, 0)  13 us
    all_to_all x1, blocking collectives, body(): stats = lax.all_to_all(stats, ('x', 'y'), 0, 0)  12.6 us
    pallas_call x1, Pallas kernels, body(): pl.pallas_call(prepare_kernel, grid=(4,), in_specs=[smem, pl.BlockSpec((c...  8.92 us
    all_to_all x1, starting transfers between devices, body(): packed = lax.all_to_all(packed, 'z', 0, 0)  8.47 us
    pallas_call x1, Pallas kernels, body(): pl.pallas_call(head_kernel, grid=(4,), in_specs=[smem, whole(cols, policy...  7.27 us
    all_to_all x1, waiting for transfers between devices, body(): parts = lax.all_to_all(spread, 'z', 0, 0)  5.03 us
  transfers between devices with their start and end apart: 4, of which 4 were waited for; matrix products, arithmetic and copies ran while one was open for 0% of the time, Pallas kernels for 14%

profile of v2, /device:TPU:2, one launch (start us, length us, event | category | flops | bytes accessed | tf_op | source)
XLA Modules:
  0.0 146.2 jit_solution(16524763271005588604)
XLA Ops:
  0.6 1.6 %pack.1 = bf16[8,176,96]{2,1,0:T(8,128)(2,1)} custom-call(bf16[160,96]{1,0:T(8,128)(2,1)} %bitcast.12, s32[1,96]{1,0:T(1,128)} %bitcast.14, f32[1,96]{1,0:T(1,128)} %bitcast.15, s32[1,96]{1,0:T(1,128)} %bitcast.16), custom_call_target="tpu_custom_call" | custom-call | tf_op jit(solution)/shard_map/pack/pallas_call | solution.py:231
  2.2 8.5 %all-to-all-start = ((bf16[8,176,96]{2,1,0:T(8,128)(2,1)}), bf16[8,176,96]{2,1,0:T(8,128)(2,1)S(1)}, u32[]{:S(2)}, u32[]{:S(2)}) async-start(bf16[8,176,96]{2,1,0:T(8,128)(2,1)} %pack.1), calls=%async_computation | async-start | bytes 720896 | tf_op jit(solution)/shard_map/all_to_all | solution.py:238
  10.7 0.6 pad_add_fusion.place_ref
  11.3 8.9 %prepare.1 = (bf16[592,2560]{1,0:T(8,128)(2,1)}, bf16[592,2560]{1,0:T(8,128)(2,1)}) custom-call(s32[2]{0:T(128)} %pad_add_fusion.place_ref, bf16[592,5120]{1,0:T(8,128)(2,1)} %bitcast.10), custom_call_target="tpu_custom_call" | custom-call | bytes 24000000 | tf_op jit(solution)/shard_map/prepare/pallas_call | solution.py:239
  20.2 4.4 %all-to-all-done.blocks_ref = bf16[8,176,96]{2,1,0:T(8,128)(2,1)S(1)} async-done(((bf16[8,176,96]{2,1,0:T(8,128)(2,1)}), bf16[8,176,96]{2,1,0:T(8,128)(2,1)S(1)}, u32[]{:S(2)}, u32[]{:S(2)}) %all-to-all-start) | async-done | bytes 270368 | tf_op jit(solution)/shard_map/all_to_all | solution.py:238
  24.7 0.8 compact.1
  25.5 0.0 copy-start.1
  25.5 31.5 %all_to_all.30.rows_ref.mine_ref = bf16[16,160,384]{2,1,0:T(8,128)(2,1)S(1)} all-to-all(bf16[16,160,384]{2,1,0:T(8,128)(2,1)S(1)} %get-tuple-element.28), channel_id=1, replica_groups=mesh['z'=8,'x'=4,'y'=4,'c'=2] {'x','y'}, dimensions={0} | all-to-all | bytes 3932160 | tf_op jit(solution)/shard_map/all_to_all | solution.py:262
  56.9 0.0 copy-start
  56.9 0.0 copy-start.3
  56.9 0.0 copy-start.5
  56.9 0.0 collective-permute-start
  56.9 0.0 copy-done.1
  56.9 2.3 %first.1.first_ref = f32[592,384]{1,0:T(8,128)S(1)} custom-call(bf16[592,2560]{1,0:T(8,128)(2,1)S(1)} %copy-done.1, bf16[16,160,384]{2,1,0:T(8,128)(2,1)S(1)} %all_to_all.30.rows_ref.mine_ref), custom_call_target="tpu_custom_call" | custom-call | flops 1163919360 | bytes 6000000 | tf_op jit(solution)/shard_map/first/pallas_call | solution.py:268
  59.3 0.0 copy-done
  59.3 1.6 %collective-permute-done.rows_ref.partner_ref = bf16[16,160,384]{2,1,0:T(8,128)(2,1)S(1)} collective-permute-done((bf16[16,160,384]{2,1,0:T(8,128)(2,1)S(1)}, bf16[16,160,384]{2,1,0:T(8,128)(2,1)S(1)}, u32[]{:S(2)}, u32[]{:S(2)}) %collective-permute-start) | collective-permute-done | bytes 1966112 | tf_op jit(solution)/shard_map/ppermute | solution.py:263
  60.9 0.0 copy-start.2
  60.9 0.0 copy-done.3
  60.9 0.0 copy-done.5
  60.9 3.3 %second.1 = (f32[592,384]{1,0:T(8,128)S(1)}, f32[16,8,384]{2,1,0:T(8,128)S(1)}) custom-call(s32[2]{0:T(128)S(1)} %copy-done.5, bf16[592,2560]{1,0:T(8,128)(2,1)S(1)} %copy-done.3, bf16[16,160,384]{2,1,0:T(8,128)(2,1)S(1)} %collective-permute-done.rows_ref.partner_ref, f32[592,384]{1,0:T(8,128)S(1)} %first.1.first_ref, f32[16,384]{1,0:T(8,128)S(1)} %get-tuple-element.30.meta_ref), custom_call_target="tpu_custom_call" | custom-call | flops 1163919360 | bytes 6000000 | tf_op jit(solution)/shard_map/second/pallas_call | solution.py:278
  64.2 0.0 copy-done.2
  64.2 13.0 %all_to_all.31.in_ref = f32[16,8,384]{2,1,0:T(8,128)S(1)} all-to-all(f32[16,8,384]{2,1,0:T(8,128)S(1)} %get-tuple-element.31), channel_id=1, replica_groups=mesh['z'=8,'x'=4,'y'=4,'c'=2] {'z','c'}, dimensions={0} | all-to-all | bytes 393216 | tf_op jit(solution)/shard_map/all_to_all | solution.py:292
  77.2 0.1 combine.1
  77.3 12.6 %all_to_all.32.stats_ref = f32[16,8,384]{2,1,0:T(8,128)S(1)} all-to-all(f32[16,8,384]{2,1,0:T(8,128)S(1)} %combine.1), channel_id=1, replica_groups=mesh['z'=8,'x'=4,'y'=4,'c'=2] {'x','y'}, dimensions={0} | all-to-all | bytes 393216 | tf_op jit(solution)/shard_map/all_to_all | solution.py:299
  89.9 4.0 %sent.1 = (bf16[16,160,384]{2,1,0:T(8,128)(2,1)S(1)}, bf16[592,384]{1,0:T(8,128)(2,1)S(1)}, f32[1,1]{1,0:T(1,128)}) custom-call(s32[2]{0:T(128)S(1)} %copy-done.5, f32[16,8,384]{2,1,0:T(8,128)S(1)} %all_to_all.32.stats_ref, f32[16,384]{1,0:T(8,128)S(1)} %get-tuple-element.30.meta_ref, f32[592,384]{1,0:T(8,128)S(1)} %get-tuple-element.32.logits_ref, ...), custom_call_target="tpu_custom_call" | custom-call | flops 1163919360 | bytes 6000000 | tf_op jit(solution)/shard_map/sent/pallas_call | solution.py:301
  93.9 0.0 copy-start.4
  93.9 0.0 collective-permute-start.1
  93.9 2.5 %kept.1.mine_ref = f32[16,160,384]{2,1,0:T(8,128)S(1)} custom-call(bf16[592,384]{1,0:T(8,128)(2,1)S(1)} %get-tuple-element.37.dlogits_ref, bf16[592,2560]{1,0:T(8,128)(2,1)S(1)} %copy-done.1), custom_call_target="tpu_custom_call" | custom-call | flops 1163919360 | bytes 6000000 | tf_op jit(solution)/shard_map/kept/pallas_call | solution.py:322
  96.4 0.0 copy-done.4
  96.4 1.5 collective-permute-done.1.partner_ref
  97.8 0.4 pair.1
  98.2 30.1 %all_to_all.33.parts_ref = bf16[16,160,384]{2,1,0:T(8,128)(2,1)S(1)} all-to-all(bf16[16,160,384]{2,1,0:T(8,128)(2,1)S(1)} %pair.1), channel_id=1, replica_groups=mesh['z'=8,'x'=4,'y'=4,'c'=2] {'x','y'}, dimensions={0} | all-to-all | bytes 3932160 | tf_op jit(solution)/shard_map/all_to_all | solution.py:341
  128.3 1.4 spread.1
  129.7 3.4 %all-to-all-start.5 = ((bf16[8,160,96]{2,1,0:T(8,128)(2,1)}), bf16[8,160,96]{2,1,0:T(8,128)(2,1)S(1)}, u32[]{:S(2)}, u32[]{:S(2)}) async-start(bf16[8,160,96]{2,1,0:T(8,128)(2,1)} %spread.1), calls=%async_computation.5 | async-start | bytes 655360 | tf_op jit(solution)/shard_map/all_to_all | solution.py:346
  133.2 7.3 %head.1 = bf16[592,5120]{1,0:T(8,128)(2,1)} custom-call(s32[2]{0:T(128)} %pad_add_fusion.place_ref, bf16[592,384]{1,0:T(8,128)(2,1)} %copy-done.4, bf16[16,160,384]{2,1,0:T(8,128)(2,1)} %copy-done, bf16[16,160,384]{2,1,0:T(8,128)(2,1)} %copy-done.2), custom_call_target="tpu_custom_call" | custom-call | flops 2327838720 | bytes 10000000 | tf_op jit(solution)/shard_map/head/pallas_call | solution.py:347
  140.4 5.0 %all-to-all-done.5.parts_ref = bf16[8,160,96]{2,1,0:T(8,128)(2,1)S(1)} async-done(((bf16[8,160,96]{2,1,0:T(8,128)(2,1)}), bf16[8,160,96]{2,1,0:T(8,128)(2,1)S(1)}, u32[]{:S(2)}, u32[]{:S(2)}) %all-to-all-start.5) | async-done | bytes 245792 | tf_op jit(solution)/shard_map/all_to_all | solution.py:346
  145.5 0.7 total.1
Async XLA Ops:
  2.2 22.4 %all-to-all-start = ((bf16[8,176,96]{2,1,0:T(8,128)(2,1)}), bf16[8,176,96]{2,1,0:T(8,128)(2,1)S(1)}, u32[]{:S(2)}, u32[]{:S(2)}) async-start(bf16[8,176,96]{2,1,0:T(8,128)(2,1)} %pack.1), calls=%async_computation | async-start | bytes 720896 | tf_op jit(solution)/shard_map/all_to_all | solution.py:238
  25.5 31.5 %copy-start.1 = (bf16[592,2560]{1,0:T(8,128)(2,1)S(1)}, bf16[592,2560]{1,0:T(8,128)(2,1)}, u32[]{:S(2)}) copy-start(bf16[592,2560]{1,0:T(8,128)(2,1)} %get-tuple-element.29.weight_ref) | copy-start | bytes 9093124
  56.9 2.3 %copy-start = (bf16[16,160,384]{2,1,0:T(8,128)(2,1)}, bf16[16,160,384]{2,1,0:T(8,128)(2,1)S(1)}, u32[]{:S(2)}) copy-start(bf16[16,160,384]{2,1,0:T(8,128)(2,1)S(1)} %all_to_all.30.rows_ref.mine_ref) | copy-start | bytes 5898244
  56.9 4.0 %copy-start.3 = (bf16[592,2560]{1,0:T(8,128)(2,1)S(1)}, bf16[592,2560]{1,0:T(8,128)(2,1)}, u32[]{:S(2)}) copy-start(bf16[592,2560]{1,0:T(8,128)(2,1)} %get-tuple-element.26.weight_ref) | copy-start | bytes 9093124
  56.9 4.0 %copy-start.5 = (s32[2]{0:T(128)S(1)}, s32[2]{0:T(128)}, u32[]{:S(2)}) copy-start(s32[2]{0:T(128)} %pad_add_fusion.place_ref) | copy-start | bytes 28
  56.9 4.0 %collective-permute-start = (bf16[16,160,384]{2,1,0:T(8,128)(2,1)S(1)}, bf16[16,160,384]{2,1,0:T(8,128)(2,1)S(1)}, u32[]{:S(2)}, u32[]{:S(2)}) collective-permute-start(bf16[16,160,384]{2,1,0:T(8,128)(2,1)S(1)} %all_to_all.30.rows_ref.mine_ref), channel_id=1, source_target_pairs={{0,1},{1,0},{2,3},{3,2},{4,5},{5,4},{6,7},{7,6},{8,9},{9,8},{10,11... | collective-permute-start | bytes 5898248 | tf_op jit(solution)/shard_map/ppermute | solution.py:263
  60.9 3.3 %copy-start.2 = (bf16[16,160,384]{2,1,0:T(8,128)(2,1)}, bf16[16,160,384]{2,1,0:T(8,128)(2,1)S(1)}, u32[]{:S(2)}) copy-start(bf16[16,160,384]{2,1,0:T(8,128)(2,1)S(1)} %collective-permute-done.rows_ref.partner_ref) | copy-start | bytes 5898244
  93.9 2.5 %copy-start.4 = (bf16[592,384]{1,0:T(8,128)(2,1)}, bf16[592,384]{1,0:T(8,128)(2,1)S(1)}, u32[]{:S(2)}) copy-start(bf16[592,384]{1,0:T(8,128)(2,1)S(1)} %get-tuple-element.37.dlogits_ref) | copy-start | bytes 1363972
  93.9 4.0 %collective-permute-start.1 = (bf16[16,160,384]{2,1,0:T(8,128)(2,1)S(1)}, bf16[16,160,384]{2,1,0:T(8,128)(2,1)S(1)}, u32[]{:S(2)}, u32[]{:S(2)}) collective-permute-start(bf16[16,160,384]{2,1,0:T(8,128)(2,1)S(1)} %get-tuple-element.34), channel_id=1, source_target_pairs={{0,1},{1,0},{2,3},{3,2},{4,5},{5,4},{6,7},{7,6},{8,9},{9,8},{10,11... | collective-permute-start | bytes 5898248 | tf_op jit(solution)/shard_map/ppermute | solution.py:321
  129.7 15.7 %all-to-all-start.5 = ((bf16[8,160,96]{2,1,0:T(8,128)(2,1)}), bf16[8,160,96]{2,1,0:T(8,128)(2,1)S(1)}, u32[]{:S(2)}, u32[]{:S(2)}) async-start(bf16[8,160,96]{2,1,0:T(8,128)(2,1)} %spread.1), calls=%async_computation.5 | async-start | bytes 655360 | tf_op jit(solution)/shard_map/all_to_all | solution.py:346

commit v3 on v2

--- a/solution.py
+++ b/solution.py
@@ -17,6 +17,16 @@
 tn_dims = (((0,), (0,)), ((), ()))
 small = pltpu.CompilerParams(vmem_limit_bytes=20 * 1024 * 1024)
 large = pltpu.CompilerParams(vmem_limit_bytes=60 * 1024 * 1024)
+
+
+def fold(block, corner):
+    rest = [block[128:, at : at + 32] for at in (0, 32, 64)]
+    return jnp.concatenate([block[:128], jnp.concatenate(rest + [corner], axis=0)], axis=1)
+
+
+def unfold(folded):
+    rest = [folded[at : at + 32, tok:] for at in (0, 32, 64)]
+    return jnp.concatenate([folded[:, :tok], jnp.concatenate(rest, axis=1)], axis=0)
 
 
 def pack_kernel(hidden_ref, targets_ref, adv_ref, mask_ref, out_ref):
@@ -35,18 +45,22 @@
         ((targets >> 6) & 63).astype(f32),
         (targets >> 12).astype(f32),
     ]
-    rows.append(jnp.zeros((meta_rows - len(rows), tok), f32))
-    meta = jnp.concatenate(rows, axis=0).astype(bf16)
+    rows.append(jnp.zeros((1, tok), f32))
+    meta = jnp.concatenate(rows, axis=0)
+    pieces = [meta[:, at : at + 32] for at in (0, 32, 64)] + [jnp.zeros((8, 32), f32)]
+    meta = jnp.concatenate(pieces, axis=0).astype(bf16)
+    packed = fold(hidden_ref[...], meta)
     for z in range(out_ref.shape[0]):
-        out_ref[z, :width, :] = hidden_ref[...]
-        out_ref[z, width:, :] = meta
+        out_ref[z] = packed
 
 
 def compact_kernel(blocks_ref, rows_ref, meta_ref, rank_ref):
     groups = blocks_ref.shape[0]
-    mask = jnp.concatenate(
-        [blocks_ref[z, width : width + meta_rows, :].astype(f32)[:1] for z in range(groups)], axis=0
-    )
+    metas = []
+    for z in range(groups):
+        corner = blocks_ref[z, 96:, :].astype(f32)[:, tok:]
+        metas.append(jnp.concatenate([corner[at : at + 8] for at in (0, 8, 16)], axis=1))
+    mask = jnp.concatenate([meta[:1] for meta in metas], axis=0)
     before = lax.broadcasted_iota(jnp.int32, (tok, tok), 0) < lax.broadcasted_iota(jnp.int32, (tok, tok), 1)
     prefix = jnp.dot(mask.astype(bf16), before.astype(bf16), preferred_element_type=f32)
     total = jnp.broadcast_to(jnp.sum(mask, axis=1, keepdims=True), mask.shape)
@@ -61,7 +75,9 @@
     acc = jnp.zeros((width + meta_rows, policy), f32)
     for z in range(groups):
         pick = (place == rank[z : z + 1]).astype(f32).astype(bf16)
-        acc += lax.dot_general(blocks_ref[z], pick, nt_dims, preferred_element_type=f32)
+        meta = jnp.concatenate([metas[z], jnp.zeros_like(metas[z])], axis=0).astype(bf16)
+        block = jnp.concatenate([unfold(blocks_ref[z]), meta], axis=0)
+        acc += lax.dot_general(block, pick, nt_dims, preferred_element_type=f32)
     meta_ref[...] = acc[width:]
     rows = acc[:width].astype(bf16)
     for other in range(rows_ref.shape[0]):
@@ -81,14 +97,15 @@
     return column == meta_target(meta)
 
 
-def prepare_kernel(place_ref, weight_ref, mine_ref, partner_ref):
-    for block in range(mine_ref.shape[1] // width):
-        pair = weight_ref[:, 2 * block * width : (2 * block + 2) * width]
-        first, second = pair[:, :width], pair[:, width:]
-        at = slice(block * width, (block + 1) * width)
-        own = place_ref[0] == 0
-        mine_ref[:, at] = jnp.where(own, first, second)
-        partner_ref[:, at] = jnp.where(own, second, first)
+def prepare_kernel(place_ref, weight_ref, kept_ref, sent_ref):
+    for core, (first_ref, second_ref) in enumerate([(kept_ref, sent_ref), (sent_ref, kept_ref)]):
+
+        @pl.when(place_ref[0] == core)
+        def _():
+            for block in range(kept_ref.shape[1] // width):
+                at = slice(block * width, (block + 1) * width)
+                first_ref[:, at] = weight_ref[:, 2 * block * width : (2 * block + 1) * width]
+                second_ref[:, at] = weight_ref[:, (2 * block + 1) * width : (2 * block + 2) * width]
 
 
 def accumulate(step, out_ref, part):
@@ -124,7 +141,7 @@
         chosen = jnp.sum(
             jnp.where(column_is_target(place_ref, meta_ref[...]), logits, 0.0), axis=0, keepdims=True
         )
-        stats = jnp.concatenate([top, total, mix, chosen, jnp.zeros((4, policy), f32)], axis=0)
+        stats = jnp.concatenate([top, total, mix, chosen], axis=0)
         for other in range(stats_ref.shape[0]):
             stats_ref[other] = stats
 
@@ -141,36 +158,36 @@
 
 def combine_kernel(in_ref, out_ref):
     top, total, mix, chosen = combine(in_ref[...])
-    stats = jnp.concatenate([top, total, mix, chosen, jnp.zeros((4, policy), f32)], axis=0)
+    stats = jnp.concatenate([top, total, mix, chosen], axis=0)
     for other in range(out_ref.shape[0]):
         out_ref[other] = stats
 
 
-def sent_kernel(place_ref, stats_ref, meta_ref, logits_ref, weight_ref, out_ref, dlogits_ref, loss_ref):
-    @pl.when(pl.program_id(0) == 0)
-    def _():
-        top, total, mix, chosen = combine(stats_ref[...])
-        meta = meta_ref[...]
-        adv = meta_advantage(meta)
-        mean = mix / total
-        log_total = top + jnp.log(total)
-        loss = jnp.sum(
-            adv * (chosen - log_total) + entropy_coef * (log_total - mean), axis=1, keepdims=True
-        )
-        loss_ref[...] = -loss / policy
-        logits = logits_ref[...]
-        probs = jnp.exp(logits - top) / total
-        hit = column_is_target(place_ref, meta).astype(f32)
-        dlogits = (adv * (probs - hit) + entropy_coef * probs * (logits - mean)) / policy
-        dlogits_ref[...] = dlogits.astype(bf16)
-
-    out = lax.dot_general(weight_ref[...], dlogits_ref[...], tn_dims, preferred_element_type=f32)
-    out_ref[...] = out.astype(bf16).reshape(out_ref.shape)
-
-
-def kept_kernel(dlogits_ref, weight_ref, out_ref):
+def dlogits_kernel(place_ref, stats_ref, meta_ref, logits_ref, dlogits_ref, loss_ref):
+    top, total, mix, chosen = combine(stats_ref[...])
+    meta = meta_ref[...]
+    adv = meta_advantage(meta)
+    mean = mix / total
+    log_total = top + jnp.log(total)
+    loss = jnp.sum(
+        adv * (chosen - log_total) + entropy_coef * (log_total - mean), axis=1, keepdims=True
+    )
+    loss_ref[...] = -loss / policy
+    logits = logits_ref[...]
+    probs = jnp.exp(logits - top) / total
+    hit = column_is_target(place_ref, meta).astype(f32)
+    dlogits = (adv * (probs - hit) + entropy_coef * probs * (logits - mean)) / policy
+    dlogits_ref[...] = dlogits.astype(bf16)
+
+
+def grad_own_kernel(dlogits_ref, weight_ref, out_ref):
     out = lax.dot_general(weight_ref[...], dlogits_ref[...], tn_dims, preferred_element_type=f32)
     out_ref[...] = out.reshape(out_ref.shape)
+
+
+def grad_sum_kernel(dlogits_ref, weight_ref, own_ref, out_ref):
+    out = lax.dot_general(weight_ref[...], dlogits_ref[...], tn_dims, preferred_element_type=f32)
+    out_ref[...] = (own_ref[...] + out.reshape(out_ref.shape)).astype(bf16)
 
 
 def head_kernel(place_ref, dlogits_ref, mine_ref, partner_ref, out_ref):
@@ -187,20 +204,17 @@
     ).astype(bf16)
 
 
-def add_kernel(mine_ref, partner_ref, out_ref):
-    out_ref[...] = (mine_ref[...] + partner_ref[...].astype(f32)).astype(bf16)
-
-
 def spread_kernel(parts_ref, rank_ref, out_ref):
     total = jnp.sum(parts_ref[...].astype(f32), axis=0).astype(bf16)
     place = lax.broadcasted_iota(jnp.int32, (policy, tok), 0)
     for z in range(out_ref.shape[0]):
         pick = (place == rank_ref[z : z + 1, :]).astype(f32).astype(bf16)
-        out_ref[z] = jnp.dot(total, pick, preferred_element_type=f32).astype(bf16)
+        rows = jnp.dot(total, pick, preferred_element_type=f32)
+        out_ref[z] = fold(rows, jnp.zeros((32, 32), f32)).astype(bf16)
 
 
 def sum_kernel(parts_ref, out_ref):
-    out_ref[...] = jnp.sum(parts_ref[...].astype(f32), axis=0).astype(bf16)
+    out_ref[...] = unfold(jnp.sum(parts_ref[...].astype(f32), axis=0)).astype(bf16)
 
 
 def shape(*dims, dtype=bf16):
@@ -230,13 +244,13 @@
 
     packed = pl.pallas_call(
         pack_kernel,
-        out_shape=shape(n_dp, width + meta_rows, tok),
+        out_shape=shape(n_dp, 128, 128),
         compiler_params=large,
         name="pack",
     )(hidden.T, targets[None], advantage[None], policy_mask[None])
     packed, weight = lax.optimization_barrier((packed, weight))
     packed = lax.all_to_all(packed, "z", 0, 0)
-    weight_mine, weight_partner = pl.pallas_call(
+    weight_own, weight_sent = pl.pallas_call(
         prepare_kernel,
         grid=(4,),
         in_specs=[smem, pl.BlockSpec((cols, depth // 4), lambda i: (0, i))],
@@ -246,9 +260,7 @@
         cost_estimate=cost(0, 24_000_000),
         name="prepare",
     )(place, weight)
-    packed, weight_mine, weight_partner = lax.optimization_barrier(
-        (packed, weight_mine, weight_partner)
-    )
+    packed, weight_own, weight_sent = lax.optimization_barrier((packed, weight_own, weight_sent))
     rows, meta, rank = pl.pallas_call(
         compact_kernel,
         out_shape=(
@@ -274,73 +286,64 @@
         compiler_params=small,
         cost_estimate=cost(cols * depth * policy, 6_000_000),
         name="first",
-    )(weight_mine, mine)
+    )(weight_own, mine)
     logits, stats = pl.pallas_call(
         second_half_kernel,
         grid=(tiles,),
         in_specs=[smem, half_spec, rows_spec, whole(cols, policy), whole(meta_rows, policy)],
-        out_specs=[whole(cols, policy), whole(2 * n_dp, 8, policy)],
+        out_specs=[whole(cols, policy), whole(2 * n_dp, 4, policy)],
         out_shape=(
             shape(cols, policy, dtype=f32),
-            shape(2 * n_dp, 8, policy, dtype=f32),
+            shape(2 * n_dp, 4, policy, dtype=f32),
         ),
         compiler_params=small,
         cost_estimate=cost(cols * depth * policy, 6_000_000),
         name="second",
-    )(place, weight_partner, partner, first, meta)
-
+    )(place, weight_sent, partner, first, meta)
+
+    logits, weight_sent = lax.optimization_barrier((logits, weight_sent))
+    weight_got = lax.ppermute(weight_sent, "c", swap)
     stats = lax.all_to_all(stats, ("z", "c"), 0, 0)
     stats = pl.pallas_call(
         combine_kernel,
-        out_shape=shape(n_plane, 8, policy, dtype=f32),
+        out_shape=shape(n_plane, 4, policy, dtype=f32),
         compiler_params=small,
         name="combine",
     )(stats)
     stats = lax.all_to_all(stats, ("x", "y"), 0, 0)
-
-    sent, dlogits, loss = pl.pallas_call(
-        sent_kernel,
-        grid=(tiles,),
-        in_specs=[
-            smem,
-            whole(n_plane, 8, policy),
-            whole(meta_rows, policy),
-            whole(cols, policy),
-            half_spec,
-        ],
-        out_specs=[rows_spec, whole(cols, policy), whole(1, 1)],
-        out_shape=(
-            shape(n_plane, width, policy),
-            shape(cols, policy),
-            shape(1, 1, dtype=f32),
-        ),
-        compiler_params=small,
-        cost_estimate=cost(cols * depth * policy, 6_000_000),
-        name="sent",
-    )(place, stats, meta, logits, weight_partner)
-    got = lax.ppermute(sent, "c", swap)
-    kept = pl.pallas_call(
-        kept_kernel,
+    stats, weight_got = lax.optimization_barrier((stats, weight_got))
+
+    dlogits, loss = pl.pallas_call(
+        dlogits_kernel,
+        in_specs=[smem] + [pl.BlockSpec(memory_space=pltpu.VMEM)] * 3,
+        out_shape=(shape(cols, policy), shape(1, 1, dtype=f32)),
+        compiler_params=small,
+        name="dlogits",
+    )(place, stats, meta, logits)
+    dlogits_got = lax.ppermute(dlogits, "c", swap)
+    grad_own = pl.pallas_call(
+        grad_own_kernel,
         grid=(tiles,),
         in_specs=[whole(cols, policy), half_spec],
         out_specs=rows_spec,
         out_shape=shape(n_plane, width, policy, dtype=f32),
         compiler_params=small,
         cost_estimate=cost(cols * depth * policy, 6_000_000),
-        name="kept",
-    )(dlogits, weight_mine)
+        name="grad_own",
+    )(dlogits, weight_own)
     summed = pl.pallas_call(
-        add_kernel,
+        grad_sum_kernel,
         grid=(tiles,),
-        in_specs=[rows_spec, rows_spec],
+        in_specs=[whole(cols, policy), half_spec, rows_spec],
         out_specs=rows_spec,
         out_shape=shape(n_plane, width, policy),
         compiler_params=small,
-        name="pair",
-    )(kept, got)
+        cost_estimate=cost(cols * depth * policy, 6_000_000),
+        name="grad_sum",
+    )(dlogits_got, weight_got, grad_own)
     parts = lax.all_to_all(summed, ("x", "y"), 0, 0)
     spread = pl.pallas_call(
-        spread_kernel, out_shape=shape(n_dp, width, tok), compiler_params=small, name="spread"
+        spread_kernel, out_shape=shape(n_dp, 128, 128), compiler_params=small, name="spread"
     )(parts, rank)
     spread, dlogits = lax.optimization_barrier((spread, dlogits))
     parts = lax.all_to_all(spread, "z", 0, 0)

time: 147 us -> 140 us (0.952)
  blocking collectives: 87.1 us -> 84.4 us
  waiting for transfers between devices: 12.5 us -> 10 us
  Pallas kernels: 33.2 us -> 31.4 us
    pallas_call x1, Pallas kernels: 8.92 us -> 6.77 us  [body(): pl.pallas_call(prepare_kernel, grid=(4,), in_specs=[smem, pl.BlockSpec((c...]
  transfers between devices with their start and end apart: 4 -> 5, of which waited for: 4 -> 3; matrix products, arithmetic and copies ran while one was open for 0% -> 0% of each run, Pallas kernels for 14% -> 14%
where the time goes in v3:
time: 140 us; the launch traced here: 139 us
  blocking collectives  84.4 us (60%)
  Pallas kernels  31.4 us (22%)
  starting transfers between devices  12.1 us (9%)
  waiting for transfers between devices  10 us (7%)
    all_to_all x1, blocking collectives, body(): mine = lax.all_to_all(rows, ('x', 'y'), 0, 0)  30.4 us
    all_to_all x1, blocking collectives, body(): parts = lax.all_to_all(summed, ('x', 'y'), 0, 0)  30.1 us
    all_to_all x1, blocking collectives, body(): stats = lax.all_to_all(stats, ('z', 'c'), 0, 0)  12.2 us
    all_to_all x1, blocking collectives, body(): stats = lax.all_to_all(stats, ('x', 'y'), 0, 0)  11.7 us
    all_to_all x1, starting transfers between devices, body(): packed = lax.all_to_all(packed, 'z', 0, 0)  8.47 us
    pallas_call x1, Pallas kernels, body(): pl.pallas_call(head_kernel, grid=(4,), in_specs=[smem, whole(cols, policy...  7.26 us
    pallas_call x1, Pallas kernels, body(): pl.pallas_call(prepare_kernel, grid=(4,), in_specs=[smem, pl.BlockSpec((c...  6.77 us
    all_to_all x1, waiting for transfers between devices, body(): packed = lax.all_to_all(packed, 'z', 0, 0)  4.49 us
  transfers between devices with their start and end apart: 5, of which 3 were waited for; matrix products, arithmetic and copies ran while one was open for 0% of the time, Pallas kernels for 14%

profile of v3, /device:TPU:2, one launch (start us, length us, event | category | flops | bytes accessed | tf_op | source)
XLA Modules:
  0.0 139.4 jit_solution(3618734126619948516)
XLA Ops:
  0.6 1.7 %pack.1 = bf16[8,128,128]{2,1,0:T(8,128)(2,1)} custom-call(bf16[160,96]{1,0:T(8,128)(2,1)} %bitcast.12, s32[1,96]{1,0:T(1,128)} %bitcast.14, f32[1,96]{1,0:T(1,128)} %bitcast.15, s32[1,96]{1,0:T(1,128)} %bitcast.16), custom_call_target="tpu_custom_call" | custom-call | tf_op jit(solution)/shard_map/pack/pallas_call | solution.py:245
  2.3 8.5 %all-to-all-start = ((bf16[8,128,128]{2,1,0:T(8,128)(2,1)}), bf16[8,128,128]{2,1,0:T(8,128)(2,1)S(1)}, u32[]{:S(2)}, u32[]{:S(2)}) async-start(bf16[8,128,128]{2,1,0:T(8,128)(2,1)} %pack.1), calls=%async_computation | async-start | bytes 524288 | tf_op jit(solution)/shard_map/all_to_all | solution.py:252
  10.8 0.6 pad_add_fusion.place_ref
  11.4 6.8 %prepare.1 = (bf16[592,2560]{1,0:T(8,128)(2,1)}, bf16[592,2560]{1,0:T(8,128)(2,1)}) custom-call(s32[2]{0:T(128)} %pad_add_fusion.place_ref, bf16[592,5120]{1,0:T(8,128)(2,1)} %bitcast.10), custom_call_target="tpu_custom_call" | custom-call | bytes 24000000 | tf_op jit(solution)/shard_map/prepare/pallas_call | solution.py:253
  18.2 4.5 %all-to-all-done.blocks_ref = bf16[8,128,128]{2,1,0:T(8,128)(2,1)S(1)} async-done(((bf16[8,128,128]{2,1,0:T(8,128)(2,1)}), bf16[8,128,128]{2,1,0:T(8,128)(2,1)S(1)}, u32[]{:S(2)}, u32[]{:S(2)}) %all-to-all-start) | async-done | bytes 262176 | tf_op jit(solution)/shard_map/all_to_all | solution.py:252
  22.6 0.0 copy-start.1
  22.6 0.9 compact.1
  23.5 30.4 %all_to_all.30.rows_ref.mine_ref = bf16[16,160,384]{2,1,0:T(8,128)(2,1)S(1)} all-to-all(bf16[16,160,384]{2,1,0:T(8,128)(2,1)S(1)} %get-tuple-element.31), channel_id=1, replica_groups=mesh['z'=8,'x'=4,'y'=4,'c'=2] {'x','y'}, dimensions={0} | all-to-all | bytes 3932160 | tf_op jit(solution)/shard_map/all_to_all | solution.py:274
  53.9 0.0 copy-start
  53.9 0.0 copy-start.3
  53.9 0.0 copy-start.5
  53.9 0.0 collective-permute-start
  54.0 0.0 copy-done.1
  54.0 2.3 %first.1.first_ref = f32[592,384]{1,0:T(8,128)S(1)} custom-call(bf16[592,2560]{1,0:T(8,128)(2,1)S(1)} %copy-done.1, bf16[16,160,384]{2,1,0:T(8,128)(2,1)S(1)} %all_to_all.30.rows_ref.mine_ref), custom_call_target="tpu_custom_call" | custom-call | flops 1163919360 | bytes 6000000 | tf_op jit(solution)/shard_map/first/pallas_call | solution.py:280
  56.3 1.6 %collective-permute-done.rows_ref.partner_ref = bf16[16,160,384]{2,1,0:T(8,128)(2,1)S(1)} collective-permute-done((bf16[16,160,384]{2,1,0:T(8,128)(2,1)S(1)}, bf16[16,160,384]{2,1,0:T(8,128)(2,1)S(1)}, u32[]{:S(2)}, u32[]{:S(2)}) %collective-permute-start) | collective-permute-done | bytes 1966112 | tf_op jit(solution)/shard_map/ppermute | solution.py:275
  57.9 0.0 copy-start.2
  57.9 0.0 copy-done.3
  57.9 0.0 copy-done.5
  57.9 3.3 %second.1 = (f32[592,384]{1,0:T(8,128)S(1)}, f32[16,4,384]{2,1,0:T(4,128)S(1)}) custom-call(s32[2]{0:T(128)S(1)} %copy-done.5, bf16[592,2560]{1,0:T(8,128)(2,1)S(1)} %copy-done.3, bf16[16,160,384]{2,1,0:T(8,128)(2,1)S(1)} %collective-permute-done.rows_ref.partner_ref, f32[592,384]{1,0:T(8,128)S(1)} %first.1.first_ref, f32[16,384]{1,0:T(8,128)S(1)} %get-tuple-element.33.meta_ref), custom_call_target="tpu_custom_call" | custom-call | flops 1163919360 | bytes 6000000 | tf_op jit(solution)/shard_map/second/pallas_call | solution.py:290
  61.2 0.0 copy-done
  61.2 0.2 collective-permute-start.1
  61.4 12.2 %all_to_all.31.in_ref = f32[16,4,384]{2,1,0:T(4,128)S(1)} all-to-all(f32[16,4,384]{2,1,0:T(4,128)S(1)} %get-tuple-element.34), channel_id=1, replica_groups=mesh['z'=8,'x'=4,'y'=4,'c'=2] {'z','c'}, dimensions={0} | all-to-all | bytes 196608 | tf_op jit(solution)/shard_map/all_to_all | solution.py:306
  73.6 0.0 copy-done.2
  73.6 0.1 combine.1
  73.7 11.7 %all_to_all.32.stats_ref = f32[16,4,384]{2,1,0:T(4,128)S(1)} all-to-all(f32[16,4,384]{2,1,0:T(4,128)S(1)} %combine.1), channel_id=1, replica_groups=mesh['z'=8,'x'=4,'y'=4,'c'=2] {'x','y'}, dimensions={0} | all-to-all | bytes 196608 | tf_op jit(solution)/shard_map/all_to_all | solution.py:313
  85.4 0.0 collective-permute-done.1.weight_ref
  85.4 1.7 %dlogits.1 = (bf16[592,384]{1,0:T(8,128)(2,1)S(1)}, f32[1,1]{1,0:T(1,128)}) custom-call(s32[2]{0:T(128)S(1)} %copy-done.5, f32[16,4,384]{2,1,0:T(4,128)S(1)} %all_to_all.32.stats_ref, f32[16,384]{1,0:T(8,128)S(1)} %get-tuple-element.33.meta_ref, f32[592,384]{1,0:T(8,128)S(1)} %get-tuple-element.38.logits_ref), custom_call_target="tpu_custom_call" | custom-call | tf_op jit(solution)/shard_map/dlogits/pallas_call | solution.py:316
  87.1 0.0 copy-start.4
  87.1 0.0 collective-permute-start.2
  87.1 2.5 %grad_own.1.own_ref = f32[16,160,384]{2,1,0:T(8,128)S(1)} custom-call(bf16[592,384]{1,0:T(8,128)(2,1)S(1)} %get-tuple-element.43.dlogits_ref, bf16[592,2560]{1,0:T(8,128)(2,1)S(1)} %copy-done.1), custom_call_target="tpu_custom_call" | custom-call | flops 1163919360 | bytes 6000000 | tf_op jit(solution)/shard_map/grad_own/pallas_call | solution.py:324
  89.6 0.0 copy-done.4
  89.6 0.0 collective-permute-done.2.dlogits_ref
  89.6 2.6 %grad_sum.1 = bf16[16,160,384]{2,1,0:T(8,128)(2,1)S(1)} custom-call(bf16[592,384]{1,0:T(8,128)(2,1)S(1)} %collective-permute-done.2.dlogits_ref, bf16[592,2560]{1,0:T(8,128)(2,1)S(1)} %collective-permute-done.1.weight_ref, f32[16,160,384]{2,1,0:T(8,128)S(1)} %grad_own.1.own_ref), custom_call_target="tpu_custom_call" | custom-call | flops 1163919360 | bytes 6000000 | tf_op jit(solution)/shard_map/grad_sum/pallas_call | solution.py:334
  92.2 30.1 %all_to_all.33.parts_ref = bf16[16,160,384]{2,1,0:T(8,128)(2,1)S(1)} all-to-all(bf16[16,160,384]{2,1,0:T(8,128)(2,1)S(1)} %grad_sum.1), channel_id=1, replica_groups=mesh['z'=8,'x'=4,'y'=4,'c'=2] {'x','y'}, dimensions={0} | all-to-all | bytes 3932160 | tf_op jit(solution)/shard_map/all_to_all | solution.py:344
  122.3 1.7 %spread.1 = bf16[8,128,128]{2,1,0:T(8,128)(2,1)} custom-call(bf16[16,160,384]{2,1,0:T(8,128)(2,1)S(1)} %all_to_all.33.parts_ref, s32[8,96]{1,0:T(8,128)S(1)} %get-tuple-element.41.rank_ref), custom_call_target="tpu_custom_call" | custom-call | tf_op jit(solution)/shard_map/spread/pallas_call | solution.py:345
  124.1 3.4 %all-to-all-start.5 = ((bf16[8,128,128]{2,1,0:T(8,128)(2,1)}), bf16[8,128,128]{2,1,0:T(8,128)(2,1)S(1)}, u32[]{:S(2)}, u32[]{:S(2)}) async-start(bf16[8,128,128]{2,1,0:T(8,128)(2,1)} %spread.1), calls=%async_computation.5 | async-start | bytes 524288 | tf_op jit(solution)/shard_map/all_to_all | solution.py:349
  127.5 7.3 %head.1 = bf16[592,5120]{1,0:T(8,128)(2,1)} custom-call(s32[2]{0:T(128)} %pad_add_fusion.place_ref, bf16[592,384]{1,0:T(8,128)(2,1)} %copy-done.4, bf16[16,160,384]{2,1,0:T(8,128)(2,1)} %copy-done, bf16[16,160,384]{2,1,0:T(8,128)(2,1)} %copy-done.2), custom_call_target="tpu_custom_call" | custom-call | flops 2327838720 | bytes 10000000 | tf_op jit(solution)/shard_map/head/pallas_call | solution.py:350
  134.7 3.9 %all-to-all-done.5.parts_ref = bf16[8,128,128]{2,1,0:T(8,128)(2,1)S(1)} async-done(((bf16[8,128,128]{2,1,0:T(8,128)(2,1)}), bf16[8,128,128]{2,1,0:T(8,128)(2,1)S(1)}, u32[]{:S(2)}, u32[]{:S(2)}) %all-to-all-start.5) | async-done | bytes 262176 | tf_op jit(solution)/shard_map/all_to_all | solution.py:349
  138.7 0.7 total.1
Async XLA Ops:
  2.3 20.3 %all-to-all-start = ((bf16[8,128,128]{2,1,0:T(8,128)(2,1)}), bf16[8,128,128]{2,1,0:T(8,128)(2,1)S(1)}, u32[]{:S(2)}, u32[]{:S(2)}) async-start(bf16[8,128,128]{2,1,0:T(8,128)(2,1)} %pack.1), calls=%async_computation | async-start | bytes 524288 | tf_op jit(solution)/shard_map/all_to_all | solution.py:252
  22.6 31.3 %copy-start.1 = (bf16[592,2560]{1,0:T(8,128)(2,1)S(1)}, bf16[592,2560]{1,0:T(8,128)(2,1)}, u32[]{:S(2)}) copy-start(bf16[592,2560]{1,0:T(8,128)(2,1)} %get-tuple-element.32.weight_ref) | copy-start | bytes 9093124
  53.9 7.3 %copy-start = (bf16[16,160,384]{2,1,0:T(8,128)(2,1)}, bf16[16,160,384]{2,1,0:T(8,128)(2,1)S(1)}, u32[]{:S(2)}) copy-start(bf16[16,160,384]{2,1,0:T(8,128)(2,1)S(1)} %all_to_all.30.rows_ref.mine_ref) | copy-start | bytes 5898244
  53.9 4.0 %copy-start.3 = (bf16[592,2560]{1,0:T(8,128)(2,1)S(1)}, bf16[592,2560]{1,0:T(8,128)(2,1)}, u32[]{:S(2)}) copy-start(bf16[592,2560]{1,0:T(8,128)(2,1)} %get-tuple-element.36.weight_ref) | copy-start | bytes 9093124
  53.9 4.0 %copy-start.5 = (s32[2]{0:T(128)S(1)}, s32[2]{0:T(128)}, u32[]{:S(2)}) copy-start(s32[2]{0:T(128)} %pad_add_fusion.place_ref) | copy-start | bytes 28
  53.9 4.0 %collective-permute-start = (bf16[16,160,384]{2,1,0:T(8,128)(2,1)S(1)}, bf16[16,160,384]{2,1,0:T(8,128)(2,1)S(1)}, u32[]{:S(2)}, u32[]{:S(2)}) collective-permute-start(bf16[16,160,384]{2,1,0:T(8,128)(2,1)S(1)} %all_to_all.30.rows_ref.mine_ref), channel_id=1, source_target_pairs={{0,1},{1,0},{2,3},{3,2},{4,5},{5,4},{6,7},{7,6},{8,9},{9,8},{10,11... | collective-permute-start | bytes 5898248 | tf_op jit(solution)/shard_map/ppermute | solution.py:275
  57.9 15.7 %copy-start.2 = (bf16[16,160,384]{2,1,0:T(8,128)(2,1)}, bf16[16,160,384]{2,1,0:T(8,128)(2,1)S(1)}, u32[]{:S(2)}) copy-start(bf16[16,160,384]{2,1,0:T(8,128)(2,1)S(1)} %collective-permute-done.rows_ref.partner_ref) | copy-start | bytes 5898244
  61.2 24.2 %collective-permute-start.1 = (bf16[592,2560]{1,0:T(8,128)(2,1)S(1)}, bf16[592,2560]{1,0:T(8,128)(2,1)S(1)}, u32[]{:S(2)}, u32[]{:S(2)}) collective-permute-start(bf16[592,2560]{1,0:T(8,128)(2,1)S(1)} %copy-done.3), channel_id=1, source_target_pairs={{0,1},{1,0},{2,3},{3,2},{4,5},{5,4},{6,7},{7,6},{8,9},{9,8},{10,11... | collective-permute-start | bytes 9093128 | tf_op jit(solution)/shard_map/ppermute | solution.py:305
  87.1 2.5 %copy-start.4 = (bf16[592,384]{1,0:T(8,128)(2,1)}, bf16[592,384]{1,0:T(8,128)(2,1)S(1)}, u32[]{:S(2)}) copy-start(bf16[592,384]{1,0:T(8,128)(2,1)S(1)} %get-tuple-element.43.dlogits_ref) | copy-start | bytes 1363972
  87.1 2.5 %collective-permute-start.2 = (bf16[592,384]{1,0:T(8,128)(2,1)S(1)}, bf16[592,384]{1,0:T(8,128)(2,1)S(1)}, u32[]{:S(2)}, u32[]{:S(2)}) collective-permute-start(bf16[592,384]{1,0:T(8,128)(2,1)S(1)} %get-tuple-element.43.dlogits_ref), channel_id=1, source_target_pairs={{0,1},{1,0},{2,3},{3,2},{4,5},{5,4},{6,7},{7,6},{8,9},{9,8},{10,11... | collective-permute-start | bytes 1363976 | tf_op jit(solution)/shard_map/ppermute | solution.py:323
  124.1 14.6 %all-to-all-start.5 = ((bf16[8,128,128]{2,1,0:T(8,128)(2,1)}), bf16[8,128,128]{2,1,0:T(8,128)(2,1)S(1)}, u32[]{:S(2)}, u32[]{:S(2)}) async-start(bf16[8,128,128]{2,1,0:T(8,128)(2,1)} %spread.1), calls=%async_computation.5 | async-start | bytes 524288 | tf_op jit(solution)/shard_map/all_to_all | solution.py:349

commit v4 on v3

--- a/solution.py
+++ b/solution.py
@@ -54,7 +54,7 @@
         out_ref[z] = packed
 
 
-def compact_kernel(blocks_ref, rows_ref, meta_ref, rank_ref):
+def compact_kernel(blocks_ref, rows_ref, meta_ref, picks_ref):
     groups = blocks_ref.shape[0]
     metas = []
     for z in range(groups):
@@ -70,11 +70,11 @@
         starts.append(start)
         start = start + total[z : z + 1]
     rank = jnp.where(mask > 0, prefix + jnp.concatenate(starts, axis=0), -1.0).astype(jnp.int32)
-    rank_ref[...] = rank
     place = lax.broadcasted_iota(jnp.int32, (policy, tok), 0)
     acc = jnp.zeros((width + meta_rows, policy), f32)
     for z in range(groups):
         pick = (place == rank[z : z + 1]).astype(f32).astype(bf16)
+        picks_ref[z] = pick
         meta = jnp.concatenate([metas[z], jnp.zeros_like(metas[z])], axis=0).astype(bf16)
         block = jnp.concatenate([unfold(blocks_ref[z]), meta], axis=0)
         acc += lax.dot_general(block, pick, nt_dims, preferred_element_type=f32)
@@ -108,42 +108,27 @@
                 second_ref[:, at] = weight_ref[:, (2 * block + 1) * width : (2 * block + 2) * width]
 
 
-def accumulate(step, out_ref, part):
-    @pl.when(step == 0)
-    def _():
-        out_ref[...] = part
-
-    @pl.when(step > 0)
-    def _():
-        out_ref[...] += part
-
-
 def first_half_kernel(weight_ref, rows_ref, out_ref):
     rows = rows_ref[...].reshape(-1, policy)
-    accumulate(pl.program_id(0), out_ref, jnp.dot(weight_ref[...], rows, preferred_element_type=f32))
+    out_ref[...] = jnp.dot(weight_ref[...], rows, preferred_element_type=f32)
 
 
 def second_half_kernel(
     place_ref, weight_ref, rows_ref, first_ref, meta_ref, logits_ref, stats_ref
 ):
-    step = pl.program_id(0)
     rows = rows_ref[...].reshape(-1, policy)
-    accumulate(step, logits_ref, jnp.dot(weight_ref[...], rows, preferred_element_type=f32))
-
-    @pl.when(step == pl.num_programs(0) - 1)
-    def _():
-        logits = logits_ref[...] + first_ref[...]
-        logits_ref[...] = logits
-        top = jnp.max(logits, axis=0, keepdims=True)
-        shifted = jnp.exp(logits - top)
-        total = jnp.sum(shifted, axis=0, keepdims=True)
-        mix = jnp.sum(shifted * logits, axis=0, keepdims=True)
-        chosen = jnp.sum(
-            jnp.where(column_is_target(place_ref, meta_ref[...]), logits, 0.0), axis=0, keepdims=True
-        )
-        stats = jnp.concatenate([top, total, mix, chosen], axis=0)
-        for other in range(stats_ref.shape[0]):
-            stats_ref[other] = stats
+    logits = first_ref[...] + jnp.dot(weight_ref[...], rows, preferred_element_type=f32)
+    logits_ref[...] = logits
+    top = jnp.max(logits, axis=0, keepdims=True)
+    shifted = jnp.exp(logits - top)
+    total = jnp.sum(shifted, axis=0, keepdims=True)
+    mix = jnp.sum(shifted * logits, axis=0, keepdims=True)
+    chosen = jnp.sum(
+        jnp.where(column_is_target(place_ref, meta_ref[...]), logits, 0.0), axis=0, keepdims=True
+    )
+    stats = jnp.concatenate([top, total, mix, chosen], axis=0)
+    for other in range(stats_ref.shape[0]):
+        stats_ref[other] = stats
 
 
 def combine(stats):
@@ -174,10 +159,11 @@
     )
     loss_ref[...] = -loss / policy
     logits = logits_ref[...]
-    probs = jnp.exp(logits - top) / total
-    hit = column_is_target(place_ref, meta).astype(f32)
-    dlogits = (adv * (probs - hit) + entropy_coef * probs * (logits - mean)) / policy
-    dlogits_ref[...] = dlogits.astype(bf16)
+    share = 1.0 / (total * policy)
+    spread = entropy_coef * share
+    dlogits = jnp.exp(logits - top) * (adv * share + spread * (logits - mean))
+    hit = jnp.where(column_is_target(place_ref, meta), adv / policy, 0.0)
+    dlogits_ref[...] = (dlogits - hit).astype(bf16)
 
 
 def grad_own_kernel(dlogits_ref, weight_ref, out_ref):
@@ -190,26 +176,38 @@
     out_ref[...] = (own_ref[...] + out.reshape(out_ref.shape)).astype(bf16)
 
 
-def head_kernel(place_ref, dlogits_ref, mine_ref, partner_ref, out_ref):
-    own = place_ref[0] == 0
-    mine, partner = mine_ref[...], partner_ref[...]
-    first = jnp.where(own, mine, partner)
-    second = jnp.where(own, partner, mine)
-    pieces = []
-    for block in range(mine.shape[0]):
-        pieces += [first[block], second[block]]
-    tile = jnp.concatenate(pieces, axis=0)
-    out_ref[...] = lax.dot_general(
-        dlogits_ref[...], tile, nt_dims, preferred_element_type=f32
-    ).astype(bf16)
-
-
-def spread_kernel(parts_ref, rank_ref, out_ref):
+def head_kernel(place_ref, dlogits_ref, mine_ref, partner_ref, out_ref, rows_ref, slots_ref, sems):
+    for core, (first, second) in enumerate([(mine_ref, partner_ref), (partner_ref, mine_ref)]):
+
+        @pl.when(place_ref[0] == core)
+        def _():
+            for block in range(first.shape[0]):
+                rows_ref[block, 0] = first[block]
+                rows_ref[block, 1] = second[block]
+
+    count = slots_ref.shape[0]
+    step = slots_ref.shape[2]
+    blocks = rows_ref.shape[0] // count
+
+    def send(part):
+        return pltpu.make_async_copy(
+            slots_ref.at[part], out_ref.at[:, part * step : (part + 1) * step], sems.at[part]
+        )
+
+    for part in range(count):
+        rows = rows_ref[part * blocks : (part + 1) * blocks].reshape(step, policy)
+        slots_ref[part] = lax.dot_general(
+            dlogits_ref[...], rows, nt_dims, preferred_element_type=f32
+        ).astype(bf16)
+        send(part).start()
+    for part in range(count):
+        send(part).wait()
+
+
+def spread_kernel(parts_ref, picks_ref, out_ref):
     total = jnp.sum(parts_ref[...].astype(f32), axis=0).astype(bf16)
-    place = lax.broadcasted_iota(jnp.int32, (policy, tok), 0)
     for z in range(out_ref.shape[0]):
-        pick = (place == rank_ref[z : z + 1, :]).astype(f32).astype(bf16)
-        rows = jnp.dot(total, pick, preferred_element_type=f32)
+        rows = jnp.dot(total, picks_ref[z], preferred_element_type=f32)
         out_ref[z] = fold(rows, jnp.zeros((32, 32), f32)).astype(bf16)
 
 
@@ -235,12 +233,8 @@
     depth = weight.shape[1]
     half = depth // 2
     swap = [(0, 1), (1, 0)]
-    tiles = 2
-    blocks = n_plane // tiles
     smem = pl.BlockSpec(memory_space=pltpu.SMEM)
-
-    def whole(*dims):
-        return pl.BlockSpec(dims, lambda *i: (0,) * len(dims))
+    local = pl.BlockSpec(memory_space=pltpu.VMEM)
 
     packed = pl.pallas_call(
         pack_kernel,
@@ -252,21 +246,21 @@
     packed = lax.all_to_all(packed, "z", 0, 0)
     weight_own, weight_sent = pl.pallas_call(
         prepare_kernel,
-        grid=(4,),
-        in_specs=[smem, pl.BlockSpec((cols, depth // 4), lambda i: (0, i))],
-        out_specs=[pl.BlockSpec((cols, half // 4), lambda i: (0, i))] * 2,
+        grid=(2,),
+        in_specs=[smem, pl.BlockSpec((cols, depth // 2), lambda i: (0, i))],
+        out_specs=[pl.BlockSpec((cols, half // 2), lambda i: (0, i))] * 2,
         out_shape=(shape(cols, half), shape(cols, half)),
         compiler_params=large,
         cost_estimate=cost(0, 24_000_000),
         name="prepare",
     )(place, weight)
     packed, weight_own, weight_sent = lax.optimization_barrier((packed, weight_own, weight_sent))
-    rows, meta, rank = pl.pallas_call(
+    rows, meta, picks = pl.pallas_call(
         compact_kernel,
         out_shape=(
             shape(n_plane, width, policy),
             shape(meta_rows, policy, dtype=f32),
-            shape(n_dp, tok, dtype=jnp.int32),
+            shape(n_dp, policy, tok),
         ),
         compiler_params=small,
         name="compact",
@@ -274,14 +268,8 @@
     mine = lax.all_to_all(rows, ("x", "y"), 0, 0)
     partner = lax.ppermute(mine, "c", swap)
 
-    rows_spec = pl.BlockSpec((blocks, width, policy), lambda i: (i, 0, 0))
-    half_spec = pl.BlockSpec((cols, half // tiles), lambda i: (0, i))
-
     first = pl.pallas_call(
         first_half_kernel,
-        grid=(tiles,),
-        in_specs=[half_spec, rows_spec],
-        out_specs=whole(cols, policy),
         out_shape=shape(cols, policy, dtype=f32),
         compiler_params=small,
         cost_estimate=cost(cols * depth * policy, 6_000_000),
@@ -289,9 +277,7 @@
     )(weight_own, mine)
     logits, stats = pl.pallas_call(
         second_half_kernel,
-        grid=(tiles,),
-        in_specs=[smem, half_spec, rows_spec, whole(cols, policy), whole(meta_rows, policy)],
-        out_specs=[whole(cols, policy), whole(2 * n_dp, 4, policy)],
+        in_specs=[smem] + [local] * 4,
         out_shape=(
             shape(cols, policy, dtype=f32),
             shape(2 * n_dp, 4, policy, dtype=f32),
@@ -315,7 +301,7 @@
 
     dlogits, loss = pl.pallas_call(
         dlogits_kernel,
-        in_specs=[smem] + [pl.BlockSpec(memory_space=pltpu.VMEM)] * 3,
+        in_specs=[smem] + [local] * 3,
         out_shape=(shape(cols, policy), shape(1, 1, dtype=f32)),
         compiler_params=small,
         name="dlogits",
@@ -323,9 +309,6 @@
     dlogits_got = lax.ppermute(dlogits, "c", swap)
     grad_own = pl.pallas_call(
         grad_own_kernel,
-        grid=(tiles,),
-        in_specs=[whole(cols, policy), half_spec],
-        out_specs=rows_spec,
         out_shape=shape(n_plane, width, policy, dtype=f32),
         compiler_params=small,
         cost_estimate=cost(cols * depth * policy, 6_000_000),
@@ -333,9 +316,6 @@
     )(dlogits, weight_own)
     summed = pl.pallas_call(
         grad_sum_kernel,
-        grid=(tiles,),
-        in_specs=[whole(cols, policy), half_spec, rows_spec],
-        out_specs=rows_spec,
         out_shape=shape(n_plane, width, policy),
         compiler_params=small,
         cost_estimate=cost(cols * depth * policy, 6_000_000),
@@ -344,20 +324,19 @@
     parts = lax.all_to_all(summed, ("x", "y"), 0, 0)
     spread = pl.pallas_call(
         spread_kernel, out_shape=shape(n_dp, 128, 128), compiler_params=small, name="spread"
-    )(parts, rank)
+    )(parts, picks)
     spread, dlogits = lax.optimization_barrier((spread, dlogits))
     parts = lax.all_to_all(spread, "z", 0, 0)
     head_grad = pl.pallas_call(
         head_kernel,
-        grid=(4,),
-        in_specs=[
-            smem,
-            whole(cols, policy),
-            pl.BlockSpec((n_plane // 4, width, policy), lambda i: (i, 0, 0)),
-            pl.BlockSpec((n_plane // 4, width, policy), lambda i: (i, 0, 0)),
+        in_specs=[smem] + [local] * 3,
+        out_specs=pl.BlockSpec(memory_space=pl.ANY),
+        out_shape=shape(cols, depth),
+        scratch_shapes=[
+            pltpu.VMEM((n_plane, 2, width, policy), bf16),
+            pltpu.VMEM((4, cols, depth // 4), bf16),
+            pltpu.SemaphoreType.DMA((4,)),
         ],
-        out_specs=pl.BlockSpec((cols, depth // 4), lambda i: (0, i)),
-        out_shape=shape(cols, depth),
         compiler_params=large,
         cost_estimate=cost(2 * cols * depth * policy, 10_000_000),
         name="head",

time: 140 us -> 138 us (0.986)
  Pallas kernels: 31.4 us -> 28.1 us
  waiting for transfers between devices: 10 us -> 11.8 us
    pallas_call x7, Pallas kernels: 26.4 us -> 23 us  [the longest x1 7.19 us: body(): pl.pallas_call(head_kernel, in_specs=[smem] + [local] * 3, out_specs=pl.B...]
  transfers between devices with their start and end apart: 5 -> 5, of which waited for: 3 -> 3; matrix products, arithmetic and copies ran while one was open for 0% -> 0% of each run, Pallas kernels for 14% -> 12%
where the time goes in v4:
time: 138 us; the launch traced here: 137 us
  blocking collectives  83.4 us (60%)
  Pallas kernels  28.1 us (20%)
  starting transfers between devices  12.1 us (9%)
  waiting for transfers between devices  11.8 us (9%)
    all_to_all x1, blocking collectives, body(): mine = lax.all_to_all(rows, ('x', 'y'), 0, 0)  30.3 us
    all_to_all x1, blocking collectives, body(): parts = lax.all_to_all(summed, ('x', 'y'), 0, 0)  30.1 us
    all_to_all x1, blocking collectives, body(): stats = lax.all_to_all(stats, ('x', 'y'), 0, 0)  11.7 us
    all_to_all x1, blocking collectives, body(): stats = lax.all_to_all(stats, ('z', 'c'), 0, 0)  11.2 us
    all_to_all x1, starting transfers between devices, body(): packed = lax.all_to_all(packed, 'z', 0, 0)  8.47 us
    pallas_call x1, Pallas kernels, body(): pl.pallas_call(head_kernel, in_specs=[smem] + [local] * 3, out_specs=pl.B...  7.19 us
    all_to_all x1, waiting for transfers between devices, body(): packed = lax.all_to_all(packed, 'z', 0, 0)  5.66 us
    pallas_call x1, Pallas kernels, body(): pl.pallas_call(prepare_kernel, grid=(2,), in_specs=[smem, pl.BlockSpec((c...  5.6 us
  transfers between devices with their start and end apart: 5, of which 3 were waited for; matrix products, arithmetic and copies ran while one was open for 0% of the time, Pallas kernels for 12%

profile of v4, /device:TPU:2, one launch (start us, length us, event | category | flops | bytes accessed | tf_op | source)
XLA Modules:
  0.0 136.8 jit_solution(16556994693011102672)
XLA Ops:
  0.6 1.7 %pack.1 = bf16[8,128,128]{2,1,0:T(8,128)(2,1)} custom-call(bf16[160,96]{1,0:T(8,128)(2,1)} %bitcast.12, s32[1,96]{1,0:T(1,128)} %bitcast.14, f32[1,96]{1,0:T(1,128)} %bitcast.15, s32[1,96]{1,0:T(1,128)} %bitcast.16), custom_call_target="tpu_custom_call" | custom-call | tf_op jit(solution)/shard_map/pack/pallas_call | solution.py:239
  2.3 8.5 %all-to-all-start = ((bf16[8,128,128]{2,1,0:T(8,128)(2,1)}), bf16[8,128,128]{2,1,0:T(8,128)(2,1)S(1)}, u32[]{:S(2)}, u32[]{:S(2)}) async-start(bf16[8,128,128]{2,1,0:T(8,128)(2,1)} %pack.1), calls=%async_computation | async-start | bytes 524288 | tf_op jit(solution)/shard_map/all_to_all | solution.py:246
  10.8 0.6 pad_add_fusion.place_ref
  11.4 5.6 %prepare.1 = (bf16[592,2560]{1,0:T(8,128)(2,1)}, bf16[592,2560]{1,0:T(8,128)(2,1)}) custom-call(s32[2]{0:T(128)} %pad_add_fusion.place_ref, bf16[592,5120]{1,0:T(8,128)(2,1)} %bitcast.10), custom_call_target="tpu_custom_call" | custom-call | bytes 24000000 | tf_op jit(solution)/shard_map/prepare/pallas_call | solution.py:247
  17.0 5.7 %all-to-all-done.blocks_ref = bf16[8,128,128]{2,1,0:T(8,128)(2,1)S(1)} async-done(((bf16[8,128,128]{2,1,0:T(8,128)(2,1)}), bf16[8,128,128]{2,1,0:T(8,128)(2,1)S(1)}, u32[]{:S(2)}, u32[]{:S(2)}) %all-to-all-start) | async-done | bytes 262176 | tf_op jit(solution)/shard_map/all_to_all | solution.py:246
  22.6 0.0 copy-start.1
  22.6 0.9 compact.1
  23.6 30.3 %all_to_all.30.rows_ref.mine_ref = bf16[16,160,384]{2,1,0:T(8,128)(2,1)S(1)} all-to-all(bf16[16,160,384]{2,1,0:T(8,128)(2,1)S(1)} %get-tuple-element.31), channel_id=1, replica_groups=mesh['z'=8,'x'=4,'y'=4,'c'=2] {'x','y'}, dimensions={0} | all-to-all | bytes 3932160 | tf_op jit(solution)/shard_map/all_to_all | solution.py:268
  53.8 0.0 copy-start
  53.8 0.0 copy-start.3
  53.9 0.0 copy-start.5
  53.9 0.0 collective-permute-start
  53.9 0.0 copy-done.1
  53.9 1.7 %first.1.first_ref = f32[592,384]{1,0:T(8,128)S(1)} custom-call(bf16[592,2560]{1,0:T(8,128)(2,1)S(1)} %copy-done.1, bf16[16,160,384]{2,1,0:T(8,128)(2,1)S(1)} %all_to_all.30.rows_ref.mine_ref), custom_call_target="tpu_custom_call" | custom-call | flops 1163919360 | bytes 6000000 | tf_op jit(solution)/shard_map/first/pallas_call | solution.py:271
  55.6 2.2 %collective-permute-done.rows_ref.partner_ref = bf16[16,160,384]{2,1,0:T(8,128)(2,1)S(1)} collective-permute-done((bf16[16,160,384]{2,1,0:T(8,128)(2,1)S(1)}, bf16[16,160,384]{2,1,0:T(8,128)(2,1)S(1)}, u32[]{:S(2)}, u32[]{:S(2)}) %collective-permute-start) | collective-permute-done | bytes 1966112 | tf_op jit(solution)/shard_map/ppermute | solution.py:269
  57.8 0.0 copy-start.2
  57.8 0.0 copy-done.3
  57.8 0.0 copy-done.5
  57.8 2.5 %second.1 = (f32[592,384]{1,0:T(8,128)S(1)}, f32[16,4,384]{2,1,0:T(4,128)S(1)}) custom-call(s32[2]{0:T(128)S(1)} %copy-done.5, bf16[592,2560]{1,0:T(8,128)(2,1)S(1)} %copy-done.3, bf16[16,160,384]{2,1,0:T(8,128)(2,1)S(1)} %collective-permute-done.rows_ref.partner_ref, f32[592,384]{1,0:T(8,128)S(1)} %first.1.first_ref, f32[16,384]{1,0:T(8,128)S(1)} %get-tuple-element.33.meta_ref), custom_call_target="tpu_custom_call" | custom-call | flops 1163919360 | bytes 6000000 | tf_op jit(solution)/shard_map/second/pallas_call | solution.py:278
  60.4 0.0 copy-done
  60.4 0.2 collective-permute-start.1
  60.6 11.2 %all_to_all.31.in_ref = f32[16,4,384]{2,1,0:T(4,128)S(1)} all-to-all(f32[16,4,384]{2,1,0:T(4,128)S(1)} %get-tuple-element.34), channel_id=1, replica_groups=mesh['z'=8,'x'=4,'y'=4,'c'=2] {'z','c'}, dimensions={0} | all-to-all | bytes 196608 | tf_op jit(solution)/shard_map/all_to_all | solution.py:292
  71.9 0.0 copy-done.2
  71.9 0.1 combine.1
  72.0 11.7 %all_to_all.32.stats_ref = f32[16,4,384]{2,1,0:T(4,128)S(1)} all-to-all(f32[16,4,384]{2,1,0:T(4,128)S(1)} %combine.1), channel_id=1, replica_groups=mesh['z'=8,'x'=4,'y'=4,'c'=2] {'x','y'}, dimensions={0} | all-to-all | bytes 196608 | tf_op jit(solution)/shard_map/all_to_all | solution.py:299
  83.7 0.0 collective-permute-done.1.weight_ref
  83.7 1.6 %dlogits.1 = (bf16[592,384]{1,0:T(8,128)(2,1)S(1)}, f32[1,1]{1,0:T(1,128)}) custom-call(s32[2]{0:T(128)S(1)} %copy-done.5, f32[16,4,384]{2,1,0:T(4,128)S(1)} %all_to_all.32.stats_ref, f32[16,384]{1,0:T(8,128)S(1)} %get-tuple-element.33.meta_ref, f32[592,384]{1,0:T(8,128)S(1)} %get-tuple-element.38.logits_ref), custom_call_target="tpu_custom_call" | custom-call | tf_op jit(solution)/shard_map/dlogits/pallas_call | solution.py:302
  85.3 0.0 copy-start.4
  85.3 0.0 collective-permute-start.2
  85.3 2.1 %grad_own.1.own_ref = f32[16,160,384]{2,1,0:T(8,128)S(1)} custom-call(bf16[592,384]{1,0:T(8,128)(2,1)S(1)} %get-tuple-element.43.dlogits_ref, bf16[592,2560]{1,0:T(8,128)(2,1)S(1)} %copy-done.1), custom_call_target="tpu_custom_call" | custom-call | flops 1163919360 | bytes 6000000 | tf_op jit(solution)/shard_map/grad_own/pallas_call | solution.py:310
  87.4 0.0 copy-done.4
  87.4 0.0 collective-permute-done.2.dlogits_ref
  87.4 2.2 %grad_sum.1 = bf16[16,160,384]{2,1,0:T(8,128)(2,1)S(1)} custom-call(bf16[592,384]{1,0:T(8,128)(2,1)S(1)} %collective-permute-done.2.dlogits_ref, bf16[592,2560]{1,0:T(8,128)(2,1)S(1)} %collective-permute-done.1.weight_ref, f32[16,160,384]{2,1,0:T(8,128)S(1)} %grad_own.1.own_ref), custom_call_target="tpu_custom_call" | custom-call | flops 1163919360 | bytes 6000000 | tf_op jit(solution)/shard_map/grad_sum/pallas_call | solution.py:317
  89.7 30.1 %all_to_all.33.parts_ref = bf16[16,160,384]{2,1,0:T(8,128)(2,1)S(1)} all-to-all(bf16[16,160,384]{2,1,0:T(8,128)(2,1)S(1)} %grad_sum.1), channel_id=1, replica_groups=mesh['z'=8,'x'=4,'y'=4,'c'=2] {'x','y'}, dimensions={0} | all-to-all | bytes 3932160 | tf_op jit(solution)/shard_map/all_to_all | solution.py:324
  119.8 1.7 %spread.1 = bf16[8,128,128]{2,1,0:T(8,128)(2,1)} custom-call(bf16[16,160,384]{2,1,0:T(8,128)(2,1)S(1)} %all_to_all.33.parts_ref, bf16[8,384,96]{2,1,0:T(8,128)(2,1)S(1)} %get-tuple-element.41.picks_ref), custom_call_target="tpu_custom_call" | custom-call | tf_op jit(solution)/shard_map/spread/pallas_call | solution.py:325
  121.5 3.4 %all-to-all-start.5 = ((bf16[8,128,128]{2,1,0:T(8,128)(2,1)}), bf16[8,128,128]{2,1,0:T(8,128)(2,1)S(1)}, u32[]{:S(2)}, u32[]{:S(2)}) async-start(bf16[8,128,128]{2,1,0:T(8,128)(2,1)} %spread.1), calls=%async_computation.5 | async-start | bytes 524288 | tf_op jit(solution)/shard_map/all_to_all | solution.py:329
  124.9 7.2 %head.1 = bf16[592,5120]{1,0:T(8,128)(2,1)} custom-call(s32[2]{0:T(128)} %pad_add_fusion.place_ref, bf16[592,384]{1,0:T(8,128)(2,1)} %copy-done.4, bf16[16,160,384]{2,1,0:T(8,128)(2,1)} %copy-done, bf16[16,160,384]{2,1,0:T(8,128)(2,1)} %copy-done.2), custom_call_target="tpu_custom_call" | custom-call | flops 2327838720 | bytes 10000000 | tf_op jit(solution)/shard_map/head/pallas_call | solution.py:330
  132.1 4.0 %all-to-all-done.5.parts_ref = bf16[8,128,128]{2,1,0:T(8,128)(2,1)S(1)} async-done(((bf16[8,128,128]{2,1,0:T(8,128)(2,1)}), bf16[8,128,128]{2,1,0:T(8,128)(2,1)S(1)}, u32[]{:S(2)}, u32[]{:S(2)}) %all-to-all-start.5) | async-done | bytes 262176 | tf_op jit(solution)/shard_map/all_to_all | solution.py:329
  136.1 0.7 total.1
Async XLA Ops:
  2.3 20.3 %all-to-all-start = ((bf16[8,128,128]{2,1,0:T(8,128)(2,1)}), bf16[8,128,128]{2,1,0:T(8,128)(2,1)S(1)}, u32[]{:S(2)}, u32[]{:S(2)}) async-start(bf16[8,128,128]{2,1,0:T(8,128)(2,1)} %pack.1), calls=%async_computation | async-start | bytes 524288 | tf_op jit(solution)/shard_map/all_to_all | solution.py:246
  22.6 31.2 %copy-start.1 = (bf16[592,2560]{1,0:T(8,128)(2,1)S(1)}, bf16[592,2560]{1,0:T(8,128)(2,1)}, u32[]{:S(2)}) copy-start(bf16[592,2560]{1,0:T(8,128)(2,1)} %get-tuple-element.32.weight_ref) | copy-start | bytes 9093124
  53.8 6.5 %copy-start = (bf16[16,160,384]{2,1,0:T(8,128)(2,1)}, bf16[16,160,384]{2,1,0:T(8,128)(2,1)S(1)}, u32[]{:S(2)}) copy-start(bf16[16,160,384]{2,1,0:T(8,128)(2,1)S(1)} %all_to_all.30.rows_ref.mine_ref) | copy-start | bytes 5898244
  53.8 4.0 %copy-start.3 = (bf16[592,2560]{1,0:T(8,128)(2,1)S(1)}, bf16[592,2560]{1,0:T(8,128)(2,1)}, u32[]{:S(2)}) copy-start(bf16[592,2560]{1,0:T(8,128)(2,1)} %get-tuple-element.36.weight_ref) | copy-start | bytes 9093124
  53.9 4.0 %copy-start.5 = (s32[2]{0:T(128)S(1)}, s32[2]{0:T(128)}, u32[]{:S(2)}) copy-start(s32[2]{0:T(128)} %pad_add_fusion.place_ref) | copy-start | bytes 28
  53.9 4.0 %collective-permute-start = (bf16[16,160,384]{2,1,0:T(8,128)(2,1)S(1)}, bf16[16,160,384]{2,1,0:T(8,128)(2,1)S(1)}, u32[]{:S(2)}, u32[]{:S(2)}) collective-permute-start(bf16[16,160,384]{2,1,0:T(8,128)(2,1)S(1)} %all_to_all.30.rows_ref.mine_ref), channel_id=1, source_target_pairs={{0,1},{1,0},{2,3},{3,2},{4,5},{5,4},{6,7},{7,6},{8,9},{9,8},{10,11... | collective-permute-start | bytes 5898248 | tf_op jit(solution)/shard_map/ppermute | solution.py:269
  57.8 14.0 %copy-start.2 = (bf16[16,160,384]{2,1,0:T(8,128)(2,1)}, bf16[16,160,384]{2,1,0:T(8,128)(2,1)S(1)}, u32[]{:S(2)}) copy-start(bf16[16,160,384]{2,1,0:T(8,128)(2,1)S(1)} %collective-permute-done.rows_ref.partner_ref) | copy-start | bytes 5898244
  60.4 23.3 %collective-permute-start.1 = (bf16[592,2560]{1,0:T(8,128)(2,1)S(1)}, bf16[592,2560]{1,0:T(8,128)(2,1)S(1)}, u32[]{:S(2)}, u32[]{:S(2)}) collective-permute-start(bf16[592,2560]{1,0:T(8,128)(2,1)S(1)} %copy-done.3), channel_id=1, source_target_pairs={{0,1},{1,0},{2,3},{3,2},{4,5},{5,4},{6,7},{7,6},{8,9},{9,8},{10,11... | collective-permute-start | bytes 9093128 | tf_op jit(solution)/shard_map/ppermute | solution.py:291
  85.3 2.1 %copy-start.4 = (bf16[592,384]{1,0:T(8,128)(2,1)}, bf16[592,384]{1,0:T(8,128)(2,1)S(1)}, u32[]{:S(2)}) copy-start(bf16[592,384]{1,0:T(8,128)(2,1)S(1)} %get-tuple-element.43.dlogits_ref) | copy-start | bytes 1363972
  85.3 2.1 %collective-permute-start.2 = (bf16[592,384]{1,0:T(8,128)(2,1)S(1)}, bf16[592,384]{1,0:T(8,128)(2,1)S(1)}, u32[]{:S(2)}, u32[]{:S(2)}) collective-permute-start(bf16[592,384]{1,0:T(8,128)(2,1)S(1)} %get-tuple-element.43.dlogits_ref), channel_id=1, source_target_pairs={{0,1},{1,0},{2,3},{3,2},{4,5},{5,4},{6,7},{7,6},{8,9},{9,8},{10,11... | collective-permute-start | bytes 1363976 | tf_op jit(solution)/shard_map/ppermute | solution.py:309
  121.5 14.6 %all-to-all-start.5 = ((bf16[8,128,128]{2,1,0:T(8,128)(2,1)}), bf16[8,128,128]{2,1,0:T(8,128)(2,1)S(1)}, u32[]{:S(2)}, u32[]{:S(2)}) async-start(bf16[8,128,128]{2,1,0:T(8,128)(2,1)} %spread.1), calls=%async_computation.5 | async-start | bytes 524288 | tf_op jit(solution)/shard_map/all_to_all | solution.py:329

commit v5 on v4

--- a/solution.py
+++ b/solution.py
@@ -92,8 +92,8 @@
     return meta[1:2] + meta[2:3] + meta[3:4]
 
 
-def column_is_target(place_ref, meta):
-    column = place_ref[1] + lax.broadcasted_iota(jnp.int32, (cols, policy), 0)
+def column_is_target(first_col, meta):
+    column = first_col + lax.broadcasted_iota(jnp.int32, (cols, policy), 0)
     return column == meta_target(meta)
 
 
@@ -124,7 +124,7 @@
     total = jnp.sum(shifted, axis=0, keepdims=True)
     mix = jnp.sum(shifted * logits, axis=0, keepdims=True)
     chosen = jnp.sum(
-        jnp.where(column_is_target(place_ref, meta_ref[...]), logits, 0.0), axis=0, keepdims=True
+        jnp.where(column_is_target(place_ref[1], meta_ref[...]), logits, 0.0), axis=0, keepdims=True
     )
     stats = jnp.concatenate([top, total, mix, chosen], axis=0)
     for other in range(stats_ref.shape[0]):
@@ -148,7 +148,9 @@
         out_ref[other] = stats
 
 
-def dlogits_kernel(place_ref, stats_ref, meta_ref, logits_ref, dlogits_ref, loss_ref):
+def grad_kernel(
+    place_ref, stats_ref, meta_ref, logits_ref, other_ref, weight_ref, weight_got_ref, grad_ref, dlogits_ref, loss_ref
+):
     top, total, mix, chosen = combine(stats_ref[...])
     meta = meta_ref[...]
     adv = meta_advantage(meta)
@@ -158,22 +160,26 @@
         adv * (chosen - log_total) + entropy_coef * (log_total - mean), axis=1, keepdims=True
     )
     loss_ref[...] = -loss / policy
-    logits = logits_ref[...]
     share = 1.0 / (total * policy)
     spread = entropy_coef * share
-    dlogits = jnp.exp(logits - top) * (adv * share + spread * (logits - mean))
-    hit = jnp.where(column_is_target(place_ref, meta), adv / policy, 0.0)
-    dlogits_ref[...] = (dlogits - hit).astype(bf16)
-
-
-def grad_own_kernel(dlogits_ref, weight_ref, out_ref):
-    out = lax.dot_general(weight_ref[...], dlogits_ref[...], tn_dims, preferred_element_type=f32)
-    out_ref[...] = out.reshape(out_ref.shape)
-
-
-def grad_sum_kernel(dlogits_ref, weight_ref, own_ref, out_ref):
-    out = lax.dot_general(weight_ref[...], dlogits_ref[...], tn_dims, preferred_element_type=f32)
-    out_ref[...] = (own_ref[...] + out.reshape(out_ref.shape)).astype(bf16)
+
+    def dlogits_of(logits, first_col):
+        soft = jnp.exp(logits - top) * (adv * share + spread * (logits - mean))
+        hit = jnp.where(column_is_target(first_col, meta), adv / policy, 0.0)
+        return (soft - hit).astype(bf16)
+
+    def part(weight, dlogits):
+        return lax.dot_general(weight, dlogits, tn_dims, preferred_element_type=f32)
+
+    whole = cols // 256 * 256
+    own = dlogits_of(logits_ref[...], place_ref[1])
+    dlogits_ref[...] = own
+    out = part(weight_ref[:whole], own[:whole])
+    other = dlogits_of(other_ref[...], place_ref[2])
+    out += part(weight_got_ref[:whole], other[:whole])
+    weight = jnp.concatenate([weight_ref[whole:], weight_got_ref[whole:]], axis=0)
+    out += part(weight, jnp.concatenate([own[whole:], other[whole:]], axis=0))
+    grad_ref[...] = out.astype(bf16).reshape(grad_ref.shape)
 
 
 def head_kernel(place_ref, dlogits_ref, mine_ref, partner_ref, out_ref, rows_ref, slots_ref, sems):
@@ -228,7 +234,7 @@
     n_plane = lax.axis_size("x") * lax.axis_size("y")
     core = lax.axis_index("c")
     device = lax.axis_index(("z", "x", "y", "c"))
-    place = jnp.stack([core, device * cols]).astype(jnp.int32)
+    place = jnp.stack([core, device * cols, (device + 1 - 2 * core) * cols]).astype(jnp.int32)
     weight = head_weight.T
     depth = weight.shape[1]
     half = depth // 2
@@ -289,6 +295,7 @@
 
     logits, weight_sent = lax.optimization_barrier((logits, weight_sent))
     weight_got = lax.ppermute(weight_sent, "c", swap)
+    logits_got = lax.ppermute(logits, "c", swap)
     stats = lax.all_to_all(stats, ("z", "c"), 0, 0)
     stats = pl.pallas_call(
         combine_kernel,
@@ -297,30 +304,20 @@
         name="combine",
     )(stats)
     stats = lax.all_to_all(stats, ("x", "y"), 0, 0)
-    stats, weight_got = lax.optimization_barrier((stats, weight_got))
-
-    dlogits, loss = pl.pallas_call(
-        dlogits_kernel,
-        in_specs=[smem] + [local] * 3,
-        out_shape=(shape(cols, policy), shape(1, 1, dtype=f32)),
-        compiler_params=small,
-        name="dlogits",
-    )(place, stats, meta, logits)
-    dlogits_got = lax.ppermute(dlogits, "c", swap)
-    grad_own = pl.pallas_call(
-        grad_own_kernel,
-        out_shape=shape(n_plane, width, policy, dtype=f32),
-        compiler_params=small,
-        cost_estimate=cost(cols * depth * policy, 6_000_000),
-        name="grad_own",
-    )(dlogits, weight_own)
-    summed = pl.pallas_call(
-        grad_sum_kernel,
-        out_shape=shape(n_plane, width, policy),
-        compiler_params=small,
-        cost_estimate=cost(cols * depth * policy, 6_000_000),
-        name="grad_sum",
-    )(dlogits_got, weight_got, grad_own)
+    stats, weight_got, logits_got = lax.optimization_barrier((stats, weight_got, logits_got))
+
+    summed, dlogits, loss = pl.pallas_call(
+        grad_kernel,
+        in_specs=[smem] + [local] * 6,
+        out_shape=(
+            shape(n_plane, width, policy),
+            shape(cols, policy),
+            shape(1, 1, dtype=f32),
+        ),
+        compiler_params=small,
+        cost_estimate=cost(2 * cols * depth * policy, 12_000_000),
+        name="grad",
+    )(place, stats, meta, logits, logits_got, weight_own, weight_got)
     parts = lax.all_to_all(summed, ("x", "y"), 0, 0)
     spread = pl.pallas_call(
         spread_kernel, out_shape=shape(n_dp, 128, 128), compiler_params=small, name="spread"

time: 138 us -> 135 us (0.978)
    pallas_call x3 -> x1, Pallas kernels: 5.91 us -> 4.82 us  [body(): pl.pallas_call(grad_kernel, in_specs=[smem] + [local] * 6, out_shape=(sha...]
  transfers between devices with their start and end apart: 5 -> 5, of which waited for: 3 -> 3; matrix products, arithmetic and copies ran while one was open for 0% -> 0% of each run, Pallas kernels for 12% -> 11%
where the time goes in v5:
time: 135 us; the launch traced here: 134 us
  blocking collectives  82.4 us (61%)
  Pallas kernels  27 us (20%)
  starting transfers between devices  12.5 us (9%)
  waiting for transfers between devices  11.1 us (8%)
    all_to_all x1, blocking collectives, body(): mine = lax.all_to_all(rows, ('x', 'y'), 0, 0)  30.3 us
    all_to_all x1, blocking collectives, body(): parts = lax.all_to_all(summed, ('x', 'y'), 0, 0)  29.1 us
    all_to_all x1, blocking collectives, body(): stats = lax.all_to_all(stats, ('x', 'y'), 0, 0)  11.7 us
    all_to_all x1, blocking collectives, body(): stats = lax.all_to_all(stats, ('z', 'c'), 0, 0)  11.2 us
    all_to_all x1, starting transfers between devices, body(): packed = lax.all_to_all(packed, 'z', 0, 0)  8.47 us
    pallas_call x1, Pallas kernels, body(): pl.pallas_call(head_kernel, in_specs=[smem] + [local] * 3, out_specs=pl.B...  7.19 us
    all_to_all x1, waiting for transfers between devices, body(): packed = lax.all_to_all(packed, 'z', 0, 0)  5.66 us
    pallas_call x1, Pallas kernels, body(): pl.pallas_call(prepare_kernel, grid=(2,), in_specs=[smem, pl.BlockSpec((c...  5.6 us
  transfers between devices with their start and end apart: 5, of which 3 were waited for; matrix products, arithmetic and copies ran while one was open for 0% of the time, Pallas kernels for 11%

profile of v5, /device:TPU:2, one launch (start us, length us, event | category | flops | bytes accessed | tf_op | source)
XLA Modules:
  0.0 134.3 jit_solution(6835092303819511401)
XLA Ops:
  0.6 1.7 %pack.1 = bf16[8,128,128]{2,1,0:T(8,128)(2,1)} custom-call(bf16[160,96]{1,0:T(8,128)(2,1)} %bitcast.13, s32[1,96]{1,0:T(1,128)} %bitcast.15, f32[1,96]{1,0:T(1,128)} %bitcast.16, s32[1,96]{1,0:T(1,128)} %bitcast.17), custom_call_target="tpu_custom_call" | custom-call | tf_op jit(solution)/shard_map/pack/pallas_call | solution.py:245
  2.3 8.5 %all-to-all-start = ((bf16[8,128,128]{2,1,0:T(8,128)(2,1)}), bf16[8,128,128]{2,1,0:T(8,128)(2,1)S(1)}, u32[]{:S(2)}, u32[]{:S(2)}) async-start(bf16[8,128,128]{2,1,0:T(8,128)(2,1)} %pack.1), calls=%async_computation | async-start | bytes 524288 | tf_op jit(solution)/shard_map/all_to_all | solution.py:252
  10.8 0.6 pad_add_fusion.place_ref
  11.4 5.6 %prepare.1 = (bf16[592,2560]{1,0:T(8,128)(2,1)}, bf16[592,2560]{1,0:T(8,128)(2,1)}) custom-call(s32[3]{0:T(128)} %pad_add_fusion.place_ref, bf16[592,5120]{1,0:T(8,128)(2,1)} %bitcast.11), custom_call_target="tpu_custom_call" | custom-call | bytes 24000000 | tf_op jit(solution)/shard_map/prepare/pallas_call | solution.py:253
  17.0 5.7 %all-to-all-done.blocks_ref = bf16[8,128,128]{2,1,0:T(8,128)(2,1)S(1)} async-done(((bf16[8,128,128]{2,1,0:T(8,128)(2,1)}), bf16[8,128,128]{2,1,0:T(8,128)(2,1)S(1)}, u32[]{:S(2)}, u32[]{:S(2)}) %all-to-all-start) | async-done | bytes 262176 | tf_op jit(solution)/shard_map/all_to_all | solution.py:252
  22.6 0.0 copy-start.3
  22.6 0.9 compact.1
  23.6 30.3 %all_to_all.30.rows_ref.mine_ref = bf16[16,160,384]{2,1,0:T(8,128)(2,1)S(1)} all-to-all(bf16[16,160,384]{2,1,0:T(8,128)(2,1)S(1)} %get-tuple-element.33), channel_id=1, replica_groups=mesh['z'=8,'x'=4,'y'=4,'c'=2] {'x','y'}, dimensions={0} | all-to-all | bytes 3932160 | tf_op jit(solution)/shard_map/all_to_all | solution.py:274
  53.8 0.0 copy-start
  53.8 0.0 copy-start.2
  53.9 0.0 copy-start.5
  53.9 0.0 collective-permute-start
  53.9 0.0 copy-done.3
  53.9 1.7 %first.1.first_ref = f32[592,384]{1,0:T(8,128)S(1)} custom-call(bf16[592,2560]{1,0:T(8,128)(2,1)S(1)} %copy-done.3, bf16[16,160,384]{2,1,0:T(8,128)(2,1)S(1)} %all_to_all.30.rows_ref.mine_ref), custom_call_target="tpu_custom_call" | custom-call | flops 1163919360 | bytes 6000000 | tf_op jit(solution)/shard_map/first/pallas_call | solution.py:277
  55.6 2.2 %collective-permute-done.rows_ref.partner_ref = bf16[16,160,384]{2,1,0:T(8,128)(2,1)S(1)} collective-permute-done((bf16[16,160,384]{2,1,0:T(8,128)(2,1)S(1)}, bf16[16,160,384]{2,1,0:T(8,128)(2,1)S(1)}, u32[]{:S(2)}, u32[]{:S(2)}) %collective-permute-start) | collective-permute-done | bytes 1966112 | tf_op jit(solution)/shard_map/ppermute | solution.py:275
  57.8 0.0 copy-start.1
  57.8 0.0 copy-done.2
  57.8 0.0 copy-done.5
  57.8 2.6 %second.1 = (f32[592,384]{1,0:T(8,128)S(1)}, f32[16,4,384]{2,1,0:T(4,128)S(1)}) custom-call(s32[3]{0:T(128)S(1)} %copy-done.5, bf16[592,2560]{1,0:T(8,128)(2,1)S(1)} %copy-done.2, bf16[16,160,384]{2,1,0:T(8,128)(2,1)S(1)} %collective-permute-done.rows_ref.partner_ref, f32[592,384]{1,0:T(8,128)S(1)} %first.1.first_ref, f32[16,384]{1,0:T(8,128)S(1)} %get-tuple-element.35.meta_ref), custom_call_target="tpu_custom_call" | custom-call | flops 1163919360 | bytes 6000000 | tf_op jit(solution)/shard_map/second/pallas_call | solution.py:284
  60.4 0.0 copy-done
  60.4 0.2 collective-permute-start.1
  60.6 0.4 collective-permute-start.2
  61.0 11.2 %all_to_all.31.in_ref = f32[16,4,384]{2,1,0:T(4,128)S(1)} all-to-all(f32[16,4,384]{2,1,0:T(4,128)S(1)} %get-tuple-element.36), channel_id=1, replica_groups=mesh['z'=8,'x'=4,'y'=4,'c'=2] {'z','c'}, dimensions={0} | all-to-all | bytes 196608 | tf_op jit(solution)/shard_map/all_to_all | solution.py:299
  72.2 0.0 copy-done.1
  72.2 0.1 combine.1
  72.3 11.7 %all_to_all.32.stats_ref = f32[16,4,384]{2,1,0:T(4,128)S(1)} all-to-all(f32[16,4,384]{2,1,0:T(4,128)S(1)} %combine.1), channel_id=1, replica_groups=mesh['z'=8,'x'=4,'y'=4,'c'=2] {'x','y'}, dimensions={0} | all-to-all | bytes 196608 | tf_op jit(solution)/shard_map/all_to_all | solution.py:306
  84.1 0.0 collective-permute-done.2.other_ref
  84.1 0.0 collective-permute-done.1.weight_got_ref
  84.1 4.8 %grad.1 = (bf16[16,160,384]{2,1,0:T(8,128)(2,1)S(1)}, bf16[592,384]{1,0:T(8,128)(2,1)S(1)}, f32[1,1]{1,0:T(1,128)}) custom-call(s32[3]{0:T(128)S(1)} %copy-done.5, f32[16,4,384]{2,1,0:T(4,128)S(1)} %all_to_all.32.stats_ref, f32[16,384]{1,0:T(8,128)S(1)} %get-tuple-element.35.meta_ref, f32[592,384]{1,0:T(8,128)S(1)} %get-tuple-element.39.logits_ref, ...), custom_call_target="tpu_custom_call" | custom-call | flops 2327838720 | bytes 12000000 | tf_op jit(solution)/shard_map/grad/pallas_call | solution.py:309
  88.9 0.0 copy-start.4
  88.9 29.1 %all_to_all.33.parts_ref = bf16[16,160,384]{2,1,0:T(8,128)(2,1)S(1)} all-to-all(bf16[16,160,384]{2,1,0:T(8,128)(2,1)S(1)} %get-tuple-element.43), channel_id=1, replica_groups=mesh['z'=8,'x'=4,'y'=4,'c'=2] {'x','y'}, dimensions={0} | all-to-all | bytes 3932160 | tf_op jit(solution)/shard_map/all_to_all | solution.py:321
  118.0 1.7 %spread.1 = bf16[8,128,128]{2,1,0:T(8,128)(2,1)} custom-call(bf16[16,160,384]{2,1,0:T(8,128)(2,1)S(1)} %all_to_all.33.parts_ref, bf16[8,384,96]{2,1,0:T(8,128)(2,1)S(1)} %get-tuple-element.44.picks_ref), custom_call_target="tpu_custom_call" | custom-call | tf_op jit(solution)/shard_map/spread/pallas_call | solution.py:322
  119.7 0.0 copy-done.4
  119.7 3.4 %all-to-all-start.5 = ((bf16[8,128,128]{2,1,0:T(8,128)(2,1)}), bf16[8,128,128]{2,1,0:T(8,128)(2,1)S(1)}, u32[]{:S(2)}, u32[]{:S(2)}) async-start(bf16[8,128,128]{2,1,0:T(8,128)(2,1)} %spread.1), calls=%async_computation.5 | async-start | bytes 524288 | tf_op jit(solution)/shard_map/all_to_all | solution.py:326
  123.1 7.2 %head.1 = bf16[592,5120]{1,0:T(8,128)(2,1)} custom-call(s32[3]{0:T(128)} %pad_add_fusion.place_ref, bf16[592,384]{1,0:T(8,128)(2,1)} %copy-done.4, bf16[16,160,384]{2,1,0:T(8,128)(2,1)} %copy-done, bf16[16,160,384]{2,1,0:T(8,128)(2,1)} %copy-done.1), custom_call_target="tpu_custom_call" | custom-call | flops 2327838720 | bytes 10000000 | tf_op jit(solution)/shard_map/head/pallas_call | solution.py:327
  130.3 3.2 %all-to-all-done.5.parts_ref = bf16[8,128,128]{2,1,0:T(8,128)(2,1)S(1)} async-done(((bf16[8,128,128]{2,1,0:T(8,128)(2,1)}), bf16[8,128,128]{2,1,0:T(8,128)(2,1)S(1)}, u32[]{:S(2)}, u32[]{:S(2)}) %all-to-all-start.5) | async-done | bytes 262176 | tf_op jit(solution)/shard_map/all_to_all | solution.py:326
  133.5 0.7 total.1
Async XLA Ops:
  2.3 20.3 %all-to-all-start = ((bf16[8,128,128]{2,1,0:T(8,128)(2,1)}), bf16[8,128,128]{2,1,0:T(8,128)(2,1)S(1)}, u32[]{:S(2)}, u32[]{:S(2)}) async-start(bf16[8,128,128]{2,1,0:T(8,128)(2,1)} %pack.1), calls=%async_computation | async-start | bytes 524288 | tf_op jit(solution)/shard_map/all_to_all | solution.py:252
  22.6 31.2 %copy-start.3 = (bf16[592,2560]{1,0:T(8,128)(2,1)S(1)}, bf16[592,2560]{1,0:T(8,128)(2,1)}, u32[]{:S(2)}) copy-start(bf16[592,2560]{1,0:T(8,128)(2,1)} %get-tuple-element.34.weight_ref) | copy-start | bytes 9093124
  53.8 6.5 %copy-start = (bf16[16,160,384]{2,1,0:T(8,128)(2,1)}, bf16[16,160,384]{2,1,0:T(8,128)(2,1)S(1)}, u32[]{:S(2)}) copy-start(bf16[16,160,384]{2,1,0:T(8,128)(2,1)S(1)} %all_to_all.30.rows_ref.mine_ref) | copy-start | bytes 5898244
  53.8 4.0 %copy-start.2 = (bf16[592,2560]{1,0:T(8,128)(2,1)S(1)}, bf16[592,2560]{1,0:T(8,128)(2,1)}, u32[]{:S(2)}) copy-start(bf16[592,2560]{1,0:T(8,128)(2,1)} %get-tuple-element.38.weight_ref) | copy-start | bytes 9093124
  53.9 4.0 %copy-start.5 = (s32[3]{0:T(128)S(1)}, s32[3]{0:T(128)}, u32[]{:S(2)}) copy-start(s32[3]{0:T(128)} %pad_add_fusion.place_ref) | copy-start | bytes 40
  53.9 4.0 %collective-permute-start = (bf16[16,160,384]{2,1,0:T(8,128)(2,1)S(1)}, bf16[16,160,384]{2,1,0:T(8,128)(2,1)S(1)}, u32[]{:S(2)}, u32[]{:S(2)}) collective-permute-start(bf16[16,160,384]{2,1,0:T(8,128)(2,1)S(1)} %all_to_all.30.rows_ref.mine_ref), channel_id=1, source_target_pairs={{0,1},{1,0},{2,3},{3,2},{4,5},{5,4},{6,7},{7,6},{8,9},{9,8},{10,11... | collective-permute-start | bytes 5898248 | tf_op jit(solution)/shard_map/ppermute | solution.py:275
  57.8 14.4 %copy-start.1 = (bf16[16,160,384]{2,1,0:T(8,128)(2,1)}, bf16[16,160,384]{2,1,0:T(8,128)(2,1)S(1)}, u32[]{:S(2)}) copy-start(bf16[16,160,384]{2,1,0:T(8,128)(2,1)S(1)} %collective-permute-done.rows_ref.partner_ref) | copy-start | bytes 5898244
  60.4 23.7 %collective-permute-start.1 = (bf16[592,2560]{1,0:T(8,128)(2,1)S(1)}, bf16[592,2560]{1,0:T(8,128)(2,1)S(1)}, u32[]{:S(2)}, u32[]{:S(2)}) collective-permute-start(bf16[592,2560]{1,0:T(8,128)(2,1)S(1)} %copy-done.2), channel_id=1, source_target_pairs={{0,1},{1,0},{2,3},{3,2},{4,5},{5,4},{6,7},{7,6},{8,9},{9,8},{10,11... | collective-permute-start | bytes 9093128 | tf_op jit(solution)/shard_map/ppermute | solution.py:297
  60.6 23.4 %collective-permute-start.2 = (f32[592,384]{1,0:T(8,128)S(1)}, f32[592,384]{1,0:T(8,128)S(1)}, u32[]{:S(2)}, u32[]{:S(2)}) collective-permute-start(f32[592,384]{1,0:T(8,128)S(1)} %get-tuple-element.39.logits_ref), channel_id=1, source_target_pairs={{0,1},{1,0},{2,3},{3,2},{4,5},{5,4},{6,7},{7,6},{8,9},{9,8},{10,11... | collective-permute-start | bytes 2727944 | tf_op jit(solution)/shard_map/ppermute | solution.py:298
  88.9 30.8 %copy-start.4 = (bf16[592,384]{1,0:T(8,128)(2,1)}, bf16[592,384]{1,0:T(8,128)(2,1)S(1)}, u32[]{:S(2)}) copy-start(bf16[592,384]{1,0:T(8,128)(2,1)S(1)} %get-tuple-element.47.dlogits_ref) | copy-start | bytes 1363972
  119.7 13.8 %all-to-all-start.5 = ((bf16[8,128,128]{2,1,0:T(8,128)(2,1)}), bf16[8,128,128]{2,1,0:T(8,128)(2,1)S(1)}, u32[]{:S(2)}, u32[]{:S(2)}) async-start(bf16[8,128,128]{2,1,0:T(8,128)(2,1)} %spread.1), calls=%async_computation.5 | async-start | bytes 524288 | tf_op jit(solution)/shard_map/all_to_all | solution.py:326

commit v6 on v5

--- a/solution.py
+++ b/solution.py
@@ -10,6 +10,7 @@
 policy = 384
 width = 160
 cols = 592
+side = 4
 meta_rows = 16
 bf16 = jnp.bfloat16
 f32 = jnp.float32
@@ -84,6 +85,14 @@
         rows_ref[other] = rows
 
 
+def place_of(core, block):
+    return jnp.where(core == 0, block, block % side * side + block // side)
+
+
+def rows_of(core, rows_ref):
+    return jnp.concatenate([rows_ref[place_of(core, k)] for k in range(rows_ref.shape[0])], axis=0)
+
+
 def meta_target(meta):
     return (meta[4:5] + 64.0 * meta[5:6] + 4096.0 * meta[6:7]).astype(jnp.int32)
 
@@ -108,15 +117,15 @@
                 second_ref[:, at] = weight_ref[:, (2 * block + 1) * width : (2 * block + 2) * width]
 
 
-def first_half_kernel(weight_ref, rows_ref, out_ref):
-    rows = rows_ref[...].reshape(-1, policy)
+def first_half_kernel(place_ref, weight_ref, rows_ref, out_ref):
+    rows = rows_of(place_ref[0], rows_ref)
     out_ref[...] = jnp.dot(weight_ref[...], rows, preferred_element_type=f32)
 
 
 def second_half_kernel(
     place_ref, weight_ref, rows_ref, first_ref, meta_ref, logits_ref, stats_ref
 ):
-    rows = rows_ref[...].reshape(-1, policy)
+    rows = rows_of(1 - place_ref[0], rows_ref)
     logits = first_ref[...] + jnp.dot(weight_ref[...], rows, preferred_element_type=f32)
     logits_ref[...] = logits
     top = jnp.max(logits, axis=0, keepdims=True)
@@ -179,7 +188,9 @@
     out += part(weight_got_ref[:whole], other[:whole])
     weight = jnp.concatenate([weight_ref[whole:], weight_got_ref[whole:]], axis=0)
     out += part(weight, jnp.concatenate([own[whole:], other[whole:]], axis=0))
-    grad_ref[...] = out.astype(bf16).reshape(grad_ref.shape)
+    for block in range(grad_ref.shape[0]):
+        rows = out[block * width : (block + 1) * width]
+        grad_ref[place_of(place_ref[0], block)] = rows.astype(bf16)
 
 
 def head_kernel(place_ref, dlogits_ref, mine_ref, partner_ref, out_ref, rows_ref, slots_ref, sems):
@@ -189,7 +200,7 @@
         def _():
             for block in range(first.shape[0]):
                 rows_ref[block, 0] = first[block]
-                rows_ref[block, 1] = second[block]
+                rows_ref[block, 1] = second[block % side * side + block // side]
 
     count = slots_ref.shape[0]
     step = slots_ref.shape[2]
@@ -210,6 +221,15 @@
         send(part).wait()
 
 
+def copies_kernel(rows_ref, out_ref):
+    for other in range(out_ref.shape[0]):
+        out_ref[other] = rows_ref[...]
+
+
+def line_sum_kernel(parts_ref, out_ref):
+    out_ref[...] = jnp.sum(parts_ref[...].astype(f32), axis=0).astype(bf16)
+
+
 def spread_kernel(parts_ref, picks_ref, out_ref):
     total = jnp.sum(parts_ref[...].astype(f32), axis=0).astype(bf16)
     for z in range(out_ref.shape[0]):
@@ -223,6 +243,17 @@
 
 def shape(*dims, dtype=bf16):
     return jax.ShapeDtypeStruct(dims, dtype)
+
+
+def along_lines(blocks, first):
+    def device(x, y, c):
+        return (x * side + y) * 2 + c
+
+    near, far = (1, 0) if first else (0, 1)
+    y_core, x_core = 1 - near, 1 - far
+    groups = [[device(x, y, y_core) for y in range(side)] for x in range(side)]
+    groups += [[device(x, y, x_core) for x in range(side)] for y in range(side)]
+    return lax.all_to_all(blocks, ("x", "y", "c"), 0, 0, axis_index_groups=groups)
 
 
 def cost(flops, nbytes):
@@ -264,23 +295,31 @@
     rows, meta, picks = pl.pallas_call(
         compact_kernel,
         out_shape=(
-            shape(n_plane, width, policy),
+            shape(side, width, policy),
             shape(meta_rows, policy, dtype=f32),
             shape(n_dp, policy, tok),
         ),
         compiler_params=small,
         name="compact",
     )(packed)
-    mine = lax.all_to_all(rows, ("x", "y"), 0, 0)
+    line = along_lines(rows, True)
+    lines = pl.pallas_call(
+        copies_kernel,
+        out_shape=shape(side, side, width, policy),
+        compiler_params=small,
+        name="copies",
+    )(line)
+    mine = along_lines(lines, False).reshape(n_plane, width, policy)
     partner = lax.ppermute(mine, "c", swap)
 
     first = pl.pallas_call(
         first_half_kernel,
+        in_specs=[smem] + [local] * 2,
         out_shape=shape(cols, policy, dtype=f32),
         compiler_params=small,
         cost_estimate=cost(cols * depth * policy, 6_000_000),
         name="first",
-    )(weight_own, mine)
+    )(place, weight_own, mine)
     logits, stats = pl.pallas_call(
         second_half_kernel,
         in_specs=[smem] + [local] * 4,
@@ -318,7 +357,14 @@
         cost_estimate=cost(2 * cols * depth * policy, 12_000_000),
         name="grad",
     )(place, stats, meta, logits, logits_got, weight_own, weight_got)
-    parts = lax.all_to_all(summed, ("x", "y"), 0, 0)
+    parts = along_lines(summed.reshape(side, side, width, policy), False)
+    line = pl.pallas_call(
+        line_sum_kernel,
+        out_shape=shape(side, width, policy),
+        compiler_params=small,
+        name="line_sum",
+    )(parts)
+    parts = along_lines(line, True)
     spread = pl.pallas_call(
         spread_kernel, out_shape=shape(n_dp, 128, 128), compiler_params=small, name="spread"
     )(parts, picks)

time: 135 us -> 134 us (level)
    pallas_call x2 -> x4, Pallas kernels: 2.64 us -> 3.47 us  [the longest x1 2.27 us: body(): pl.pallas_call(first_half_kernel, in_specs=[smem] + [local] * 2, out_shap...]
    all_to_all x2 -> x4, blocking collectives: 59.4 us -> 60.2 us  [along_lines(): lax.all_to_all(blocks, ('x', 'y', 'c'), 0, 0, axis_index_groups=groups)]
where the time goes in v6:
time: 134 us
  blocking collectives  81.7 us (61%)
  Pallas kernels  27.6 us (21%)
  starting transfers between devices  12.5 us (9%)
  waiting for transfers between devices  10.5 us (8%)
    all_to_all x4, blocking collectives, along_lines(): lax.all_to_all(blocks, ('x', 'y', 'c'), 0, 0, axis_index_groups=groups)  60.2 us
    all_to_all x1, blocking collectives, body(): stats = lax.all_to_all(stats, ('z', 'c'), 0, 0)  10.8 us
    all_to_all x1, blocking collectives, body(): stats = lax.all_to_all(stats, ('x', 'y'), 0, 0)  10.6 us
    all_to_all x1, starting transfers between devices, body(): packed = lax.all_to_all(packed, 'z', 0, 0)  8.47 us
    pallas_call x1, Pallas kernels, body(): pl.pallas_call(head_kernel, in_specs=[smem] + [local] * 3, out_specs=pl.B...  7.19 us
    all_to_all x1, waiting for transfers between devices, body(): packed = lax.all_to_all(packed, 'z', 0, 0)  5.66 us
    pallas_call x1, Pallas kernels, body(): pl.pallas_call(prepare_kernel, grid=(2,), in_specs=[smem, pl.BlockSpec((c...  5.6 us
    pallas_call x1, Pallas kernels, body(): pl.pallas_call(grad_kernel, in_specs=[smem] + [local] * 6, out_shape=(sha...  4.83 us
  transfers between devices with their start and end apart: 5, of which 3 were waited for; matrix products, arithmetic and copies ran while one was open for 0% of the time, Pallas kernels for 11%

profile of v6, /device:TPU:2, one launch (start us, length us, event | category | flops | bytes accessed | tf_op | source)
XLA Modules:
  0.0 133.7 jit_solution(8753111483952690849)
XLA Ops:
  0.6 1.7 %pack.1 = bf16[8,128,128]{2,1,0:T(8,128)(2,1)} custom-call(bf16[160,96]{1,0:T(8,128)(2,1)} %bitcast.19, s32[1,96]{1,0:T(1,128)} %bitcast.21, f32[1,96]{1,0:T(1,128)} %bitcast.22, s32[1,96]{1,0:T(1,128)} %bitcast.23), custom_call_target="tpu_custom_call" | custom-call | tf_op jit(solution)/shard_map/pack/pallas_call | solution.py:276
  2.3 8.5 %all-to-all-start = ((bf16[8,128,128]{2,1,0:T(8,128)(2,1)}), bf16[8,128,128]{2,1,0:T(8,128)(2,1)S(1)}, u32[]{:S(2)}, u32[]{:S(2)}) async-start(bf16[8,128,128]{2,1,0:T(8,128)(2,1)} %pack.1), calls=%async_computation | async-start | bytes 524288 | tf_op jit(solution)/shard_map/all_to_all | solution.py:283
  10.8 0.6 pad_add_fusion.place_ref
  11.4 5.6 %prepare.1 = (bf16[592,2560]{1,0:T(8,128)(2,1)}, bf16[592,2560]{1,0:T(8,128)(2,1)}) custom-call(s32[3]{0:T(128)} %pad_add_fusion.place_ref, bf16[592,5120]{1,0:T(8,128)(2,1)} %bitcast.17), custom_call_target="tpu_custom_call" | custom-call | bytes 24000000 | tf_op jit(solution)/shard_map/prepare/pallas_call | solution.py:284
  17.0 5.7 %all-to-all-done.blocks_ref = bf16[8,128,128]{2,1,0:T(8,128)(2,1)S(1)} async-done(((bf16[8,128,128]{2,1,0:T(8,128)(2,1)}), bf16[8,128,128]{2,1,0:T(8,128)(2,1)S(1)}, u32[]{:S(2)}, u32[]{:S(2)}) %all-to-all-start) | async-done | bytes 262176 | tf_op jit(solution)/shard_map/all_to_all | solution.py:283
  22.6 0.8 compact.1
  23.4 12.2 %all_to_all.40.rows_ref = bf16[4,160,384]{2,1,0:T(8,128)(2,1)S(1)} all-to-all(bf16[4,160,384]{2,1,0:T(8,128)(2,1)S(1)} %get-tuple-element.33), channel_id=1, replica_groups={{0,2,4,6},{8,10,12,14},{16,18,20,22},{24,26,28,30},{1,9,17,25},{3,11,19..., dimensions={0} | all-to-all | bytes 983040 | tf_op jit(solution)/shard_map/all_to_all | solution.py:256
  35.6 0.0 copy-start.3
  35.6 0.0 copy-start.5
  35.6 0.2 copies.1
  35.8 19.1 %all_to_all.41 = bf16[4,4,160,384]{3,2,1,0:T(8,128)(2,1)S(1)} all-to-all(bf16[4,4,160,384]{3,2,1,0:T(8,128)(2,1)S(1)} %copies.1), channel_id=1, replica_groups={{1,3,5,7},{9,11,13,15},{17,19,21,23},{25,27,29,31},{0,8,16,24},{2,10,18..., dimensions={0} | all-to-all | bytes 3932160 | tf_op jit(solution)/shard_map/all_to_all | solution.py:256
  54.9 0.0 copy-start
  54.9 0.0 copy-start.2
  54.9 0.0 collective-permute-start
  54.9 0.0 copy-done.3
  54.9 0.0 copy-done.5
  54.9 2.3 %first.1.first_ref = f32[592,384]{1,0:T(8,128)S(1)} custom-call(s32[3]{0:T(128)S(1)} %copy-done.5, bf16[592,2560]{1,0:T(8,128)(2,1)S(1)} %copy-done.3, bf16[16,160,384]{2,1,0:T(8,128)(2,1)S(1)} %bitcast.14), custom_call_target="tpu_custom_call" | custom-call | flops 1163919360 | bytes 6000000 | tf_op jit(solution)/shard_map/first/pallas_call | solution.py:315
  57.2 1.7 %collective-permute-done.rows_ref.partner_ref = bf16[16,160,384]{2,1,0:T(8,128)(2,1)S(1)} collective-permute-done((bf16[16,160,384]{2,1,0:T(8,128)(2,1)S(1)}, bf16[16,160,384]{2,1,0:T(8,128)(2,1)S(1)}, u32[]{:S(2)}, u32[]{:S(2)}) %collective-permute-start) | collective-permute-done | bytes 1966112 | tf_op jit(solution)/shard_map/ppermute | solution.py:313
  58.9 0.0 copy-start.1
  58.9 0.0 copy-done.2
  58.9 2.5 %second.1 = (f32[592,384]{1,0:T(8,128)S(1)}, f32[16,4,384]{2,1,0:T(4,128)S(1)}) custom-call(s32[3]{0:T(128)S(1)} %copy-done.5, bf16[592,2560]{1,0:T(8,128)(2,1)S(1)} %copy-done.2, bf16[16,160,384]{2,1,0:T(8,128)(2,1)S(1)} %collective-permute-done.rows_ref.partner_ref, f32[592,384]{1,0:T(8,128)S(1)} %first.1.first_ref, f32[16,384]{1,0:T(8,128)S(1)} %get-tuple-element.35.meta_ref), custom_call_target="tpu_custom_call" | custom-call | flops 1163919360 | bytes 6000000 | tf_op jit(solution)/shard_map/second/pallas_call | solution.py:323
  61.4 0.0 copy-done
  61.4 0.2 collective-permute-start.1
  61.6 0.4 collective-permute-start.2
  62.0 10.8 %all_to_all.42.in_ref = f32[16,4,384]{2,1,0:T(4,128)S(1)} all-to-all(f32[16,4,384]{2,1,0:T(4,128)S(1)} %get-tuple-element.36), channel_id=1, replica_groups=mesh['z'=8,'x'=4,'y'=4,'c'=2] {'z','c'}, dimensions={0} | all-to-all | bytes 196608 | tf_op jit(solution)/shard_map/all_to_all | solution.py:338
  72.9 0.0 copy-done.1
  72.9 0.1 combine.1
  73.0 10.6 %all_to_all.43.stats_ref = f32[16,4,384]{2,1,0:T(4,128)S(1)} all-to-all(f32[16,4,384]{2,1,0:T(4,128)S(1)} %combine.1), channel_id=1, replica_groups=mesh['z'=8,'x'=4,'y'=4,'c'=2] {'x','y'}, dimensions={0} | all-to-all | bytes 196608 | tf_op jit(solution)/shard_map/all_to_all | solution.py:345
  83.6 0.0 collective-permute-done.2.other_ref
  83.6 0.0 collective-permute-done.1.weight_got_ref
  83.6 4.8 %grad.1 = (bf16[16,160,384]{2,1,0:T(8,128)(2,1)S(1)}, bf16[592,384]{1,0:T(8,128)(2,1)S(1)}, f32[1,1]{1,0:T(1,128)}) custom-call(s32[3]{0:T(128)S(1)} %copy-done.5, f32[16,4,384]{2,1,0:T(4,128)S(1)} %all_to_all.43.stats_ref, f32[16,384]{1,0:T(8,128)S(1)} %get-tuple-element.35.meta_ref, f32[592,384]{1,0:T(8,128)S(1)} %get-tuple-element.39.logits_ref, ...), custom_call_target="tpu_custom_call" | custom-call | flops 2327838720 | bytes 12000000 | tf_op jit(solution)/shard_map/grad/pallas_call | solution.py:348
  88.5 0.0 copy-start.4
  88.5 18.5 %all_to_all.44.parts_ref = bf16[4,4,160,384]{3,2,1,0:T(8,128)(2,1)S(1)} all-to-all(bf16[4,4,160,384]{3,2,1,0:T(8,128)(2,1)S(1)} %bitcast.16), channel_id=1, replica_groups={{1,3,5,7},{9,11,13,15},{17,19,21,23},{25,27,29,31},{0,8,16,24},{2,10,18..., dimensions={0} | all-to-all | bytes 3932160 | tf_op jit(solution)/shard_map/all_to_all | solution.py:256
  107.0 0.2 line_sum.1
  107.2 0.0 copy-done.4
  107.2 10.4 %all_to_all.45.parts_ref = bf16[4,160,384]{2,1,0:T(8,128)(2,1)S(1)} all-to-all(bf16[4,160,384]{2,1,0:T(8,128)(2,1)S(1)} %line_sum.1), channel_id=1, replica_groups={{0,2,4,6},{8,10,12,14},{16,18,20,22},{24,26,28,30},{1,9,17,25},{3,11,19..., dimensions={0} | all-to-all | bytes 983040 | tf_op jit(solution)/shard_map/all_to_all | solution.py:256
  117.7 1.5 %spread.1 = bf16[8,128,128]{2,1,0:T(8,128)(2,1)} custom-call(bf16[4,160,384]{2,1,0:T(8,128)(2,1)S(1)} %all_to_all.45.parts_ref, bf16[8,384,96]{2,1,0:T(8,128)(2,1)S(1)} %get-tuple-element.44.picks_ref), custom_call_target="tpu_custom_call" | custom-call | tf_op jit(solution)/shard_map/spread/pallas_call | solution.py:368
  119.2 3.4 %all-to-all-start.7 = ((bf16[8,128,128]{2,1,0:T(8,128)(2,1)}), bf16[8,128,128]{2,1,0:T(8,128)(2,1)S(1)}, u32[]{:S(2)}, u32[]{:S(2)}) async-start(bf16[8,128,128]{2,1,0:T(8,128)(2,1)} %spread.1), calls=%async_computation.7 | async-start | bytes 524288 | tf_op jit(solution)/shard_map/all_to_all | solution.py:372
  122.6 7.2 %head.1 = bf16[592,5120]{1,0:T(8,128)(2,1)} custom-call(s32[3]{0:T(128)} %pad_add_fusion.place_ref, bf16[592,384]{1,0:T(8,128)(2,1)} %copy-done.4, bf16[16,160,384]{2,1,0:T(8,128)(2,1)} %bitcast.15, bf16[16,160,384]{2,1,0:T(8,128)(2,1)} %copy-done.1), custom_call_target="tpu_custom_call" | custom-call | flops 2327838720 | bytes 10000000 | tf_op jit(solution)/shard_map/head/pallas_call | solution.py:373
  129.8 3.2 %all-to-all-done.7.parts_ref = bf16[8,128,128]{2,1,0:T(8,128)(2,1)S(1)} async-done(((bf16[8,128,128]{2,1,0:T(8,128)(2,1)}), bf16[8,128,128]{2,1,0:T(8,128)(2,1)S(1)}, u32[]{:S(2)}, u32[]{:S(2)}) %all-to-all-start.7) | async-done | bytes 262176 | tf_op jit(solution)/shard_map/all_to_all | solution.py:372
  133.0 0.7 total.1
Async XLA Ops:
  2.3 20.3 %all-to-all-start = ((bf16[8,128,128]{2,1,0:T(8,128)(2,1)}), bf16[8,128,128]{2,1,0:T(8,128)(2,1)S(1)}, u32[]{:S(2)}, u32[]{:S(2)}) async-start(bf16[8,128,128]{2,1,0:T(8,128)(2,1)} %pack.1), calls=%async_computation | async-start | bytes 524288 | tf_op jit(solution)/shard_map/all_to_all | solution.py:283
  35.6 19.3 %copy-start.3 = (bf16[592,2560]{1,0:T(8,128)(2,1)S(1)}, bf16[592,2560]{1,0:T(8,128)(2,1)}, u32[]{:S(2)}) copy-start(bf16[592,2560]{1,0:T(8,128)(2,1)} %get-tuple-element.34.weight_ref) | copy-start | bytes 9093124
  35.6 19.3 %copy-start.5 = (s32[3]{0:T(128)S(1)}, s32[3]{0:T(128)}, u32[]{:S(2)}) copy-start(s32[3]{0:T(128)} %pad_add_fusion.place_ref) | copy-start | bytes 40
  54.9 6.5 %copy-start = (bf16[4,4,160,384]{3,2,1,0:T(8,128)(2,1)}, bf16[4,4,160,384]{3,2,1,0:T(8,128)(2,1)S(1)}, u32[]{:S(2)}) copy-start(bf16[4,4,160,384]{3,2,1,0:T(8,128)(2,1)S(1)} %all_to_all.41) | copy-start | bytes 5898244
  54.9 4.0 %copy-start.2 = (bf16[592,2560]{1,0:T(8,128)(2,1)S(1)}, bf16[592,2560]{1,0:T(8,128)(2,1)}, u32[]{:S(2)}) copy-start(bf16[592,2560]{1,0:T(8,128)(2,1)} %get-tuple-element.38.weight_ref) | copy-start | bytes 9093124
  54.9 4.0 %collective-permute-start = (bf16[16,160,384]{2,1,0:T(8,128)(2,1)S(1)}, bf16[16,160,384]{2,1,0:T(8,128)(2,1)S(1)}, u32[]{:S(2)}, u32[]{:S(2)}) collective-permute-start(bf16[16,160,384]{2,1,0:T(8,128)(2,1)S(1)} %bitcast.13), channel_id=1, source_target_pairs={{0,1},{1,0},{2,3},{3,2},{4,5},{5,4},{6,7},{7,6},{8,9},{9,8},{10,11... | collective-permute-start | bytes 5898248 | tf_op jit(solution)/shard_map/ppermute | solution.py:313
  58.9 14.0 %copy-start.1 = (bf16[16,160,384]{2,1,0:T(8,128)(2,1)}, bf16[16,160,384]{2,1,0:T(8,128)(2,1)S(1)}, u32[]{:S(2)}) copy-start(bf16[16,160,384]{2,1,0:T(8,128)(2,1)S(1)} %collective-permute-done.rows_ref.partner_ref) | copy-start | bytes 5898244
  61.4 22.2 %collective-permute-start.1 = (bf16[592,2560]{1,0:T(8,128)(2,1)S(1)}, bf16[592,2560]{1,0:T(8,128)(2,1)S(1)}, u32[]{:S(2)}, u32[]{:S(2)}) collective-permute-start(bf16[592,2560]{1,0:T(8,128)(2,1)S(1)} %copy-done.2), channel_id=1, source_target_pairs={{0,1},{1,0},{2,3},{3,2},{4,5},{5,4},{6,7},{7,6},{8,9},{9,8},{10,11... | collective-permute-start | bytes 9093128 | tf_op jit(solution)/shard_map/ppermute | solution.py:336
  61.6 22.0 %collective-permute-start.2 = (f32[592,384]{1,0:T(8,128)S(1)}, f32[592,384]{1,0:T(8,128)S(1)}, u32[]{:S(2)}, u32[]{:S(2)}) collective-permute-start(f32[592,384]{1,0:T(8,128)S(1)} %get-tuple-element.39.logits_ref), channel_id=1, source_target_pairs={{0,1},{1,0},{2,3},{3,2},{4,5},{5,4},{6,7},{7,6},{8,9},{9,8},{10,11... | collective-permute-start | bytes 2727944 | tf_op jit(solution)/shard_map/ppermute | solution.py:337
  88.5 18.8 %copy-start.4 = (bf16[592,384]{1,0:T(8,128)(2,1)}, bf16[592,384]{1,0:T(8,128)(2,1)S(1)}, u32[]{:S(2)}) copy-start(bf16[592,384]{1,0:T(8,128)(2,1)S(1)} %get-tuple-element.47.dlogits_ref) | copy-start | bytes 1363972
  119.2 13.8 %all-to-all-start.7 = ((bf16[8,128,128]{2,1,0:T(8,128)(2,1)}), bf16[8,128,128]{2,1,0:T(8,128)(2,1)S(1)}, u32[]{:S(2)}, u32[]{:S(2)}) async-start(bf16[8,128,128]{2,1,0:T(8,128)(2,1)} %spread.1), calls=%async_computation.7 | async-start | bytes 524288 | tf_op jit(solution)/shard_map/all_to_all | solution.py:372

commit v7 on v6

--- a/solution.py
+++ b/solution.py
@@ -85,12 +85,17 @@
         rows_ref[other] = rows
 
 
+def core_index():
+    return lax.axis_index("c")
+
+
+def first_column(core):
+    line = lax.axis_index("z") * side + lax.axis_index("x")
+    return ((line * side + lax.axis_index("y")) * 2 + core) * cols
+
+
 def place_of(core, block):
     return jnp.where(core == 0, block, block % side * side + block // side)
-
-
-def rows_of(core, rows_ref):
-    return jnp.concatenate([rows_ref[place_of(core, k)] for k in range(rows_ref.shape[0])], axis=0)
 
 
 def meta_target(meta):
@@ -106,10 +111,10 @@
     return column == meta_target(meta)
 
 
-def prepare_kernel(place_ref, weight_ref, kept_ref, sent_ref):
+def prepare_kernel(weight_ref, kept_ref, sent_ref):
     for core, (first_ref, second_ref) in enumerate([(kept_ref, sent_ref), (sent_ref, kept_ref)]):
 
-        @pl.when(place_ref[0] == core)
+        @pl.when(core_index() == core)
         def _():
             for block in range(kept_ref.shape[1] // width):
                 at = slice(block * width, (block + 1) * width)
@@ -117,23 +122,28 @@
                 second_ref[:, at] = weight_ref[:, (2 * block + 1) * width : (2 * block + 2) * width]
 
 
-def first_half_kernel(place_ref, weight_ref, rows_ref, out_ref):
-    rows = rows_of(place_ref[0], rows_ref)
-    out_ref[...] = jnp.dot(weight_ref[...], rows, preferred_element_type=f32)
-
-
-def second_half_kernel(
-    place_ref, weight_ref, rows_ref, first_ref, meta_ref, logits_ref, stats_ref
-):
-    rows = rows_of(1 - place_ref[0], rows_ref)
-    logits = first_ref[...] + jnp.dot(weight_ref[...], rows, preferred_element_type=f32)
+def partial_kernel(weight_ref, rows_ref, out_ref):
+    @pl.when(core_index() == 0)
+    def _():
+        rows = rows_ref[...].reshape(-1, policy)
+        out_ref[...] = jnp.dot(weight_ref[...], rows, preferred_element_type=f32)
+
+    @pl.when(core_index() == 1)
+    def _():
+        blocks = [rows_ref[k % side * side + k // side] for k in range(rows_ref.shape[0])]
+        rows = jnp.concatenate(blocks, axis=0)
+        out_ref[...] = jnp.dot(weight_ref[...], rows, preferred_element_type=f32)
+
+
+def stats_kernel(own_ref, got_ref, meta_ref, logits_ref, stats_ref):
+    logits = own_ref[...] + got_ref[...]
     logits_ref[...] = logits
     top = jnp.max(logits, axis=0, keepdims=True)
     shifted = jnp.exp(logits - top)
     total = jnp.sum(shifted, axis=0, keepdims=True)
     mix = jnp.sum(shifted * logits, axis=0, keepdims=True)
     chosen = jnp.sum(
-        jnp.where(column_is_target(place_ref[1], meta_ref[...]), logits, 0.0), axis=0, keepdims=True
+        jnp.where(column_is_target(first_column(core_index()), meta_ref[...]), logits, 0.0), axis=0, keepdims=True
     )
     stats = jnp.concatenate([top, total, mix, chosen], axis=0)
     for other in range(stats_ref.shape[0]):
@@ -157,8 +167,7 @@
         out_ref[other] = stats
 
 
-def grad_kernel(
-    place_ref, stats_ref, meta_ref, logits_ref, other_ref, weight_ref, weight_got_ref, grad_ref, dlogits_ref, loss_ref
+def grad_kernel(stats_ref, meta_ref, logits_ref, other_ref, weight_ref, weight_got_ref, grad_ref, dlogits_ref, loss_ref
 ):
     top, total, mix, chosen = combine(stats_ref[...])
     meta = meta_ref[...]
@@ -181,22 +190,22 @@
         return lax.dot_general(weight, dlogits, tn_dims, preferred_element_type=f32)
 
     whole = cols // 256 * 256
-    own = dlogits_of(logits_ref[...], place_ref[1])
+    own = dlogits_of(logits_ref[...], first_column(core_index()))
     dlogits_ref[...] = own
     out = part(weight_ref[:whole], own[:whole])
-    other = dlogits_of(other_ref[...], place_ref[2])
+    other = dlogits_of(other_ref[...], first_column(1 - core_index()))
     out += part(weight_got_ref[:whole], other[:whole])
     weight = jnp.concatenate([weight_ref[whole:], weight_got_ref[whole:]], axis=0)
     out += part(weight, jnp.concatenate([own[whole:], other[whole:]], axis=0))
     for block in range(grad_ref.shape[0]):
         rows = out[block * width : (block + 1) * width]
-        grad_ref[place_of(place_ref[0], block)] = rows.astype(bf16)
-
-
-def head_kernel(place_ref, dlogits_ref, mine_ref, partner_ref, out_ref, rows_ref, slots_ref, sems):
+        grad_ref[place_of(core_index(), block)] = rows.astype(bf16)
+
+
+def head_kernel(dlogits_ref, mine_ref, partner_ref, out_ref, rows_ref, slots_ref, sems):
     for core, (first, second) in enumerate([(mine_ref, partner_ref), (partner_ref, mine_ref)]):
 
-        @pl.when(place_ref[0] == core)
+        @pl.when(core_index() == core)
         def _():
             for block in range(first.shape[0]):
                 rows_ref[block, 0] = first[block]
@@ -263,14 +272,10 @@
 def body(hidden, head_weight, targets, advantage, policy_mask):
     n_dp = lax.axis_size("z")
     n_plane = lax.axis_size("x") * lax.axis_size("y")
-    core = lax.axis_index("c")
-    device = lax.axis_index(("z", "x", "y", "c"))
-    place = jnp.stack([core, device * cols, (device + 1 - 2 * core) * cols]).astype(jnp.int32)
     weight = head_weight.T
     depth = weight.shape[1]
     half = depth // 2
     swap = [(0, 1), (1, 0)]
-    smem = pl.BlockSpec(memory_space=pltpu.SMEM)
     local = pl.BlockSpec(memory_space=pltpu.VMEM)
 
     packed = pl.pallas_call(
@@ -284,13 +289,13 @@
     weight_own, weight_sent = pl.pallas_call(
         prepare_kernel,
         grid=(2,),
-        in_specs=[smem, pl.BlockSpec((cols, depth // 2), lambda i: (0, i))],
+        in_specs=[pl.BlockSpec((cols, depth // 2), lambda i: (0, i))],
         out_specs=[pl.BlockSpec((cols, half // 2), lambda i: (0, i))] * 2,
         out_shape=(shape(cols, half), shape(cols, half)),
         compiler_params=large,
         cost_estimate=cost(0, 24_000_000),
         name="prepare",
-    )(place, weight)
+    )(weight)
     packed, weight_own, weight_sent = lax.optimization_barrier((packed, weight_own, weight_sent))
     rows, meta, picks = pl.pallas_call(
         compact_kernel,
@@ -302,6 +307,8 @@
         compiler_params=small,
         name="compact",
     )(packed)
+    rows, weight_sent = lax.optimization_barrier((rows, weight_sent))
+    weight_got = lax.ppermute(weight_sent, "c", swap)
     line = along_lines(rows, True)
     lines = pl.pallas_call(
         copies_kernel,
@@ -310,31 +317,34 @@
         name="copies",
     )(line)
     mine = along_lines(lines, False).reshape(n_plane, width, policy)
-    partner = lax.ppermute(mine, "c", swap)
-
-    first = pl.pallas_call(
-        first_half_kernel,
-        in_specs=[smem] + [local] * 2,
-        out_shape=shape(cols, policy, dtype=f32),
-        compiler_params=small,
-        cost_estimate=cost(cols * depth * policy, 6_000_000),
-        name="first",
-    )(place, weight_own, mine)
+
+    def partial_logits(name, half_weight):
+        return pl.pallas_call(
+            partial_kernel,
+            in_specs=[local] * 2,
+            out_shape=shape(cols, policy, dtype=f32),
+            compiler_params=small,
+            cost_estimate=cost(cols * depth * policy, 6_000_000),
+            name=name,
+        )(half_weight, mine)
+
+    sent = partial_logits("partial_sent", weight_got)
+    got = lax.ppermute(sent, "c", swap)
+    own = partial_logits("partial_own", weight_own)
+    got, own, rows_sent = lax.optimization_barrier((got, own, mine))
+    partner = lax.ppermute(rows_sent, "c", swap)
     logits, stats = pl.pallas_call(
-        second_half_kernel,
-        in_specs=[smem] + [local] * 4,
+        stats_kernel,
+        in_specs=[local] * 3,
         out_shape=(
             shape(cols, policy, dtype=f32),
             shape(2 * n_dp, 4, policy, dtype=f32),
         ),
         compiler_params=small,
-        cost_estimate=cost(cols * depth * policy, 6_000_000),
-        name="second",
-    )(place, weight_sent, partner, first, meta)
-
-    logits, weight_sent = lax.optimization_barrier((logits, weight_sent))
-    weight_got = lax.ppermute(weight_sent, "c", swap)
+        name="stats",
+    )(own, got, meta)
     logits_got = lax.ppermute(logits, "c", swap)
+
     stats = lax.all_to_all(stats, ("z", "c"), 0, 0)
     stats = pl.pallas_call(
         combine_kernel,
@@ -343,11 +353,11 @@
         name="combine",
     )(stats)
     stats = lax.all_to_all(stats, ("x", "y"), 0, 0)
-    stats, weight_got, logits_got = lax.optimization_barrier((stats, weight_got, logits_got))
+    stats, partner, logits_got = lax.optimization_barrier((stats, partner, logits_got))
 
     summed, dlogits, loss = pl.pallas_call(
         grad_kernel,
-        in_specs=[smem] + [local] * 6,
+        in_specs=[local] * 6,
         out_shape=(
             shape(n_plane, width, policy),
             shape(cols, policy),
@@ -356,7 +366,7 @@
         compiler_params=small,
         cost_estimate=cost(2 * cols * depth * policy, 12_000_000),
         name="grad",
-    )(place, stats, meta, logits, logits_got, weight_own, weight_got)
+    )(stats, meta, logits, logits_got, weight_own, weight_got)
     parts = along_lines(summed.reshape(side, side, width, policy), False)
     line = pl.pallas_call(
         line_sum_kernel,
@@ -372,7 +382,7 @@
     parts = lax.all_to_all(spread, "z", 0, 0)
     head_grad = pl.pallas_call(
         head_kernel,
-        in_specs=[smem] + [local] * 3,
+        in_specs=[local] * 3,
         out_specs=pl.BlockSpec(memory_space=pl.ANY),
         out_shape=shape(cols, depth),
         scratch_shapes=[
@@ -383,7 +393,7 @@
         compiler_params=large,
         cost_estimate=cost(2 * cols * depth * policy, 10_000_000),
         name="head",
-    )(place, dlogits, mine, partner)
+    )(dlogits, mine, partner)
     parts, head_grad = lax.optimization_barrier((parts, head_grad))
     grad_rows = pl.pallas_call(
         sum_kernel, out_shape=shape(width, tok), compiler_params=small, name="total"

time: 134 us -> 132 us (0.985)
  Pallas kernels: 27.6 us -> 26.2 us
    ppermute x1 -> x2, waiting for transfers between devices: 1.68 us -> 0.01 us  [the longest x1 0.01 us: body(): got = lax.ppermute(sent, 'c', swap)]
    pallas_call x5 -> x6, Pallas kernels: 22.4 us -> 21.1 us  [the longest x1 7.17 us: body(): pl.pallas_call(head_kernel, in_specs=[local] * 3, out_specs=pl.BlockSpec(...]
  transfers between devices with their start and end apart: 5 -> 6, of which waited for: 3 -> 2; matrix products, arithmetic and copies ran while one was open for 0% -> 0% of each run, Pallas kernels for 11% -> 12%
where the time goes in v7:
time: 132 us; the launch traced here: 131 us
  blocking collectives  81.4 us (62%)
  Pallas kernels  26.2 us (20%)
  starting transfers between devices  12.7 us (10%)
  waiting for transfers between devices  9.51 us (7%)
    all_to_all x4, blocking collectives, along_lines(): lax.all_to_all(blocks, ('x', 'y', 'c'), 0, 0, axis_index_groups=groups)  59.9 us
    all_to_all x1, blocking collectives, body(): stats = lax.all_to_all(stats, ('z', 'c'), 0, 0)  10.8 us
    all_to_all x1, blocking collectives, body(): stats = lax.all_to_all(stats, ('x', 'y'), 0, 0)  10.6 us
    all_to_all x1, starting transfers between devices, body(): packed = lax.all_to_all(packed, 'z', 0, 0)  8.47 us
    pallas_call x1, Pallas kernels, body(): pl.pallas_call(head_kernel, in_specs=[local] * 3, out_specs=pl.BlockSpec(...  7.17 us
    all_to_all x1, waiting for transfers between devices, body(): packed = lax.all_to_all(packed, 'z', 0, 0)  6.29 us
    pallas_call x1, Pallas kernels, body(): pl.pallas_call(prepare_kernel, grid=(2,), in_specs=[pl.BlockSpec((cols, d...  5.59 us
    pallas_call x1, Pallas kernels, body(): pl.pallas_call(grad_kernel, in_specs=[local] * 6, out_shape=(shape(n_plan...  4.27 us
  transfers between devices with their start and end apart: 6, of which 2 were waited for; matrix products, arithmetic and copies ran while one was open for 0% of the time, Pallas kernels for 12%

profile of v7, /device:TPU:2, one launch (start us, length us, event | category | flops | bytes accessed | tf_op | source)
XLA Modules:
  0.0 131.4 jit_solution(10646086839162499903)
XLA Ops:
  0.6 1.7 %pack.1 = bf16[8,128,128]{2,1,0:T(8,128)(2,1)} custom-call(bf16[160,96]{1,0:T(8,128)(2,1)} %bitcast.17, s32[1,96]{1,0:T(1,128)} %bitcast.19, f32[1,96]{1,0:T(1,128)} %bitcast.20, s32[1,96]{1,0:T(1,128)} %bitcast.21), custom_call_target="tpu_custom_call" | custom-call | tf_op jit(solution)/shard_map/pack/pallas_call | solution.py:281
  2.3 8.5 %all-to-all-start = ((bf16[8,128,128]{2,1,0:T(8,128)(2,1)}), bf16[8,128,128]{2,1,0:T(8,128)(2,1)S(1)}, u32[]{:S(2)}, u32[]{:S(2)}) async-start(bf16[8,128,128]{2,1,0:T(8,128)(2,1)} %pack.1), calls=%async_computation | async-start | bytes 524288 | tf_op jit(solution)/shard_map/all_to_all | solution.py:288
  10.8 5.6 %prepare.1 = (bf16[592,2560]{1,0:T(8,128)(2,1)}, bf16[592,2560]{1,0:T(8,128)(2,1)}) custom-call(bf16[592,5120]{1,0:T(8,128)(2,1)} %bitcast.15), custom_call_target="tpu_custom_call" | custom-call | bytes 24000000 | tf_op jit(solution)/shard_map/prepare/pallas_call | solution.py:289
  16.3 6.3 %all-to-all-done.blocks_ref = bf16[8,128,128]{2,1,0:T(8,128)(2,1)S(1)} async-done(((bf16[8,128,128]{2,1,0:T(8,128)(2,1)}), bf16[8,128,128]{2,1,0:T(8,128)(2,1)S(1)}, u32[]{:S(2)}, u32[]{:S(2)}) %all-to-all-start) | async-done | bytes 262176 | tf_op jit(solution)/shard_map/all_to_all | solution.py:288
  22.6 0.8 compact.1
  23.4 0.1 collective-permute-start
  23.5 12.2 %all_to_all.40.rows_ref = bf16[4,160,384]{2,1,0:T(8,128)(2,1)S(1)} all-to-all(bf16[4,160,384]{2,1,0:T(8,128)(2,1)S(1)} %get-tuple-element.38), channel_id=1, replica_groups={{0,2,4,6},{8,10,12,14},{16,18,20,22},{24,26,28,30},{1,9,17,25},{3,11,19..., dimensions={0} | all-to-all | bytes 983040 | tf_op jit(solution)/shard_map/all_to_all | solution.py:265
  35.7 0.2 copies.1
  35.9 19.0 %all_to_all.41 = bf16[4,4,160,384]{3,2,1,0:T(8,128)(2,1)S(1)} all-to-all(bf16[4,4,160,384]{3,2,1,0:T(8,128)(2,1)S(1)} %copies.1), channel_id=1, replica_groups={{1,3,5,7},{9,11,13,15},{17,19,21,23},{25,27,29,31},{0,8,16,24},{2,10,18..., dimensions={0} | all-to-all | bytes 3932160 | tf_op jit(solution)/shard_map/all_to_all | solution.py:265
  54.8 0.0 copy-start
  54.8 0.0 copy-start.1
  54.8 0.0 collective-permute-done.weight_ref.weight_got_ref
  54.9 1.7 %partial_sent.1 = f32[592,384]{1,0:T(8,128)S(1)} custom-call(bf16[592,2560]{1,0:T(8,128)(2,1)S(1)} %collective-permute-done.weight_ref.weight_got_ref, bf16[16,160,384]{2,1,0:T(8,128)(2,1)S(1)} %bitcast.10), custom_call_target="tpu_custom_call" | custom-call | flops 1163919360 | bytes 6000000 | tf_op jit(solution)/shard_map/partial_sent/pallas_call | solution.py:322
  56.6 0.1 collective-permute-start.1
  56.7 0.7 copy-done.1
  57.4 1.7 %partial_own.1.own_ref = f32[592,384]{1,0:T(8,128)S(1)} custom-call(bf16[592,2560]{1,0:T(8,128)(2,1)S(1)} %copy-done.1, bf16[16,160,384]{2,1,0:T(8,128)(2,1)S(1)} %bitcast.11), custom_call_target="tpu_custom_call" | custom-call | flops 1163919360 | bytes 6000000 | tf_op jit(solution)/shard_map/partial_own/pallas_call | solution.py:322
  59.1 0.0 collective-permute-done.1.got_ref
  59.2 0.0 copy-done
  59.2 0.1 collective-permute-start.2
  59.3 0.6 stats.1
  59.9 0.6 collective-permute-start.3
  60.4 10.8 %all_to_all.42.in_ref = f32[16,4,384]{2,1,0:T(4,128)S(1)} all-to-all(f32[16,4,384]{2,1,0:T(4,128)S(1)} %get-tuple-element.43), channel_id=1, replica_groups=mesh['z'=8,'x'=4,'y'=4,'c'=2] {'z','c'}, dimensions={0} | all-to-all | bytes 196608 | tf_op jit(solution)/shard_map/all_to_all | solution.py:348
  71.3 0.1 combine.1
  71.4 10.6 %all_to_all.43.stats_ref = f32[16,4,384]{2,1,0:T(4,128)S(1)} all-to-all(f32[16,4,384]{2,1,0:T(4,128)S(1)} %combine.1), channel_id=1, replica_groups=mesh['z'=8,'x'=4,'y'=4,'c'=2] {'x','y'}, dimensions={0} | all-to-all | bytes 196608 | tf_op jit(solution)/shard_map/all_to_all | solution.py:355
  82.0 0.0 collective-permute-done.3.other_ref
  82.0 0.0 collective-permute-done.2.partner_ref
  82.0 4.3 %grad.1 = (bf16[16,160,384]{2,1,0:T(8,128)(2,1)S(1)}, bf16[592,384]{1,0:T(8,128)(2,1)S(1)}, f32[1,1]{1,0:T(1,128)}) custom-call(f32[16,4,384]{2,1,0:T(4,128)S(1)} %all_to_all.43.stats_ref, f32[16,384]{1,0:T(8,128)S(1)} %get-tuple-element.42.meta_ref, f32[592,384]{1,0:T(8,128)S(1)} %get-tuple-element.45.logits_ref, ...), custom_call_target="tpu_custom_call" | custom-call | flops 2327838720 | bytes 12000000 | tf_op jit(solution)/shard_map/grad/pallas_call | solution.py:358
  86.3 0.0 copy-start.2
  86.3 18.3 %all_to_all.44.parts_ref = bf16[4,4,160,384]{3,2,1,0:T(8,128)(2,1)S(1)} all-to-all(bf16[4,4,160,384]{3,2,1,0:T(8,128)(2,1)S(1)} %bitcast.14), channel_id=1, replica_groups={{1,3,5,7},{9,11,13,15},{17,19,21,23},{25,27,29,31},{0,8,16,24},{2,10,18..., dimensions={0} | all-to-all | bytes 3932160 | tf_op jit(solution)/shard_map/all_to_all | solution.py:265
  104.6 0.2 line_sum.1
  104.9 0.0 copy-done.2
  104.9 10.4 %all_to_all.45.parts_ref = bf16[4,160,384]{2,1,0:T(8,128)(2,1)S(1)} all-to-all(bf16[4,160,384]{2,1,0:T(8,128)(2,1)S(1)} %line_sum.1), channel_id=1, replica_groups={{0,2,4,6},{8,10,12,14},{16,18,20,22},{24,26,28,30},{1,9,17,25},{3,11,19..., dimensions={0} | all-to-all | bytes 983040 | tf_op jit(solution)/shard_map/all_to_all | solution.py:265
  115.3 1.5 %spread.1 = bf16[8,128,128]{2,1,0:T(8,128)(2,1)} custom-call(bf16[4,160,384]{2,1,0:T(8,128)(2,1)S(1)} %all_to_all.45.parts_ref, bf16[8,384,96]{2,1,0:T(8,128)(2,1)S(1)} %get-tuple-element.49.picks_ref), custom_call_target="tpu_custom_call" | custom-call | tf_op jit(solution)/shard_map/spread/pallas_call | solution.py:378
  116.8 3.4 %all-to-all-start.7 = ((bf16[8,128,128]{2,1,0:T(8,128)(2,1)}), bf16[8,128,128]{2,1,0:T(8,128)(2,1)S(1)}, u32[]{:S(2)}, u32[]{:S(2)}) async-start(bf16[8,128,128]{2,1,0:T(8,128)(2,1)} %spread.1), calls=%async_computation.7 | async-start | bytes 524288 | tf_op jit(solution)/shard_map/all_to_all | solution.py:382
  120.2 7.2 %head.1 = bf16[592,5120]{1,0:T(8,128)(2,1)} custom-call(bf16[592,384]{1,0:T(8,128)(2,1)} %copy-done.2, bf16[16,160,384]{2,1,0:T(8,128)(2,1)} %bitcast.13, bf16[16,160,384]{2,1,0:T(8,128)(2,1)} %collective-permute-done.2.partner_ref), custom_call_target="tpu_custom_call" | custom-call | flops 2327838720 | bytes 10000000 | tf_op jit(solution)/shard_map/head/pallas_call | solution.py:383
  127.4 3.2 %all-to-all-done.7.parts_ref = bf16[8,128,128]{2,1,0:T(8,128)(2,1)S(1)} async-done(((bf16[8,128,128]{2,1,0:T(8,128)(2,1)}), bf16[8,128,128]{2,1,0:T(8,128)(2,1)S(1)}, u32[]{:S(2)}, u32[]{:S(2)}) %all-to-all-start.7) | async-done | bytes 262176 | tf_op jit(solution)/shard_map/all_to_all | solution.py:382
  130.6 0.7 total.1
Async XLA Ops:
  2.3 20.3 %all-to-all-start = ((bf16[8,128,128]{2,1,0:T(8,128)(2,1)}), bf16[8,128,128]{2,1,0:T(8,128)(2,1)S(1)}, u32[]{:S(2)}, u32[]{:S(2)}) async-start(bf16[8,128,128]{2,1,0:T(8,128)(2,1)} %pack.1), calls=%async_computation | async-start | bytes 524288 | tf_op jit(solution)/shard_map/all_to_all | solution.py:288
  23.4 31.4 %collective-permute-start = (bf16[592,2560]{1,0:T(8,128)(2,1)}, bf16[592,2560]{1,0:T(8,128)(2,1)S(1)}, u32[]{:S(2)}, u32[]{:S(2)}) collective-permute-start(bf16[592,2560]{1,0:T(8,128)(2,1)} %get-tuple-element.37), channel_id=1, source_target_pairs={{0,1},{1,0},{2,3},{3,2},{4,5},{5,4},{6,7},{7,6},{8,9},{9,8},{10,11... | collective-permute-start | bytes 9093128 | tf_op jit(solution)/shard_map/ppermute | solution.py:311
  54.8 4.3 %copy-start = (bf16[4,4,160,384]{3,2,1,0:T(8,128)(2,1)}, bf16[4,4,160,384]{3,2,1,0:T(8,128)(2,1)S(1)}, u32[]{:S(2)}) copy-start(bf16[4,4,160,384]{3,2,1,0:T(8,128)(2,1)S(1)} %all_to_all.41) | copy-start | bytes 5898244
  54.8 2.6 %copy-start.1 = (bf16[592,2560]{1,0:T(8,128)(2,1)S(1)}, bf16[592,2560]{1,0:T(8,128)(2,1)}, u32[]{:S(2)}) copy-start(bf16[592,2560]{1,0:T(8,128)(2,1)} %get-tuple-element.39.weight_ref) | copy-start | bytes 9093124
  56.6 2.6 %collective-permute-start.1 = (f32[592,384]{1,0:T(8,128)S(1)}, f32[592,384]{1,0:T(8,128)S(1)}, u32[]{:S(2)}, u32[]{:S(2)}) collective-permute-start(f32[592,384]{1,0:T(8,128)S(1)} %partial_sent.1), channel_id=1, source_target_pairs={{0,1},{1,0},{2,3},{3,2},{4,5},{5,4},{6,7},{7,6},{8,9},{9,8},{10,11... | collective-permute-start | bytes 2727944 | tf_op jit(solution)/shard_map/ppermute | solution.py:332
  59.2 22.9 %collective-permute-start.2 = (bf16[16,160,384]{2,1,0:T(8,128)(2,1)S(1)}, bf16[16,160,384]{2,1,0:T(8,128)(2,1)}, u32[]{:S(2)}, u32[]{:S(2)}) collective-permute-start(bf16[16,160,384]{2,1,0:T(8,128)(2,1)S(1)} %bitcast.12), channel_id=1, source_target_pairs={{0,1},{1,0},{2,3},{3,2},{4,5},{5,4},{6,7},{7,6},{8,9},{9,8},{10,11... | collective-permute-start | bytes 5898248 | tf_op jit(solution)/shard_map/ppermute | solution.py:335
  59.9 22.2 %collective-permute-start.3 = (f32[592,384]{1,0:T(8,128)S(1)}, f32[592,384]{1,0:T(8,128)S(1)}, u32[]{:S(2)}, u32[]{:S(2)}) collective-permute-start(f32[592,384]{1,0:T(8,128)S(1)} %get-tuple-element.45.logits_ref), channel_id=1, source_target_pairs={{0,1},{1,0},{2,3},{3,2},{4,5},{5,4},{6,7},{7,6},{8,9},{9,8},{10,11... | collective-permute-start | bytes 2727944 | tf_op jit(solution)/shard_map/ppermute | solution.py:346
  86.3 18.6 %copy-start.2 = (bf16[592,384]{1,0:T(8,128)(2,1)}, bf16[592,384]{1,0:T(8,128)(2,1)S(1)}, u32[]{:S(2)}) copy-start(bf16[592,384]{1,0:T(8,128)(2,1)S(1)} %get-tuple-element.52.dlogits_ref) | copy-start | bytes 1363972
  116.8 13.8 %all-to-all-start.7 = ((bf16[8,128,128]{2,1,0:T(8,128)(2,1)}), bf16[8,128,128]{2,1,0:T(8,128)(2,1)S(1)}, u32[]{:S(2)}, u32[]{:S(2)}) async-start(bf16[8,128,128]{2,1,0:T(8,128)(2,1)} %spread.1), calls=%async_computation.7 | async-start | bytes 524288 | tf_op jit(solution)/shard_map/all_to_all | solution.py:382

commit v8 on v7

--- a/solution.py
+++ b/solution.py
@@ -71,11 +71,12 @@
         starts.append(start)
         start = start + total[z : z + 1]
     rank = jnp.where(mask > 0, prefix + jnp.concatenate(starts, axis=0), -1.0).astype(jnp.int32)
+    picks_ref[...] = jnp.zeros_like(picks_ref)
     place = lax.broadcasted_iota(jnp.int32, (policy, tok), 0)
     acc = jnp.zeros((width + meta_rows, policy), f32)
     for z in range(groups):
         pick = (place == rank[z : z + 1]).astype(f32).astype(bf16)
-        picks_ref[z] = pick
+        picks_ref[:, z * 128 : z * 128 + tok] = pick
         meta = jnp.concatenate([metas[z], jnp.zeros_like(metas[z])], axis=0).astype(bf16)
         block = jnp.concatenate([unfold(blocks_ref[z]), meta], axis=0)
         acc += lax.dot_general(block, pick, nt_dims, preferred_element_type=f32)
@@ -241,9 +242,10 @@
 
 def spread_kernel(parts_ref, picks_ref, out_ref):
     total = jnp.sum(parts_ref[...].astype(f32), axis=0).astype(bf16)
+    rows = jnp.dot(total, picks_ref[...], preferred_element_type=f32)
     for z in range(out_ref.shape[0]):
-        rows = jnp.dot(total, picks_ref[z], preferred_element_type=f32)
-        out_ref[z] = fold(rows, jnp.zeros((32, 32), f32)).astype(bf16)
+        at = z * 128
+        out_ref[z] = fold(rows[:, at : at + tok], jnp.zeros((32, 32), f32)).astype(bf16)
 
 
 def sum_kernel(parts_ref, out_ref):
@@ -263,6 +265,11 @@
     groups = [[device(x, y, y_core) for y in range(side)] for x in range(side)]
     groups += [[device(x, y, x_core) for x in range(side)] for y in range(side)]
     return lax.all_to_all(blocks, ("x", "y", "c"), 0, 0, axis_index_groups=groups)
+
+
+def along_z(blocks):
+    planes = list(range(blocks.shape[0]))[::-1]
+    return lax.all_to_all(blocks, "z", 0, 0, axis_index_groups=[planes])
 
 
 def cost(flops, nbytes):
@@ -285,7 +292,7 @@
         name="pack",
     )(hidden.T, targets[None], advantage[None], policy_mask[None])
     packed, weight = lax.optimization_barrier((packed, weight))
-    packed = lax.all_to_all(packed, "z", 0, 0)
+    packed = along_z(packed)
     weight_own, weight_sent = pl.pallas_call(
         prepare_kernel,
         grid=(2,),
@@ -302,7 +309,7 @@
         out_shape=(
             shape(side, width, policy),
             shape(meta_rows, policy, dtype=f32),
-            shape(n_dp, policy, tok),
+            shape(policy, n_dp * 128),
         ),
         compiler_params=small,
         name="compact",
@@ -379,7 +386,7 @@
         spread_kernel, out_shape=shape(n_dp, 128, 128), compiler_params=small, name="spread"
     )(parts, picks)
     spread, dlogits = lax.optimization_barrier((spread, dlogits))
-    parts = lax.all_to_all(spread, "z", 0, 0)
+    parts = along_z(spread)
     head_grad = pl.pallas_call(
         head_kernel,
         in_specs=[local] * 3,

time: 132 us -> 130 us (0.985)
  waiting for transfers between devices: 9.51 us -> 1.71 us
  blocking collectives: 81.4 us -> 84.9 us
  starting transfers between devices: 12.7 us -> 15 us
    all_to_all x2, waiting for transfers between devices: 9.5 us -> 1.7 us  [along_z(): return lax.all_to_all(blocks, 'z', 0, 0, axis_index_groups=[planes])]
    all_to_all x1, blocking collectives: 10.8 us -> 14.4 us  [body(): stats = lax.all_to_all(stats, ('z', 'c'), 0, 0)]
    all_to_all x2, starting transfers between devices: 11.9 us -> 14.1 us  [along_z(): return lax.all_to_all(blocks, 'z', 0, 0, axis_index_groups=[planes])]
  transfers between devices with their start and end apart: 6 -> 6, of which waited for: 2 -> 1; matrix products, arithmetic and copies ran while one was open for 0% -> 0% of each run, Pallas kernels for 12% -> 12%
where the time goes in v8:
time: 130 us; the launch traced here: 129 us
  blocking collectives  84.9 us (65%)
  Pallas kernels  26.3 us (20%)
  starting transfers between devices  15 us (12%)
  waiting for transfers between devices  1.71 us (1%)
    all_to_all x4, blocking collectives, along_lines(): lax.all_to_all(blocks, ('x', 'y', 'c'), 0, 0, axis_index_groups=groups)  59.9 us
    all_to_all x1, blocking collectives, body(): stats = lax.all_to_all(stats, ('z', 'c'), 0, 0)  14.4 us
    all_to_all x2, starting transfers between devices, along_z(): return lax.all_to_all(blocks, 'z', 0, 0, axis_index_groups=[planes])  14.1 us
    all_to_all x1, blocking collectives, body(): stats = lax.all_to_all(stats, ('x', 'y'), 0, 0)  10.6 us
    pallas_call x1, Pallas kernels, body(): pl.pallas_call(head_kernel, in_specs=[local] * 3, out_specs=pl.BlockSpec(...  7.17 us
    pallas_call x1, Pallas kernels, body(): pl.pallas_call(prepare_kernel, grid=(2,), in_specs=[pl.BlockSpec((cols, d...  5.58 us
    pallas_call x1, Pallas kernels, body(): pl.pallas_call(grad_kernel, in_specs=[local] * 6, out_shape=(shape(n_plan...  4.27 us
    pallas_call x2, Pallas kernels, partial_logits(): pl.pallas_call(partial_kernel, in_specs=[local] * 2, out_shape=shape(cols...  3.45 us
  transfers between devices with their start and end apart: 6, of which 1 were waited for; matrix products, arithmetic and copies ran while one was open for 0% of the time, Pallas kernels for 12%

profile of v8, /device:TPU:2, one launch (start us, length us, event | category | flops | bytes accessed | tf_op | source)
XLA Modules:
  0.0 129.3 jit_solution(17017977632016893551)
XLA Ops:
  0.6 1.7 %pack.1 = bf16[8,128,128]{2,1,0:T(8,128)(2,1)} custom-call(bf16[160,96]{1,0:T(8,128)(2,1)} %bitcast.17, s32[1,96]{1,0:T(1,128)} %bitcast.19, f32[1,96]{1,0:T(1,128)} %bitcast.20, s32[1,96]{1,0:T(1,128)} %bitcast.21), custom_call_target="tpu_custom_call" | custom-call | tf_op jit(solution)/shard_map/pack/pallas_call | solution.py:288
  2.3 9.2 %all-to-all-start = ((bf16[8,128,128]{2,1,0:T(8,128)(2,1)}), bf16[8,128,128]{2,1,0:T(8,128)(2,1)S(1)}, u32[]{:S(2)}, u32[]{:S(2)}) async-start(bf16[8,128,128]{2,1,0:T(8,128)(2,1)} %pack.1), calls=%async_computation | async-start | bytes 524288 | tf_op jit(solution)/shard_map/all_to_all | solution.py:272
  11.5 5.6 %prepare.1 = (bf16[592,2560]{1,0:T(8,128)(2,1)}, bf16[592,2560]{1,0:T(8,128)(2,1)}) custom-call(bf16[592,5120]{1,0:T(8,128)(2,1)} %bitcast.15), custom_call_target="tpu_custom_call" | custom-call | bytes 24000000 | tf_op jit(solution)/shard_map/prepare/pallas_call | solution.py:296
  17.1 1.7 %all-to-all-done.blocks_ref = bf16[8,128,128]{2,1,0:T(8,128)(2,1)S(1)} async-done(((bf16[8,128,128]{2,1,0:T(8,128)(2,1)}), bf16[8,128,128]{2,1,0:T(8,128)(2,1)S(1)}, u32[]{:S(2)}, u32[]{:S(2)}) %all-to-all-start) | async-done | bytes 262176 | tf_op jit(solution)/shard_map/all_to_all | solution.py:272
  18.8 0.8 compact.1
  19.6 0.1 collective-permute-start
  19.7 12.2 %all_to_all.40.rows_ref = bf16[4,160,384]{2,1,0:T(8,128)(2,1)S(1)} all-to-all(bf16[4,160,384]{2,1,0:T(8,128)(2,1)S(1)} %get-tuple-element.38), channel_id=1, replica_groups={{0,2,4,6},{8,10,12,14},{16,18,20,22},{24,26,28,30},{1,9,17,25},{3,11,19..., dimensions={0} | all-to-all | bytes 983040 | tf_op jit(solution)/shard_map/all_to_all | solution.py:267
  31.9 0.2 copies.1
  32.0 19.0 %all_to_all.41 = bf16[4,4,160,384]{3,2,1,0:T(8,128)(2,1)S(1)} all-to-all(bf16[4,4,160,384]{3,2,1,0:T(8,128)(2,1)S(1)} %copies.1), channel_id=1, replica_groups={{1,3,5,7},{9,11,13,15},{17,19,21,23},{25,27,29,31},{0,8,16,24},{2,10,18..., dimensions={0} | all-to-all | bytes 3932160 | tf_op jit(solution)/shard_map/all_to_all | solution.py:267
  51.0 0.0 copy-start
  51.0 0.0 copy-start.1
  51.0 0.0 collective-permute-done.weight_ref.weight_got_ref
  51.0 1.7 %partial_sent.1 = f32[592,384]{1,0:T(8,128)S(1)} custom-call(bf16[592,2560]{1,0:T(8,128)(2,1)S(1)} %collective-permute-done.weight_ref.weight_got_ref, bf16[16,160,384]{2,1,0:T(8,128)(2,1)S(1)} %bitcast.10), custom_call_target="tpu_custom_call" | custom-call | flops 1163919360 | bytes 6000000 | tf_op jit(solution)/shard_map/partial_sent/pallas_call | solution.py:329
  52.8 0.1 collective-permute-start.1
  52.9 0.7 copy-done.1
  53.6 1.7 %partial_own.1.own_ref = f32[592,384]{1,0:T(8,128)S(1)} custom-call(bf16[592,2560]{1,0:T(8,128)(2,1)S(1)} %copy-done.1, bf16[16,160,384]{2,1,0:T(8,128)(2,1)S(1)} %bitcast.11), custom_call_target="tpu_custom_call" | custom-call | flops 1163919360 | bytes 6000000 | tf_op jit(solution)/shard_map/partial_own/pallas_call | solution.py:329
  55.3 0.0 collective-permute-done.1.got_ref
  55.3 0.0 copy-done
  55.3 0.1 collective-permute-start.2
  55.4 0.6 stats.1
  56.0 0.6 collective-permute-start.3
  56.6 14.4 %all_to_all.42.in_ref = f32[16,4,384]{2,1,0:T(4,128)S(1)} all-to-all(f32[16,4,384]{2,1,0:T(4,128)S(1)} %get-tuple-element.43), channel_id=1, replica_groups=mesh['z'=8,'x'=4,'y'=4,'c'=2] {'z','c'}, dimensions={0} | all-to-all | bytes 196608 | tf_op jit(solution)/shard_map/all_to_all | solution.py:355
  71.0 0.1 combine.1
  71.1 10.6 %all_to_all.43.stats_ref = f32[16,4,384]{2,1,0:T(4,128)S(1)} all-to-all(f32[16,4,384]{2,1,0:T(4,128)S(1)} %combine.1), channel_id=1, replica_groups=mesh['z'=8,'x'=4,'y'=4,'c'=2] {'x','y'}, dimensions={0} | all-to-all | bytes 196608 | tf_op jit(solution)/shard_map/all_to_all | solution.py:362
  81.7 0.0 collective-permute-done.3.other_ref
  81.7 0.0 collective-permute-done.2.partner_ref
  81.7 4.3 %grad.1 = (bf16[16,160,384]{2,1,0:T(8,128)(2,1)S(1)}, bf16[592,384]{1,0:T(8,128)(2,1)S(1)}, f32[1,1]{1,0:T(1,128)}) custom-call(f32[16,4,384]{2,1,0:T(4,128)S(1)} %all_to_all.43.stats_ref, f32[16,384]{1,0:T(8,128)S(1)} %get-tuple-element.42.meta_ref, f32[592,384]{1,0:T(8,128)S(1)} %get-tuple-element.45.logits_ref, ...), custom_call_target="tpu_custom_call" | custom-call | flops 2327838720 | bytes 12000000 | tf_op jit(solution)/shard_map/grad/pallas_call | solution.py:365
  86.0 0.0 copy-start.2
  86.0 18.3 %all_to_all.44.parts_ref = bf16[4,4,160,384]{3,2,1,0:T(8,128)(2,1)S(1)} all-to-all(bf16[4,4,160,384]{3,2,1,0:T(8,128)(2,1)S(1)} %bitcast.14), channel_id=1, replica_groups={{1,3,5,7},{9,11,13,15},{17,19,21,23},{25,27,29,31},{0,8,16,24},{2,10,18..., dimensions={0} | all-to-all | bytes 3932160 | tf_op jit(solution)/shard_map/all_to_all | solution.py:267
  104.3 0.2 line_sum.1
  104.6 0.0 copy-done.2
  104.6 10.4 %all_to_all.45.parts_ref = bf16[4,160,384]{2,1,0:T(8,128)(2,1)S(1)} all-to-all(bf16[4,160,384]{2,1,0:T(8,128)(2,1)S(1)} %line_sum.1), channel_id=1, replica_groups={{0,2,4,6},{8,10,12,14},{16,18,20,22},{24,26,28,30},{1,9,17,25},{3,11,19..., dimensions={0} | all-to-all | bytes 983040 | tf_op jit(solution)/shard_map/all_to_all | solution.py:267
  115.0 1.5 %spread.1 = bf16[8,128,128]{2,1,0:T(8,128)(2,1)} custom-call(bf16[4,160,384]{2,1,0:T(8,128)(2,1)S(1)} %all_to_all.45.parts_ref, bf16[384,1024]{1,0:T(8,128)(2,1)S(1)} %get-tuple-element.49.picks_ref), custom_call_target="tpu_custom_call" | custom-call | tf_op jit(solution)/shard_map/spread/pallas_call | solution.py:385
  116.5 4.9 %all-to-all-start.7 = ((bf16[8,128,128]{2,1,0:T(8,128)(2,1)}), bf16[8,128,128]{2,1,0:T(8,128)(2,1)S(1)}, u32[]{:S(2)}, u32[]{:S(2)}) async-start(bf16[8,128,128]{2,1,0:T(8,128)(2,1)} %spread.1), calls=%async_computation.7 | async-start | bytes 524288 | tf_op jit(solution)/shard_map/all_to_all | solution.py:272
  121.4 7.2 %head.1 = bf16[592,5120]{1,0:T(8,128)(2,1)} custom-call(bf16[592,384]{1,0:T(8,128)(2,1)} %copy-done.2, bf16[16,160,384]{2,1,0:T(8,128)(2,1)} %bitcast.13, bf16[16,160,384]{2,1,0:T(8,128)(2,1)} %collective-permute-done.2.partner_ref), custom_call_target="tpu_custom_call" | custom-call | flops 2327838720 | bytes 10000000 | tf_op jit(solution)/shard_map/head/pallas_call | solution.py:390
  128.6 0.0 all-to-all-done.7.parts_ref
  128.6 0.7 total.1
Async XLA Ops:
  2.3 16.5 %all-to-all-start = ((bf16[8,128,128]{2,1,0:T(8,128)(2,1)}), bf16[8,128,128]{2,1,0:T(8,128)(2,1)S(1)}, u32[]{:S(2)}, u32[]{:S(2)}) async-start(bf16[8,128,128]{2,1,0:T(8,128)(2,1)} %pack.1), calls=%async_computation | async-start | bytes 524288 | tf_op jit(solution)/shard_map/all_to_all | solution.py:272
  19.6 31.4 %collective-permute-start = (bf16[592,2560]{1,0:T(8,128)(2,1)}, bf16[592,2560]{1,0:T(8,128)(2,1)S(1)}, u32[]{:S(2)}, u32[]{:S(2)}) collective-permute-start(bf16[592,2560]{1,0:T(8,128)(2,1)} %get-tuple-element.37), channel_id=1, source_target_pairs={{0,1},{1,0},{2,3},{3,2},{4,5},{5,4},{6,7},{7,6},{8,9},{9,8},{10,11... | collective-permute-start | bytes 9093128 | tf_op jit(solution)/shard_map/ppermute | solution.py:318
  51.0 4.3 %copy-start = (bf16[4,4,160,384]{3,2,1,0:T(8,128)(2,1)}, bf16[4,4,160,384]{3,2,1,0:T(8,128)(2,1)S(1)}, u32[]{:S(2)}) copy-start(bf16[4,4,160,384]{3,2,1,0:T(8,128)(2,1)S(1)} %all_to_all.41) | copy-start | bytes 5898244
  51.0 2.6 %copy-start.1 = (bf16[592,2560]{1,0:T(8,128)(2,1)S(1)}, bf16[592,2560]{1,0:T(8,128)(2,1)}, u32[]{:S(2)}) copy-start(bf16[592,2560]{1,0:T(8,128)(2,1)} %get-tuple-element.39.weight_ref) | copy-start | bytes 9093124
  52.8 2.6 %collective-permute-start.1 = (f32[592,384]{1,0:T(8,128)S(1)}, f32[592,384]{1,0:T(8,128)S(1)}, u32[]{:S(2)}, u32[]{:S(2)}) collective-permute-start(f32[592,384]{1,0:T(8,128)S(1)} %partial_sent.1), channel_id=1, source_target_pairs={{0,1},{1,0},{2,3},{3,2},{4,5},{5,4},{6,7},{7,6},{8,9},{9,8},{10,11... | collective-permute-start | bytes 2727944 | tf_op jit(solution)/shard_map/ppermute | solution.py:339
  55.3 26.4 %collective-permute-start.2 = (bf16[16,160,384]{2,1,0:T(8,128)(2,1)S(1)}, bf16[16,160,384]{2,1,0:T(8,128)(2,1)}, u32[]{:S(2)}, u32[]{:S(2)}) collective-permute-start(bf16[16,160,384]{2,1,0:T(8,128)(2,1)S(1)} %bitcast.12), channel_id=1, source_target_pairs={{0,1},{1,0},{2,3},{3,2},{4,5},{5,4},{6,7},{7,6},{8,9},{9,8},{10,11... | collective-permute-start | bytes 5898248 | tf_op jit(solution)/shard_map/ppermute | solution.py:342
  56.0 25.7 %collective-permute-start.3 = (f32[592,384]{1,0:T(8,128)S(1)}, f32[592,384]{1,0:T(8,128)S(1)}, u32[]{:S(2)}, u32[]{:S(2)}) collective-permute-start(f32[592,384]{1,0:T(8,128)S(1)} %get-tuple-element.45.logits_ref), channel_id=1, source_target_pairs={{0,1},{1,0},{2,3},{3,2},{4,5},{5,4},{6,7},{7,6},{8,9},{9,8},{10,11... | collective-permute-start | bytes 2727944 | tf_op jit(solution)/shard_map/ppermute | solution.py:353
  86.0 18.6 %copy-start.2 = (bf16[592,384]{1,0:T(8,128)(2,1)}, bf16[592,384]{1,0:T(8,128)(2,1)S(1)}, u32[]{:S(2)}) copy-start(bf16[592,384]{1,0:T(8,128)(2,1)S(1)} %get-tuple-element.52.dlogits_ref) | copy-start | bytes 1363972
  116.5 12.1 %all-to-all-start.7 = ((bf16[8,128,128]{2,1,0:T(8,128)(2,1)}), bf16[8,128,128]{2,1,0:T(8,128)(2,1)S(1)}, u32[]{:S(2)}, u32[]{:S(2)}) async-start(bf16[8,128,128]{2,1,0:T(8,128)(2,1)} %spread.1), calls=%async_computation.7 | async-start | bytes 524288 | tf_op jit(solution)/shard_map/all_to_all | solution.py:272

commit v9 on v8

--- a/solution.py
+++ b/solution.py
@@ -352,7 +352,8 @@
     )(own, got, meta)
     logits_got = lax.ppermute(logits, "c", swap)
 
-    stats = lax.all_to_all(stats, ("z", "c"), 0, 0)
+    falling = list(range(2 * n_dp))[::-1]
+    stats = lax.all_to_all(stats, ("z", "c"), 0, 0, axis_index_groups=[falling])
     stats = pl.pallas_call(
         combine_kernel,
         out_shape=shape(n_plane, 4, policy, dtype=f32),

time: 130 us -> 130 us (level)
  blocking collectives: 84.9 us -> 83 us
  starting transfers between devices: 15 us -> 16.3 us
    all_to_all x1, blocking collectives: 14.4 us -> 12.4 us  [body(): stats = lax.all_to_all(stats, ('z', 'c'), 0, 0, axis_index_groups=[falling])]
    all_to_all x2, starting transfers between devices: 14.1 us -> 15.4 us  [along_z(): return lax.all_to_all(blocks, 'z', 0, 0, axis_index_groups=[planes])]
where the time goes in v9:
time: 130 us; the launch traced here: 129 us
  blocking collectives  83 us (64%)
  Pallas kernels  26.3 us (20%)
  starting transfers between devices  16.3 us (13%)
  waiting for transfers between devices  1.71 us (1%)
    all_to_all x4, blocking collectives, along_lines(): lax.all_to_all(blocks, ('x', 'y', 'c'), 0, 0, axis_index_groups=groups)  59.9 us
    all_to_all x2, starting transfers between devices, along_z(): return lax.all_to_all(blocks, 'z', 0, 0, axis_index_groups=[planes])  15.4 us
    all_to_all x1, blocking collectives, body(): stats = lax.all_to_all(stats, ('z', 'c'), 0, 0, axis_index_groups=[falling])  12.4 us
    all_to_all x1, blocking collectives, body(): stats = lax.all_to_all(stats, ('x', 'y'), 0, 0)  10.6 us
    pallas_call x1, Pallas kernels, body(): pl.pallas_call(head_kernel, in_specs=[local] * 3, out_specs=pl.BlockSpec(...  7.16 us
    pallas_call x1, Pallas kernels, body(): pl.pallas_call(prepare_kernel, grid=(2,), in_specs=[pl.BlockSpec((cols, d...  5.58 us
    pallas_call x1, Pallas kernels, body(): pl.pallas_call(grad_kernel, in_specs=[local] * 6, out_shape=(shape(n_plan...  4.27 us
    pallas_call x2, Pallas kernels, partial_logits(): pl.pallas_call(partial_kernel, in_specs=[local] * 2, out_shape=shape(cols...  3.45 us
  transfers between devices with their start and end apart: 6, of which 1 were waited for; matrix products, arithmetic and copies ran while one was open for 0% of the time, Pallas kernels for 12%

profile of v9, /device:TPU:2, one launch (start us, length us, event | category | flops | bytes accessed | tf_op | source)
XLA Modules:
  0.0 128.7 jit_solution(16192829263258954880)
XLA Ops:
  0.6 1.7 %pack.1 = bf16[8,128,128]{2,1,0:T(8,128)(2,1)} custom-call(bf16[160,96]{1,0:T(8,128)(2,1)} %bitcast.17, s32[1,96]{1,0:T(1,128)} %bitcast.19, f32[1,96]{1,0:T(1,128)} %bitcast.20, s32[1,96]{1,0:T(1,128)} %bitcast.21), custom_call_target="tpu_custom_call" | custom-call | tf_op jit(solution)/shard_map/pack/pallas_call | solution.py:288
  2.3 9.2 %all-to-all-start = ((bf16[8,128,128]{2,1,0:T(8,128)(2,1)}), bf16[8,128,128]{2,1,0:T(8,128)(2,1)S(1)}, u32[]{:S(2)}, u32[]{:S(2)}) async-start(bf16[8,128,128]{2,1,0:T(8,128)(2,1)} %pack.1), calls=%async_computation | async-start | bytes 524288 | tf_op jit(solution)/shard_map/all_to_all | solution.py:272
  11.5 5.6 %prepare.1 = (bf16[592,2560]{1,0:T(8,128)(2,1)}, bf16[592,2560]{1,0:T(8,128)(2,1)}) custom-call(bf16[592,5120]{1,0:T(8,128)(2,1)} %bitcast.15), custom_call_target="tpu_custom_call" | custom-call | bytes 24000000 | tf_op jit(solution)/shard_map/prepare/pallas_call | solution.py:296
  17.1 1.7 %all-to-all-done.blocks_ref = bf16[8,128,128]{2,1,0:T(8,128)(2,1)S(1)} async-done(((bf16[8,128,128]{2,1,0:T(8,128)(2,1)}), bf16[8,128,128]{2,1,0:T(8,128)(2,1)S(1)}, u32[]{:S(2)}, u32[]{:S(2)}) %all-to-all-start) | async-done | bytes 262176 | tf_op jit(solution)/shard_map/all_to_all | solution.py:272
  18.8 0.8 compact.1
  19.6 0.1 collective-permute-start
  19.7 12.2 %all_to_all.40.rows_ref = bf16[4,160,384]{2,1,0:T(8,128)(2,1)S(1)} all-to-all(bf16[4,160,384]{2,1,0:T(8,128)(2,1)S(1)} %get-tuple-element.38), channel_id=1, replica_groups={{0,2,4,6},{8,10,12,14},{16,18,20,22},{24,26,28,30},{1,9,17,25},{3,11,19..., dimensions={0} | all-to-all | bytes 983040 | tf_op jit(solution)/shard_map/all_to_all | solution.py:267
  31.9 0.2 copies.1
  32.0 19.0 %all_to_all.41 = bf16[4,4,160,384]{3,2,1,0:T(8,128)(2,1)S(1)} all-to-all(bf16[4,4,160,384]{3,2,1,0:T(8,128)(2,1)S(1)} %copies.1), channel_id=1, replica_groups={{1,3,5,7},{9,11,13,15},{17,19,21,23},{25,27,29,31},{0,8,16,24},{2,10,18..., dimensions={0} | all-to-all | bytes 3932160 | tf_op jit(solution)/shard_map/all_to_all | solution.py:267
  51.0 0.0 copy-start
  51.0 0.0 copy-start.1
  51.0 0.0 collective-permute-done.weight_ref.weight_got_ref
  51.0 1.7 %partial_sent.1 = f32[592,384]{1,0:T(8,128)S(1)} custom-call(bf16[592,2560]{1,0:T(8,128)(2,1)S(1)} %collective-permute-done.weight_ref.weight_got_ref, bf16[16,160,384]{2,1,0:T(8,128)(2,1)S(1)} %bitcast.10), custom_call_target="tpu_custom_call" | custom-call | flops 1163919360 | bytes 6000000 | tf_op jit(solution)/shard_map/partial_sent/pallas_call | solution.py:329
  52.8 0.1 collective-permute-start.1
  52.9 0.7 copy-done.1
  53.6 1.7 %partial_own.1.own_ref = f32[592,384]{1,0:T(8,128)S(1)} custom-call(bf16[592,2560]{1,0:T(8,128)(2,1)S(1)} %copy-done.1, bf16[16,160,384]{2,1,0:T(8,128)(2,1)S(1)} %bitcast.11), custom_call_target="tpu_custom_call" | custom-call | flops 1163919360 | bytes 6000000 | tf_op jit(solution)/shard_map/partial_own/pallas_call | solution.py:329
  55.3 0.0 collective-permute-done.1.got_ref
  55.3 0.0 copy-done
  55.3 0.1 collective-permute-start.2
  55.4 0.6 stats.1
  56.0 0.6 collective-permute-start.3
  56.6 12.4 %all_to_all.42.in_ref = f32[16,4,384]{2,1,0:T(4,128)S(1)} all-to-all(f32[16,4,384]{2,1,0:T(4,128)S(1)} %get-tuple-element.43), channel_id=1, replica_groups={{225,224,193,192,161,160,129,128,97,96,65,64,33,32,1,0},{227,226,195,19..., dimensions={0} | all-to-all | bytes 196608 | tf_op jit(solution)/shard_map/all_to_all | solution.py:356
  69.0 0.1 combine.1
  69.2 10.6 %all_to_all.43.stats_ref = f32[16,4,384]{2,1,0:T(4,128)S(1)} all-to-all(f32[16,4,384]{2,1,0:T(4,128)S(1)} %combine.1), channel_id=1, replica_groups=mesh['z'=8,'x'=4,'y'=4,'c'=2] {'x','y'}, dimensions={0} | all-to-all | bytes 196608 | tf_op jit(solution)/shard_map/all_to_all | solution.py:363
  79.8 0.0 collective-permute-done.3.other_ref
  79.8 0.0 collective-permute-done.2.partner_ref
  79.8 4.3 %grad.1 = (bf16[16,160,384]{2,1,0:T(8,128)(2,1)S(1)}, bf16[592,384]{1,0:T(8,128)(2,1)S(1)}, f32[1,1]{1,0:T(1,128)}) custom-call(f32[16,4,384]{2,1,0:T(4,128)S(1)} %all_to_all.43.stats_ref, f32[16,384]{1,0:T(8,128)S(1)} %get-tuple-element.42.meta_ref, f32[592,384]{1,0:T(8,128)S(1)} %get-tuple-element.45.logits_ref, ...), custom_call_target="tpu_custom_call" | custom-call | flops 2327838720 | bytes 12000000 | tf_op jit(solution)/shard_map/grad/pallas_call | solution.py:366
  84.1 0.0 copy-start.2
  84.1 18.3 %all_to_all.44.parts_ref = bf16[4,4,160,384]{3,2,1,0:T(8,128)(2,1)S(1)} all-to-all(bf16[4,4,160,384]{3,2,1,0:T(8,128)(2,1)S(1)} %bitcast.14), channel_id=1, replica_groups={{1,3,5,7},{9,11,13,15},{17,19,21,23},{25,27,29,31},{0,8,16,24},{2,10,18..., dimensions={0} | all-to-all | bytes 3932160 | tf_op jit(solution)/shard_map/all_to_all | solution.py:267
  102.4 0.2 line_sum.1
  102.6 0.0 copy-done.2
  102.7 10.4 %all_to_all.45.parts_ref = bf16[4,160,384]{2,1,0:T(8,128)(2,1)S(1)} all-to-all(bf16[4,160,384]{2,1,0:T(8,128)(2,1)S(1)} %line_sum.1), channel_id=1, replica_groups={{0,2,4,6},{8,10,12,14},{16,18,20,22},{24,26,28,30},{1,9,17,25},{3,11,19..., dimensions={0} | all-to-all | bytes 983040 | tf_op jit(solution)/shard_map/all_to_all | solution.py:267
  113.1 1.5 %spread.1 = bf16[8,128,128]{2,1,0:T(8,128)(2,1)} custom-call(bf16[4,160,384]{2,1,0:T(8,128)(2,1)S(1)} %all_to_all.45.parts_ref, bf16[384,1024]{1,0:T(8,128)(2,1)S(1)} %get-tuple-element.49.picks_ref), custom_call_target="tpu_custom_call" | custom-call | tf_op jit(solution)/shard_map/spread/pallas_call | solution.py:386
  114.6 6.2 %all-to-all-start.7 = ((bf16[8,128,128]{2,1,0:T(8,128)(2,1)}), bf16[8,128,128]{2,1,0:T(8,128)(2,1)S(1)}, u32[]{:S(2)}, u32[]{:S(2)}) async-start(bf16[8,128,128]{2,1,0:T(8,128)(2,1)} %spread.1), calls=%async_computation.7 | async-start | bytes 524288 | tf_op jit(solution)/shard_map/all_to_all | solution.py:272
  120.8 7.2 %head.1 = bf16[592,5120]{1,0:T(8,128)(2,1)} custom-call(bf16[592,384]{1,0:T(8,128)(2,1)} %copy-done.2, bf16[16,160,384]{2,1,0:T(8,128)(2,1)} %bitcast.13, bf16[16,160,384]{2,1,0:T(8,128)(2,1)} %collective-permute-done.2.partner_ref), custom_call_target="tpu_custom_call" | custom-call | flops 2327838720 | bytes 10000000 | tf_op jit(solution)/shard_map/head/pallas_call | solution.py:391
  128.0 0.0 all-to-all-done.7.parts_ref
  128.0 0.7 total.1
Async XLA Ops:
  2.3 16.5 %all-to-all-start = ((bf16[8,128,128]{2,1,0:T(8,128)(2,1)}), bf16[8,128,128]{2,1,0:T(8,128)(2,1)S(1)}, u32[]{:S(2)}, u32[]{:S(2)}) async-start(bf16[8,128,128]{2,1,0:T(8,128)(2,1)} %pack.1), calls=%async_computation | async-start | bytes 524288 | tf_op jit(solution)/shard_map/all_to_all | solution.py:272
  19.6 31.4 %collective-permute-start = (bf16[592,2560]{1,0:T(8,128)(2,1)}, bf16[592,2560]{1,0:T(8,128)(2,1)S(1)}, u32[]{:S(2)}, u32[]{:S(2)}) collective-permute-start(bf16[592,2560]{1,0:T(8,128)(2,1)} %get-tuple-element.37), channel_id=1, source_target_pairs={{0,1},{1,0},{2,3},{3,2},{4,5},{5,4},{6,7},{7,6},{8,9},{9,8},{10,11... | collective-permute-start | bytes 9093128 | tf_op jit(solution)/shard_map/ppermute | solution.py:318
  51.0 4.3 %copy-start = (bf16[4,4,160,384]{3,2,1,0:T(8,128)(2,1)}, bf16[4,4,160,384]{3,2,1,0:T(8,128)(2,1)S(1)}, u32[]{:S(2)}) copy-start(bf16[4,4,160,384]{3,2,1,0:T(8,128)(2,1)S(1)} %all_to_all.41) | copy-start | bytes 5898244
  51.0 2.6 %copy-start.1 = (bf16[592,2560]{1,0:T(8,128)(2,1)S(1)}, bf16[592,2560]{1,0:T(8,128)(2,1)}, u32[]{:S(2)}) copy-start(bf16[592,2560]{1,0:T(8,128)(2,1)} %get-tuple-element.39.weight_ref) | copy-start | bytes 9093124
  52.8 2.6 %collective-permute-start.1 = (f32[592,384]{1,0:T(8,128)S(1)}, f32[592,384]{1,0:T(8,128)S(1)}, u32[]{:S(2)}, u32[]{:S(2)}) collective-permute-start(f32[592,384]{1,0:T(8,128)S(1)} %partial_sent.1), channel_id=1, source_target_pairs={{0,1},{1,0},{2,3},{3,2},{4,5},{5,4},{6,7},{7,6},{8,9},{9,8},{10,11... | collective-permute-start | bytes 2727944 | tf_op jit(solution)/shard_map/ppermute | solution.py:339
  55.3 24.5 %collective-permute-start.2 = (bf16[16,160,384]{2,1,0:T(8,128)(2,1)S(1)}, bf16[16,160,384]{2,1,0:T(8,128)(2,1)}, u32[]{:S(2)}, u32[]{:S(2)}) collective-permute-start(bf16[16,160,384]{2,1,0:T(8,128)(2,1)S(1)} %bitcast.12), channel_id=1, source_target_pairs={{0,1},{1,0},{2,3},{3,2},{4,5},{5,4},{6,7},{7,6},{8,9},{9,8},{10,11... | collective-permute-start | bytes 5898248 | tf_op jit(solution)/shard_map/ppermute | solution.py:342
  56.0 23.8 %collective-permute-start.3 = (f32[592,384]{1,0:T(8,128)S(1)}, f32[592,384]{1,0:T(8,128)S(1)}, u32[]{:S(2)}, u32[]{:S(2)}) collective-permute-start(f32[592,384]{1,0:T(8,128)S(1)} %get-tuple-element.45.logits_ref), channel_id=1, source_target_pairs={{0,1},{1,0},{2,3},{3,2},{4,5},{5,4},{6,7},{7,6},{8,9},{9,8},{10,11... | collective-permute-start | bytes 2727944 | tf_op jit(solution)/shard_map/ppermute | solution.py:353
  84.1 18.6 %copy-start.2 = (bf16[592,384]{1,0:T(8,128)(2,1)}, bf16[592,384]{1,0:T(8,128)(2,1)S(1)}, u32[]{:S(2)}) copy-start(bf16[592,384]{1,0:T(8,128)(2,1)S(1)} %get-tuple-element.52.dlogits_ref) | copy-start | bytes 1363972
  114.6 13.4 %all-to-all-start.7 = ((bf16[8,128,128]{2,1,0:T(8,128)(2,1)}), bf16[8,128,128]{2,1,0:T(8,128)(2,1)S(1)}, u32[]{:S(2)}, u32[]{:S(2)}) async-start(bf16[8,128,128]{2,1,0:T(8,128)(2,1)} %spread.1), calls=%async_computation.7 | async-start | bytes 524288 | tf_op jit(solution)/shard_map/all_to_all | solution.py:272
